TPU v7x, 32 devices: a whole 2x2x4 slice. The times are simulated.
32 devices in a mesh: rep: 4 (over y, x), shard: 8 (over z, core).
Axes of the slice: x: 2, y: 2, z: 4, core: 2. Of those that a mesh axis runs over, the one named last changes fastest.
Arguments:
- tokens: bfloat16 [8192, 1536], P(('rep', 'shard')), may hold values from -6 to 6
- cotangent: bfloat16 [8192, 1536], P(('rep', 'shard')), may hold values from -6 to 6
- dealt_to: int32 [32], P(('rep', 'shard')), may hold values from 0 to 7, as said below
- lengths: int32 [32, 3], P(('rep', 'shard')), may hold values from 1 to 192, 256 in all within a row
- routes: int32 [8192, 6], P(('rep', 'shard')), may hold values from 0 to 15, as said below
- slot_index: int32 [8192, 6], P(('rep', 'shard')), may hold values from 0 to 127, as said below
- in_norm: bfloat16 [1536], P('shard'), may hold values from 0.5 to 1.5
- in_proj: bfloat16 [1536, 6448], P('shard'), may hold values from -0.15625 to 0.15625
- conv_weight: bfloat16 [4, 3328], P(None, 'shard'), may hold values from -3 to 3
- conv_bias: bfloat16 [3328], P('shard'), may hold values from -3 to 3
- dt_bias: bfloat16 [48], P('shard'), may hold values from -5 to -2
- decay_log: bfloat16 [48], P('shard'), may hold values from -1 to 2.5
- skip_gain: bfloat16 [48], P('shard'), may hold values from 0.5 to 1.5
- mixer_norm: bfloat16 [3072], P('shard'), may hold values from 0.5 to 1.5
- out_proj: bfloat16 [3072, 1536], P('shard'), may hold values from -0.109375 to 0.109375
- post_norm: bfloat16 [1536], P('shard'), may hold values from 0.5 to 1.5
- router: bfloat16 [1536, 16], P('shard'), may hold values from -0.078125 to 0.078125
- shared_in: bfloat16 [1536, 2048], P('shard'), may hold values from -0.15625 to 0.15625
- shared_out: bfloat16 [1024, 1536], P('shard'), may hold values from -0.1875 to 0.1875
- expert_in: bfloat16 [16, 1536, 1024], P('shard'), may hold values from -0.15625 to 0.15625
- expert_out: bfloat16 [16, 512, 1536], P('shard'), may hold values from -0.5 to 0.5
Outputs:
- layer_out: bfloat16 [8192, 1536], P(('rep', 'shard'))
- grad_tokens: bfloat16 [8192, 1536], P(('rep', 'shard'))
- grad_in_norm: float32 [1536], P('shard')
- grad_in_proj: float32 [1536, 6448], P('shard')
- grad_conv_weight: float32 [4, 3328], P(None, 'shard')
- grad_conv_bias: float32 [3328], P('shard')
- grad_dt_bias: float32 [48], P('shard')
- grad_decay_log: float32 [48], P('shard')
- grad_skip_gain: float32 [48], P('shard')
- grad_mixer_norm: float32 [3072], P('shard')
- grad_out_proj: float32 [3072, 1536], P('shard')
- grad_post_norm: float32 [1536], P('shard')
- grad_router: float32 [1536, 16], P('shard')
- grad_shared_in: float32 [1536, 2048], P('shard')
- grad_shared_out: float32 [1024, 1536], P('shard')
- grad_expert_in: float32 [16, 1536, 1024], P('shard')
- grad_expert_out: float32 [16, 512, 1536], P('shard')
Inputs may be any that keep to these rules, and one draw needn't show every extreme that they name: `dealt_to`: the blocks come in groups of 8 consecutive ones; in each group, with q the block's place in it, the entry is q XOR m for one m of that group. `routes`: each row names 6 different experts in rising order. In the rows of one block no expert is named more than 128 times and some expert exactly 128 times; in each group of 8 consecutive blocks one expert is named exactly 128 times in every block. `slot_index`: in one block, the entries of the places that name expert e are 0 to n - 1, once each, where n is how often the block names e.
All inputs are finite; a program needn't handle non-finite values.
Results may differ from a plain program's by a relative error of at most 0.012.
Values may be sent and summed in bfloat16 or wider, within the bound.
A program may use at most 384 MiB of HBM per device.

v0:
```python
import jax
import jax.numpy as jnp
from jax import lax
from jax.sharding import PartitionSpec as P

EPS = 1e-05
HIGH = lax.Precision.HIGHEST
block_limit = 128


def from_partner(value, axis, distance):
    mask = 2**distance
    pairs = [(source, source ^ mask) for source in range(lax.axis_size(axis))]
    return lax.ppermute(value, axis, pairs)


def rms_scale(values, scale_gain):
    return values * lax.rsqrt(jnp.mean(values * values, axis=-1, keepdims=True) + EPS) * scale_gain


def segment_ids(lengths_row, row_count):
    length_ends = jnp.cumsum(lengths_row)
    position = jnp.arange(row_count, dtype=jnp.int32)
    return jnp.sum((position[:, None] >= length_ends[None, :]).astype(jnp.int32), axis=1)


def conv_mix(channels, conv_weight, conv_bias, seg_ids):
    row_count = channels.shape[0]
    tap_count = conv_weight.shape[0]
    result = jnp.zeros_like(channels) + conv_bias[None, :]
    for tap_index in range(tap_count):
        offset = tap_count - 1 - tap_index
        earlier = jnp.pad(channels, ((offset, 0), (0, 0)))[:row_count]
        earlier_seg = jnp.pad(seg_ids, (offset, 0), constant_values=-1)[:row_count]
        same_segment = (earlier_seg == seg_ids).astype(channels.dtype)
        result = result + conv_weight[tap_index][None, :] * earlier * same_segment[:, None]
    return result


def state_scan(inputs, step_sizes, decay_log, write_rows, read_rows, seg_ids):
    row_count, head_count, head_width = inputs.shape
    block_size = min(block_limit, row_count)
    block_count = row_count // block_size
    state_width = write_rows.shape[1]
    log_decay = -step_sizes * jnp.exp(decay_log)[None, :]
    scaled = inputs * step_sizes[:, :, None]
    causal_mask = jnp.arange(block_size)[:, None] >= jnp.arange(block_size)[None, :]

    def advance(carry_in, pieces):
        carried_state, last_seg = carry_in
        block_log, block_input, block_write, block_read, block_seg = pieces
        cumulative = jnp.cumsum(block_log, axis=0)
        keep_mask = causal_mask & (block_seg[:, None] == block_seg[None, :])
        log_gaps = jnp.where(
            keep_mask[:, :, None], cumulative[:, None, :] - cumulative[None, :, :], 0.0
        )
        weights = jnp.exp(log_gaps) * keep_mask[:, :, None].astype(log_gaps.dtype)
        scores = jnp.dot(block_read, block_write.T, precision=HIGH)
        inner_part = jnp.einsum(
            "tsh,shp->thp", scores[:, :, None] * weights, block_input, precision=HIGH
        )
        carried_flag = (block_seg == last_seg).astype(cumulative.dtype)
        entry_decay = jnp.exp(cumulative) * carried_flag[:, None]
        outer_part = (
            jnp.einsum("tn,hnp->thp", block_read, carried_state, precision=HIGH)
            * entry_decay[:, :, None]
        )
        end_seg = block_seg[-1]
        tail_weights = (
            jnp.exp(cumulative[-1][None, :] - cumulative)
            * (block_seg == end_seg).astype(cumulative.dtype)[:, None]
        )
        fresh_state = jnp.einsum(
            "sn,sh,shp->hnp", block_write, tail_weights, block_input, precision=HIGH
        )
        through = jnp.exp(cumulative[-1]) * (end_seg == last_seg).astype(cumulative.dtype)
        carried_state = carried_state * through[:, None, None] + fresh_state
        return ((carried_state, end_seg), inner_part + outer_part)

    start_carry = (
        jnp.zeros((head_count, state_width, head_width), inputs.dtype),
        jnp.array(-1, jnp.int32),
    )
    pieces = (
        log_decay.reshape(block_count, block_size, head_count),
        scaled.reshape(block_count, block_size, head_count, head_width),
        write_rows.reshape(block_count, block_size, state_width),
        read_rows.reshape(block_count, block_size, state_width),
        seg_ids.reshape(block_count, block_size),
    )
    final_carry, outputs = lax.scan(advance, start_carry, pieces)
    return outputs.reshape(row_count, head_count, head_width)


def mixer_middle(
    projected, conv_weight, conv_bias, dt_shift, decay_log, skip_gain, norm_gain, seg_ids
):
    inner_width = norm_gain.shape[0]
    xbc_width = conv_bias.shape[0]
    row_count = projected.shape[0]
    head_count = decay_log.shape[0]
    head_width = inner_width // head_count
    state_width = (xbc_width - inner_width) // 2
    gate_side = projected[:, :inner_width]
    channels = projected[:, inner_width : inner_width + xbc_width]
    dt_raw = projected[:, inner_width + xbc_width :]
    activated = jax.nn.silu(conv_mix(channels, conv_weight, conv_bias, seg_ids))
    values_in = activated[:, :inner_width].reshape(row_count, head_count, head_width)
    write_rows = activated[:, inner_width : inner_width + state_width]
    read_rows = activated[:, inner_width + state_width :]
    step_sizes = jax.nn.softplus(dt_raw + dt_shift[None, :])
    scanned = state_scan(values_in, step_sizes, decay_log, write_rows, read_rows, seg_ids)
    scanned = scanned + skip_gain[None, :, None] * values_in
    gated = scanned.reshape(row_count, inner_width) * jax.nn.silu(gate_side)
    return rms_scale(gated, norm_gain)


def silu_parts(pre_values):
    half_width = pre_values.shape[-1] // 2
    gate_side = pre_values[..., :half_width]
    up_side = pre_values[..., half_width:]
    sigmoid_gate = jax.nn.sigmoid(gate_side)
    return (gate_side * sigmoid_gate, up_side, sigmoid_gate, gate_side)


def swiglu_back(pre_values, hidden_grad):
    swiglu_parts = silu_parts(pre_values)
    slope = swiglu_parts[2] * (1.0 + swiglu_parts[3] * (1.0 - swiglu_parts[2]))
    return jnp.concatenate(
        [hidden_grad * swiglu_parts[1] * slope, hidden_grad * swiglu_parts[0]], axis=-1
    )


def move_tables(values, shift_bits, bit_count):
    for bit_number in range(bit_count):
        arrived = from_partner(values, "shard", bit_number)
        values = jnp.where(shift_bits >> bit_number & 1 == 1, arrived, values)
    return values


def shards(
    tokens,
    cotangent,
    dealt_to,
    lengths,
    routes,
    slot_index,
    in_norm,
    in_proj,
    conv_weight,
    conv_bias,
    dt_bias,
    decay_log,
    skip_gain,
    mixer_norm,
    out_proj,
    post_norm,
    router,
    shared_in,
    shared_out,
    expert_in,
    expert_out,
):
    group_size = lax.axis_size("shard")
    bit_count = group_size.bit_length() - 1
    shift_bits = dealt_to[0] ^ lax.axis_index("shard")
    row_count = tokens.shape[0]
    model_width = tokens.shape[1]
    top_count = routes.shape[1]
    local_experts = expert_in.shape[0]
    expert_count = local_experts * group_size
    capacity = row_count * top_count * 4 // (3 * expert_count)
    seg_ids = segment_ids(lengths[0], row_count)
    packed = jnp.concatenate([routes, slot_index, seg_ids[:, None]], axis=1)
    packed = move_tables(packed, shift_bits, bit_count)
    routes = packed[:, :top_count]
    slot_index = packed[:, top_count : 2 * top_count]
    seg_ids = packed[:, 2 * top_count]
    (
        norm_first,
        proj_full,
        conv_full,
        bias_full,
        shift_full,
        decay_full,
        skip_full,
        gate_norm_full,
        out_full,
        norm_second,
        router_full,
        shared_in_full,
        shared_out_full,
    ) = (
        lax.all_gather(in_norm, "shard", axis=0, tiled=True),
        lax.all_gather(in_proj, "shard", axis=0, tiled=True),
        lax.all_gather(conv_weight, "shard", axis=1, tiled=True),
        lax.all_gather(conv_bias, "shard", axis=0, tiled=True),
        lax.all_gather(dt_bias, "shard", axis=0, tiled=True),
        lax.all_gather(decay_log, "shard", axis=0, tiled=True),
        lax.all_gather(skip_gain, "shard", axis=0, tiled=True),
        lax.all_gather(mixer_norm, "shard", axis=0, tiled=True),
        lax.all_gather(out_proj, "shard", axis=0, tiled=True),
        lax.all_gather(post_norm, "shard", axis=0, tiled=True),
        lax.all_gather(router, "shard", axis=0, tiled=True),
        lax.all_gather(shared_in, "shard", axis=0, tiled=True),
        lax.all_gather(shared_out, "shard", axis=0, tiled=True),
    )
    rows_float = tokens.astype(jnp.float32)
    first_normed, first_back = jax.vjp(rms_scale, rows_float, norm_first.astype(jnp.float32))
    first_low = first_normed.astype(jnp.bfloat16)
    projected = jnp.dot(first_low, proj_full, preferred_element_type=jnp.float32)

    def middle(projected_in, conv_in, bias_in, shift_in, decay_in, skip_in, gain_in):
        return mixer_middle(
            projected_in, conv_in, bias_in, shift_in, decay_in, skip_in, gain_in, seg_ids
        )

    normed, middle_back = jax.vjp(
        middle,
        projected,
        conv_full.astype(jnp.float32),
        bias_full.astype(jnp.float32),
        shift_full.astype(jnp.float32),
        decay_full.astype(jnp.float32),
        skip_full.astype(jnp.float32),
        gate_norm_full.astype(jnp.float32),
    )
    normed_low = normed.astype(jnp.bfloat16)
    after_mixer = rows_float + jnp.dot(normed_low, out_full, preferred_element_type=jnp.float32)
    second_normed, second_back = jax.vjp(rms_scale, after_mixer, norm_second.astype(jnp.float32))
    second_low = second_normed.astype(jnp.bfloat16)
    logits = jnp.dot(second_low, router_full, preferred_element_type=jnp.float32)
    gate_weights = jax.nn.softmax(jnp.take_along_axis(logits, routes, axis=1), axis=1)
    shared_pre = jnp.dot(second_low, shared_in_full, preferred_element_type=jnp.float32)
    shared_parts = silu_parts(shared_pre)
    shared_hidden = (shared_parts[0] * shared_parts[1]).astype(jnp.bfloat16)
    shared_result = jnp.dot(shared_hidden, shared_out_full, preferred_element_type=jnp.float32)
    flat_slot = (routes * capacity + slot_index).reshape(-1)
    send_rows = (
        jnp.zeros((expert_count * capacity, model_width), jnp.bfloat16)
        .at[flat_slot]
        .set(jnp.repeat(second_low, top_count, axis=0))
        .reshape(group_size, local_experts, capacity, model_width)
    )
    received = lax.all_to_all(send_rows, "shard", split_axis=0, concat_axis=0, tiled=True)
    expert_pre = jnp.einsum(
        "secd,edf->secf", received, expert_in, preferred_element_type=jnp.float32
    )
    expert_parts = silu_parts(expert_pre)
    hidden = (expert_parts[0] * expert_parts[1]).astype(jnp.bfloat16)
    result = jnp.einsum(
        "secf,efd->secd", hidden, expert_out, preferred_element_type=jnp.float32
    ).astype(jnp.bfloat16)
    returned = lax.all_to_all(result, "shard", split_axis=0, concat_axis=0, tiled=True)
    returned, received, expert_pre = (returned, received, expert_pre)
    returned_rows = returned.reshape(expert_count * capacity, model_width)[flat_slot].reshape(
        row_count, top_count, model_width
    )
    routed = jnp.zeros((row_count, model_width), jnp.float32)
    for pick_index in range(top_count):
        routed = routed + gate_weights[:, pick_index, None] * returned_rows[:, pick_index].astype(
            jnp.float32
        )
    layer_out = (after_mixer + shared_result + routed).astype(jnp.bfloat16)
    grad_float = cotangent.astype(jnp.float32)
    gate_grad = jnp.einsum(
        "tkd,td->tk", returned_rows, cotangent, preferred_element_type=jnp.float32
    )
    picked_grad = gate_weights * (
        gate_grad - jnp.sum(gate_weights * gate_grad, axis=1, keepdims=True)
    )
    onehot = (
        routes[:, :, None] == jnp.arange(expert_count, dtype=jnp.int32)[None, None, :]
    ).astype(jnp.float32)
    logit_grad = jnp.sum(onehot * picked_grad[:, :, None], axis=1).astype(jnp.bfloat16)
    slot_grad = (
        (gate_weights[:, :, None] * grad_float[:, None, :])
        .astype(jnp.bfloat16)
        .reshape(row_count * top_count, model_width)
    )
    send_grad = (
        jnp.zeros((expert_count * capacity, model_width), jnp.bfloat16)
        .at[flat_slot]
        .set(slot_grad)
        .reshape(group_size, local_experts, capacity, model_width)
    )
    owner_grad = lax.all_to_all(send_grad, "shard", split_axis=0, concat_axis=0, tiled=True)
    owner_parts = silu_parts(expert_pre)
    owner_hidden = (owner_parts[0] * owner_parts[1]).astype(jnp.bfloat16)
    grad_expert_out = jnp.einsum(
        "secf,secd->efd", owner_hidden, owner_grad, preferred_element_type=jnp.float32
    )
    hidden_grad = jnp.einsum(
        "secd,efd->secf", owner_grad, expert_out, preferred_element_type=jnp.float32
    )
    pre_grad = swiglu_back(expert_pre, hidden_grad).astype(jnp.bfloat16)
    grad_expert_in = jnp.einsum(
        "secd,secf->edf", received, pre_grad, preferred_element_type=jnp.float32
    )
    row_grad = jnp.einsum(
        "secf,edf->secd", pre_grad, expert_in, preferred_element_type=jnp.float32
    ).astype(jnp.bfloat16)
    back_rows = (
        lax.all_to_all(row_grad, "shard", split_axis=0, concat_axis=0, tiled=True)
        .reshape(expert_count * capacity, model_width)[flat_slot]
        .reshape(row_count, top_count, model_width)
    )
    second_grad = jnp.dot(logit_grad, router_full.T, preferred_element_type=jnp.float32)
    for pick_index in range(top_count):
        second_grad = second_grad + back_rows[:, pick_index].astype(jnp.float32)
    shared_out_grad = jnp.dot(shared_hidden.T, cotangent, preferred_element_type=jnp.float32)
    shared_hidden_grad = jnp.dot(cotangent, shared_out_full.T, preferred_element_type=jnp.float32)
    shared_pre_grad = swiglu_back(shared_pre, shared_hidden_grad).astype(jnp.bfloat16)
    shared_in_grad = jnp.dot(second_low.T, shared_pre_grad, preferred_element_type=jnp.float32)
    second_grad = second_grad + jnp.dot(
        shared_pre_grad, shared_in_full.T, preferred_element_type=jnp.float32
    )
    router_grad = jnp.dot(second_low.T, logit_grad, preferred_element_type=jnp.float32)
    after_part, post_grad = second_back(second_grad)
    after_grad = grad_float + after_part
    after_low = after_grad.astype(jnp.bfloat16)
    out_proj_grad = jnp.dot(normed_low.T, after_low, preferred_element_type=jnp.float32)
    normed_grad = jnp.dot(after_low, out_full.T, preferred_element_type=jnp.float32)
    projected_grad, conv_grad, bias_grad, shift_grad, decay_grad, skip_grad, gain_grad = (
        middle_back(normed_grad)
    )
    projected_low = projected_grad.astype(jnp.bfloat16)
    in_proj_grad = jnp.dot(first_low.T, projected_low, preferred_element_type=jnp.float32)
    first_grad = jnp.dot(projected_low, proj_full.T, preferred_element_type=jnp.float32)
    input_part, first_norm_grad = first_back(first_grad)
    input_grad = (after_grad + input_part).astype(jnp.bfloat16)
    dense_grads = (
        lax.psum_scatter(first_norm_grad, "shard", scatter_dimension=0, tiled=True),
        lax.psum_scatter(in_proj_grad, "shard", scatter_dimension=0, tiled=True),
        lax.psum_scatter(conv_grad, "shard", scatter_dimension=1, tiled=True),
        lax.psum_scatter(bias_grad, "shard", scatter_dimension=0, tiled=True),
        lax.psum_scatter(shift_grad, "shard", scatter_dimension=0, tiled=True),
        lax.psum_scatter(decay_grad, "shard", scatter_dimension=0, tiled=True),
        lax.psum_scatter(skip_grad, "shard", scatter_dimension=0, tiled=True),
        lax.psum_scatter(gain_grad, "shard", scatter_dimension=0, tiled=True),
        lax.psum_scatter(out_proj_grad, "shard", scatter_dimension=0, tiled=True),
        lax.psum_scatter(post_grad, "shard", scatter_dimension=0, tiled=True),
        lax.psum_scatter(router_grad, "shard", scatter_dimension=0, tiled=True),
        lax.psum_scatter(shared_in_grad, "shard", scatter_dimension=0, tiled=True),
        lax.psum_scatter(shared_out_grad, "shard", scatter_dimension=0, tiled=True),
    )
    summed = lax.psum(
        (
            dense_grads[0],
            dense_grads[1],
            dense_grads[2],
            dense_grads[3],
            dense_grads[4],
            dense_grads[5],
            dense_grads[6],
            dense_grads[7],
            dense_grads[8],
            dense_grads[9],
            dense_grads[10],
            dense_grads[11],
            dense_grads[12],
            grad_expert_in,
            grad_expert_out,
        ),
        "rep",
    )
    return (
        layer_out,
        input_grad,
        summed[0],
        summed[1],
        summed[2],
        summed[3],
        summed[4],
        summed[5],
        summed[6],
        summed[7],
        summed[8],
        summed[9],
        summed[10],
        summed[11],
        summed[12],
        summed[13],
        summed[14],
    )


def solution(mesh):
    return jax.shard_map(
        shards,
        mesh=mesh,
        in_specs=(
            P(("rep", "shard"), None),
            P(("rep", "shard"), None),
            P(("rep", "shard")),
            P(("rep", "shard"), None),
            P(("rep", "shard"), None),
            P(("rep", "shard"), None),
            P("shard"),
            P("shard", None),
            P(None, "shard"),
            P("shard"),
            P("shard"),
            P("shard"),
            P("shard"),
            P("shard"),
            P("shard", None),
            P("shard"),
            P("shard", None),
            P("shard", None),
            P("shard", None),
            P("shard", None, None),
            P("shard", None, None),
        ),
        out_specs=(
            P(("rep", "shard"), None),
            P(("rep", "shard"), None),
            P("shard"),
            P("shard", None),
            P(None, "shard"),
            P("shard"),
            P("shard"),
            P("shard"),
            P("shard"),
            P("shard"),
            P("shard", None),
            P("shard"),
            P("shard", None),
            P("shard", None),
            P("shard", None),
            P("shard", None, None),
            P("shard", None, None),
        ),
        check_vma=False,
    )
```

profile of v0, /device:TPU:0, one launch (start us, length us, event | category | flops | bytes accessed | tf_op | source)
XLA Modules:
  0.0 2726.3 jit_solution(5526642501140290934)
XLA Ops:
  11.2 15.4 all-gather
  31.4 32.4 %all-reduce.37 = (bf16[1536]{0:T(1024)(128)(2,1)S(1)}, bf16[48]{0:T(256)(128)(2,1)}, bf16[48]{0:T(256)(128)(2,1)}, bf16[48]{0:T(256)(128)(2,1)S(1)}, bf16[3328]{...) all-reduce(bf16[1536]{0:T(1024)(128)(2,1)S(1)} %dynamic-update-slice, ...), channel_id=1, replica_groups=mesh['rep'=4,'shard'=8] {'shard'}, use_global_device_ids=true, to_apply=%add.21 | all-reduce | flops 6544 | bytes 26176
  64.4 12.2 collective-permute-done.1
  79.2 24.3 all-gather.1
  106.9 89.8 %all-gather.8.cloned.1.call-done = bf16[1536,6448]{1,0:T(8,128)(2,1)} async-done(((bf16[192,6448]{1,0:T(8,128)(2,1)}), bf16[1536,6448]{1,0:T(8,128)(2,1)}) %all-gather.8.cloned.1.call-update) | async-done | bytes 19808272 | tf_op jit(solution)/shard_map/all_gather | solution.py:195
  196.8 14.3 fusion.200
  239.0 250.1 %while.79 = (s32[]{:T(128)}, f32[48,128,64]{1,2,0:T(8,128)}, s32[]{:T(128)}, f32[2,128,48,64]{1,0,3,2:T(2,128)}, pred[2,128,128,48]{2,1,3,0:T(32,128)(4,1)}, /*i...) while((s32[]{:T(128)}, f32[48,128,64]{1,2,0:T(8,128)}, ...), condition=%wide.region_5.6_spmd.clone.clone, body=%wide.region_3.5_spmd.clone.clone.sunk | while | flops 1847098368 | bytes 83333624 | solution.py:91
  257.0 9.0 bitcast_add_fusion.12
  266.0 36.8 %dynamic_update_slice.251 = f32[2,128,48,64]{1,0,3,2:T(2,128)} dynamic-update-slice(f32[2,128,48,64]{1,0,3,2:T(2,128)} %get-tuple-element.2142, f32[1,128,48,64]{1,0,3,2:T(1,128)} %bitcast.596, s32[]{:T(128)S(6)} %copy.596, s32[]{:T(128)} %constant.206.clone.1..sunk.1, s32[]{:T(128)} %constant.206.clone.1..sunk.1, s32[]{:T(128)} %constant.206.clone.1..sunk.1) | dynamic-update-slice | bytes 3145732 | tf_op jit(solution)/shard_map/jvp()/while/body/jit(dynamic_update_index_in_dim)/dynamic_update_slice | solution.py:91
  304.1 10.2 broadcast_multiply_fusion.5
  382.8 9.0 bitcast_add_fusion.12
  391.8 36.8 %dynamic_update_slice.251 = f32[2,128,48,64]{1,0,3,2:T(2,128)} dynamic-update-slice(f32[2,128,48,64]{1,0,3,2:T(2,128)} %get-tuple-element.2142, f32[1,128,48,64]{1,0,3,2:T(1,128)} %bitcast.596, s32[]{:T(128)S(6)} %copy.596, s32[]{:T(128)} %constant.206.clone.1..sunk.1, s32[]{:T(128)} %constant.206.clone.1..sunk.1, s32[]{:T(128)} %constant.206.clone.1..sunk.1) | dynamic-update-slice | bytes 3145732 | tf_op jit(solution)/shard_map/jvp()/while/body/jit(dynamic_update_index_in_dim)/dynamic_update_slice | solution.py:91
  429.9 10.2 broadcast_multiply_fusion.5
  508.7 8.4 reshape.880
  517.1 12.4 scatter_custom_fusion
  534.9 163.6 %all-to-all-done = bf16[8,2,128,1536]{3,2,1,0:T(8,128)(2,1)} async-done(((bf16[8,2,128,1536]{3,2,1,0:T(8,128)(2,1)}), bf16[8,2,128,1536]{3,2,1,0:T(8,128)(2,1)}, u32[]{:S(2)}, u32[]{:S(2)}) %all-to-all-start) | async-done | bytes 6291488 | tf_op jit(solution)/shard_map/all_to_all | solution.py:245
  698.5 10.1 fusion.151
  742.8 187.5 %all-gather.2 = bf16[8,192,16]{1,2,0:T(8,128)(2,1)S(1)} all-gather(bf16[1,192,16]{1,2,0:T(8,128)(2,1)S(1)} %bitcast.623), channel_id=1, replica_groups=mesh['rep'=4,'shard'=8] {'shard'}, dimensions={0}, use_global_device_ids=true | all-gather | bytes 55296 | tf_op jit(solution)/shard_map/all_gather | solution.py:204
  938.0 11.9 mul.1051
  951.6 12.7 gather_fusion.2
  966.0 14.0 gather_fusion
  979.9 8.3 reshape.824
  995.7 13.2 scatter_custom_fusion.1
  1021.9 219.9 %all-to-all-done.2 = bf16[8,2,128,1536]{3,2,1,0:T(8,128)(2,1)} async-done(((bf16[8,2,128,1536]{3,2,1,0:T(8,128)(2,1)}), bf16[8,2,128,1536]{3,2,1,0:T(8,128)(2,1)}, u32[]{:S(2)}, u32[]{:S(2)}) %all-to-all-start.2) | async-done | bytes 6291488 | tf_op jit(solution)/shard_map/all_to_all | solution.py:287
  1241.8 9.5 fusion.141
  1251.2 11.6 convert_bitcast_fusion
  1278.5 132.6 %all-to-all-done.3 = bf16[8,2,128,1536]{3,2,1,0:T(8,128)(2,1)} async-done(((bf16[8,2,128,1536]{3,2,1,0:T(8,128)(2,1)}), bf16[8,2,128,1536]{3,2,1,0:T(8,128)(2,1)}, u32[]{:S(2)}, u32[]{:S(2)}) %all-to-all-start.3) | async-done | bytes 6291488 | tf_op jit(solution)/shard_map/all_to_all | solution.py:304
  1411.1 14.0 gather_fusion.1
  1425.1 8.3 reshape.827
  1433.4 17.3 fusion.226
  1464.4 9.4 multiply_reduce_fusion.4
  1491.3 185.0 %while.78 = (s32[]{:T(128)}, f32[48,128,64]{1,2,0:T(8,128)S(1)}, f32[2,128,48]{2,1,0:T(8,128)}, f32[2,128,48,64]{1,0,3,2:T(2,128)}, f32[2,128,128]{2,1,0:T(8,128...) while((s32[]{:T(128)}, f32[48,128,64]{1,2,0:T(8,128)S(1)}, ...), condition=%wide.region_24.25_spmd.clone, body=%wide.region_16.24_spmd.clone.sunk | while | flops 3687651328 | bytes 132334400 | solution.py:91
  1506.6 8.2 fusion.311
  1540.1 36.9 %dynamic_update_slice.236 = f32[2,128,48,64]{1,0,3,2:T(2,128)} dynamic-update-slice(f32[2,128,48,64]{1,0,3,2:T(2,128)} %get-tuple-element.2236, f32[1,128,48,64]{1,0,3,2:T(1,128)} %bitcast.593, s32[]{:T(128)S(6)} %sub.230, s32[]{:T(128)} %constant.206.clone.1..sunk, s32[]{:T(128)} %constant.206.clone.1..sunk, s32[]{:T(128)} %constant.206.clone.1..sunk) | dynamic-update-slice | bytes 3145732 | tf_op jit(solution)/shard_map/transpose(jvp())/while/body/jit(dynamic_update_index_in_dim)/dynamic_update_slice | solution.py:91
  1598.7 8.2 fusion.311
  1632.3 36.8 %dynamic_update_slice.236 = f32[2,128,48,64]{1,0,3,2:T(2,128)} dynamic-update-slice(f32[2,128,48,64]{1,0,3,2:T(2,128)} %get-tuple-element.2236, f32[1,128,48,64]{1,0,3,2:T(1,128)} %bitcast.593, s32[]{:T(128)S(6)} %sub.230, s32[]{:T(128)} %constant.206.clone.1..sunk, s32[]{:T(128)} %constant.206.clone.1..sunk, s32[]{:T(128)} %constant.206.clone.1..sunk) | dynamic-update-slice | bytes 3145732 | tf_op jit(solution)/shard_map/transpose(jvp())/while/body/jit(dynamic_update_index_in_dim)/dynamic_update_slice | solution.py:91
  1693.5 9.3 multiply_reduce_fusion.2
  1709.9 17.7 fusion.198
  1730.2 14.0 convolution_bitcast_fusion
  1746.1 9.7 fusion.137
  1755.8 357.2 %reduce-scatter.11.cloned.1.call-done = f32[192,6448]{1,0:T(8,128)} async-done(((f32[1536,6448]{1,0:T(8,128)}), f32[192,6448]{1,0:T(8,128)}) %reduce-scatter.11.cloned.1.call-update) | async-done | bytes 4952080 | tf_op jit(solution)/shard_map/reduce_scatter | solution.py:334
  2116.2 17.2 fusion.227
  2136.2 9.5 reduce-scatter.21.cloned.1.call-done
  2147.0 12.9 fusion.176
  2159.9 26.9 all-reduce.34
  2191.2 18.2 all-reduce.35
  2209.4 482.5 %all-reduce.40.cloned.1.call-done = (f32[192,6448]{1,0:T(8,128)}, f32[384,1536]{1,0:T(8,128)}, f32[192,2048]{1,0:T(8,128)}, f32[128,1536]{1,0:T(8,128)}, f32[2,1...) async-done(((f32[192,6448]{1,0:T(8,128)}, f32[384,1536]{1,0:T(8,128)}, f32[192,2048]{1,0:T(8,128)}, f32[128,1536]{1,0:T(8,128)}, f32[2,1536,1024]{2,1,0:T(8,128)}, ...) | async-done | bytes 28545040 | tf_op jit(solution)/shard_map/psum | solution.py:347
  2701.4 12.1 copy.680
  (681 shorter events, 458.6 us)
Async XLA Ops:
  7.2 707.5 %copy-start = (bf16[2,512,1536]{2,1,0:T(8,128)(2,1)S(1)}, bf16[2,512,1536]{2,1,0:T(8,128)(2,1)}, u32[]{:S(2)}) copy-start(bf16[2,512,1536]{2,1,0:T(8,128)(2,1)} %param.45) | copy-start | bytes 9437188
  7.2 19.4 copy-start.132
  7.3 22.6 copy-start.138
  7.3 22.8 copy-start.139
  7.3 23.1 copy-start.140
  7.3 23.3 copy-start.141
  7.3 23.6 copy-start.142
  7.3 23.8 copy-start.133
  7.3 71.8 %copy-start.134 = (bf16[384]{0:T(512)(128)(2,1)S(1)}, bf16[384]{0:T(512)(128)(2,1)}, u32[]{:S(2)}) copy-start(bf16[384]{0:T(512)(128)(2,1)} %param.38) | copy-start | bytes 2308
  7.3 189.4 %all-gather.8.cloned.1.call-start = ((), (), s32[]{:S(2)}) async-start(), calls=%async_computation.10 | async-start | bytes 22560768 | tf_op jit(solution)/shard_map/all_gather | solution.py:195
  8.1 487.3 %all-gather.10.cloned.1.call-start = ((), (), s32[]{:S(2)}) async-start(), calls=%async_computation.11 | async-start | bytes 10616832 | tf_op jit(solution)/shard_map/all_gather | solution.py:202
  8.8 717.6 %all-gather.12.cloned.1.call-start = ((), (), s32[]{:S(2)}) async-start(), calls=%async_computation.12 | async-start | bytes 7077888 | tf_op jit(solution)/shard_map/all_gather | solution.py:205
  9.3 54.6 %collective-permute-start = (s32[256,13]{1,0:T(8,128)S(1)}, s32[256,13]{1,0:T(8,128)}, u32[]{:S(2)}, u32[]{:S(2)}) collective-permute-start(s32[256,13]{1,0:T(8,128)S(1)} %copy.299), channel_id=1, source_target_pairs={{0,1},{1,0},{2,3},{3,2},{4,5},{5,4},{6,7},{7,6},{8,9},{9,8},{10,11... | collective-permute-start | bytes 39944 | tf_op jit(solution)/shard_map/ppermute | solution.py:14
  11.2 19.9 copy-start.114
  26.6 184.4 %copy-start.91 = (f32[256]{0:T(256)}, f32[256]{0:T(256)S(1)}, u32[]{:S(2)}) copy-start(f32[256]{0:T(256)S(1)} %fusion.211) | copy-start | bytes 3076
  63.9 12.7 collective-permute-start.1
  64.3 159.4 %copy-start.129 = (f32[48]{0:T(128)}, f32[48]{0:T(128)S(1)}, u32[]{:S(2)}) copy-start(f32[48]{0:T(128)S(1)} %convert_exponential_fusion) | copy-start | bytes 580
  76.6 28.1 %collective-permute-start.2 = (s32[256,13]{1,0:T(8,128)S(1)}, s32[256,13]{1,0:T(8,128)}, u32[]{:S(2)}, u32[]{:S(2)}) collective-permute-start(s32[256,13]{1,0:T(8,128)S(1)} %broadcast_select_fusion.2), channel_id=1, source_target_pairs={{0,4},{1,5},{2,6},{3,7},{4,0},{5,1},{6,2},{7,3},{8,12},{9,13},{10,... | collective-permute-start | bytes 39944 | tf_op jit(solution)/shard_map/ppermute | solution.py:14
  76.8 136.5 %copy-start.70 = (f32[3328]{0:T(1024)}, f32[3328]{0:T(1024)S(1)}, u32[]{:S(2)}) copy-start(f32[3328]{0:T(1024)S(1)} %get-tuple-element.1468) | copy-start | bytes 39940
  76.8 136.5 %copy-start.72 = (f32[3328]{0:T(1024)}, f32[3328]{0:T(1024)S(1)}, u32[]{:S(2)}) copy-start(f32[3328]{0:T(1024)S(1)} %get-tuple-element.1467) | copy-start | bytes 39940
  76.8 136.5 %copy-start.74 = (f32[3328]{0:T(1024)}, f32[3328]{0:T(1024)S(1)}, u32[]{:S(2)}) copy-start(f32[3328]{0:T(1024)S(1)} %get-tuple-element.1469) | copy-start | bytes 39940
  76.9 136.5 %copy-start.76 = (f32[3328]{0:T(1024)}, f32[3328]{0:T(1024)S(1)}, u32[]{:S(2)}) copy-start(f32[3328]{0:T(1024)S(1)} %get-tuple-element.1470) | copy-start | bytes 39940
  77.1 134.0 %copy-start.64 = (f32[1536]{0:T(1024)}, f32[1536]{0:T(1024)S(1)}, u32[]{:S(2)}) copy-start(f32[1536]{0:T(1024)S(1)} %convert_element_type.246) | copy-start | bytes 18436
  79.2 144.5 %copy-start.130 = (f32[48]{0:T(128)}, f32[48]{0:T(128)S(1)}, u32[]{:S(2)}) copy-start(f32[48]{0:T(128)S(1)} %convert_element_type.248) | copy-start | bytes 580
  106.2 107.2 %copy-start.104 = (f32[256]{0:T(256)}, f32[256]{0:T(256)S(1)}, u32[]{:S(2)}) copy-start(f32[256]{0:T(256)S(1)} %get-tuple-element.1684) | copy-start | bytes 3076
  106.2 107.2 %copy-start.106 = (f32[256]{0:T(256)}, f32[256]{0:T(256)S(1)}, u32[]{:S(2)}) copy-start(f32[256]{0:T(256)S(1)} %get-tuple-element.1685) | copy-start | bytes 3076
  106.2 107.2 %copy-start.108 = (f32[256]{0:T(256)}, f32[256]{0:T(256)S(1)}, u32[]{:S(2)}) copy-start(f32[256]{0:T(256)S(1)} %get-tuple-element.1686) | copy-start | bytes 3076
  529.5 169.0 %all-to-all-start = ((bf16[8,2,128,1536]{3,2,1,0:T(8,128)(2,1)}), bf16[8,2,128,1536]{3,2,1,0:T(8,128)(2,1)}, u32[]{:S(2)}, u32[]{:S(2)}) async-start(bf16[8,2,128,1536]{3,2,1,0:T(8,128)(2,1)} %bitcast.602), calls=%async_computation | async-start | bytes 12582912 | tf_op jit(solution)/shard_map/all_to_all | solution.py:245
  534.3 198.3 %all-gather.14.cloned.1.call-start = ((), (), s32[]{:S(2)}) async-start(), calls=%async_computation.13 | async-start | bytes 3538944 | tf_op jit(solution)/shard_map/all_gather | solution.py:206
  721.6 244.4 %all-to-all-start.1 = ((bf16[8,2,128,1536]{3,2,1,0:T(8,128)(2,1)}), bf16[8,2,128,1536]{3,2,1,0:T(8,128)(2,1)}, u32[]{:S(2)}, u32[]{:S(2)}) async-start(bf16[8,2,128,1536]{3,2,1,0:T(8,128)(2,1)} %copy.310), calls=%async_computation.1 | async-start | bytes 12582912 | tf_op jit(solution)/shard_map/all_to_all | solution.py:254
  726.4 1029.5 %reduce-scatter.17.cloned.1.call-start = ((), (), s32[]{:S(2)}) async-start(), calls=%async_computation.17 | async-start | bytes 7077888 | tf_op jit(solution)/shard_map/reduce_scatter | solution.py:345
  930.5 19.7 copy-start.66
  995.6 282.7 %copy-start.30 = (f32[256,6]{1,0:T(8,128)}, f32[256,6]{1,0:T(8,128)S(1)}, u32[]{:S(2)}) copy-start(f32[256,6]{1,0:T(8,128)S(1)} %get-tuple-element.1625) | copy-start | bytes 18436
  1009.0 232.8 %all-to-all-start.2 = ((bf16[8,2,128,1536]{3,2,1,0:T(8,128)(2,1)}), bf16[8,2,128,1536]{3,2,1,0:T(8,128)(2,1)}, u32[]{:S(2)}, u32[]{:S(2)}) async-start(bf16[8,2,128,1536]{3,2,1,0:T(8,128)(2,1)} %bitcast.601), calls=%async_computation.2 | async-start | bytes 12582912 | tf_op jit(solution)/shard_map/all_to_all | solution.py:287
  1013.8 742.0 %reduce-scatter.15.cloned.1.call-start = ((), (), s32[]{:S(2)}) async-start(), calls=%async_computation.16 | async-start | bytes 14155776 | tf_op jit(solution)/shard_map/reduce_scatter | solution.py:344
  1265.9 145.3 %all-to-all-start.3 = ((bf16[8,2,128,1536]{3,2,1,0:T(8,128)(2,1)}), bf16[8,2,128,1536]{3,2,1,0:T(8,128)(2,1)}, u32[]{:S(2)}, u32[]{:S(2)}) async-start(bf16[8,2,128,1536]{3,2,1,0:T(8,128)(2,1)} %copy.320), calls=%async_computation.3 | async-start | bytes 12582912 | tf_op jit(solution)/shard_map/all_to_all | solution.py:304
  1272.1 483.8 %reduce-scatter.13.cloned.1.call-start = ((), (), s32[]{:S(2)}) async-start(), calls=%async_computation.15 | async-start | bytes 21233664 | tf_op jit(solution)/shard_map/reduce_scatter | solution.py:341
  1278.5 172.2 %copy-start.84 = (bf16[256,16]{0,1:T(8,128)(2,1)}, bf16[256,16]{0,1:T(8,128)(2,1)S(1)}, u32[]{:S(2)}) copy-start(bf16[256,16]{0,1:T(8,128)(2,1)S(1)} %select_reduce_fusion) | copy-start | bytes 24580
  1433.4 17.3 copy-start.44
  1433.4 17.3 copy-start.67
  1433.4 17.3 copy-start.79
  1433.4 17.3 copy-start.103
  1463.0 650.0 %reduce-scatter.11.cloned.1.call-start = ((), (), s32[]{:S(2)}) async-start(), calls=%async_computation.14 | async-start | bytes 45121536 | tf_op jit(solution)/shard_map/reduce_scatter | solution.py:334
  1727.6 418.1 %reduce-scatter.21.cloned.1.call-start = ((), (), s32[]{:S(2)}) async-start(), calls=%async_computation.19 | async-start | bytes 884736
  1730.2 459.9 %reduce-scatter.19.cloned.1.call-start = ((), (), s32[]{:S(2)}) async-start(), calls=%async_computation.18 | async-start | bytes 1916928
  1746.1 945.8 %all-reduce.40.cloned.1.call-start = ((), (), s32[]{:S(2)}) async-start(), calls=%async_computation.20 | async-start | bytes 57212928 | tf_op jit(solution)/shard_map/psum | solution.py:347
  2147.0 40.3 %copy-start.115 = (f32[256]{0:T(256)S(1)}, f32[256]{0:T(256)}, u32[]{:S(2)}) copy-start(f32[256]{0:T(256)} %copy-done.114) | copy-start | bytes 3076
  2147.0 40.3 %copy-start.26 = (f32[256,1536]{1,0:T(8,128)S(1)}, f32[256,1536]{1,0:T(8,128)}, u32[]{:S(2)}) copy-start(f32[256,1536]{1,0:T(8,128)} %copy-done.24) | copy-start | bytes 4718596
  (149 other events, 920.8 us)
Sparse Core Ops, SparseCore 0:
  9.8 186.9 all-gather.7
  198.4 88.9 all-gather.9
  289.1 63.1 all-gather.11
  536.5 67.8 all-gather.13
  742.3 154.9 reduce-scatter.16
  1022.0 232.3 reduce-scatter.14
  1463.2 186.8 reduce-scatter.12
  1727.8 385.2 reduce-scatter.10
  2115.9 29.8 reduce-scatter.20
  2148.6 33.1 reduce-scatter.18
  2187.0 504.8 all-reduce.39
where the time goes:
time: 2740 us; the launch traced here: 2730 us
  waiting for transfers between devices  1470 us (54%)
  local copies, waits for them, and re-layouts  500 us (18%)
  blocking collectives  305 us (11%)
  matrix products  263 us (10%)
  other arithmetic  142 us (5%)
    psum x1, waiting for transfers between devices, shards(): lax.psum((dense_grads[0], dense_grads[1], dense_grads[2], dense_grads[3],...  483 us
    reduce_scatter x1, waiting for transfers between devices, shards(): lax.psum_scatter(in_proj_grad, 'shard', scatter_dimension=0, tiled=True)  357 us
    dynamic_update_slice x38, local copies, waits for them, and re-layouts, state_scan(): final_carry, outputs = lax.scan(advance, start_carry, pieces)  236 us
    all_to_all x1, waiting for transfers between devices, shards(): lax.all_to_all(send_grad, 'shard', split_axis=0, concat_axis=0, tiled=True)  220 us
    all_gather x1, blocking collectives, shards(): lax.all_gather(router, 'shard', axis=0, tiled=True)  188 us
    all_to_all x1, waiting for transfers between devices, shards(): lax.all_to_all(send_rows, 'shard', split_axis=0, concat_axis=0, tiled=True)  164 us
    all_to_all x1, waiting for transfers between devices, shards(): lax.all_to_all(row_grad, 'shard', split_axis=0, concat_axis=0, tiled=True)  133 us
    all_gather x1, waiting for transfers between devices, shards(): lax.all_gather(in_proj, 'shard', axis=0, tiled=True)  89.8 us
  transfers between devices with their start and end apart: 18, of which 8 were waited for; matrix products, arithmetic and copies ran while one was open for 32% of the time, Pallas kernels for 0%

commit v1 on v0

v1 whole, which is shorter than its diff:
```python
import functools

import jax
import jax.numpy as jnp
from jax import lax
from jax.experimental import pallas as pl
from jax.experimental.pallas import tpu as pltpu
from jax.sharding import Mesh
from jax.sharding import PartitionSpec as P

EPS = 1e-05
HIGH = lax.Precision.HIGHEST
F32 = jnp.float32
BF16 = jnp.bfloat16
ALL = ("rep", "z", "core")
COLUMN = ("z", "core")
PLANE = ("rep", "core")
LANES = 128


def rms_rows(values):
    return lax.rsqrt(jnp.mean(values * values, axis=-1, keepdims=True) + EPS)


def mm(left, right):
    return jnp.dot(left, right, preferred_element_type=F32)


def mm_nt(left, right):
    return lax.dot_general(left, right, (((1,), (1,)), ((), ())), preferred_element_type=F32)


def mm_tn(left, right):
    return lax.dot_general(left, right, (((0,), (0,)), ((), ())), preferred_element_type=F32)


def silu_slope(values, sig):
    return sig * (1.0 + values * (1.0 - sig))


def split_two(values):
    high = values.astype(BF16)
    return high, (values - high.astype(F32)).astype(BF16)


class Block:
    def __init__(self, proj, seg_col, seg_row, taps, heads, channels, width, state):
        rows = proj.shape[0]
        self.rows, self.channels, self.width, self.state = rows, channels, width, state
        self.gate = proj[:, :channels]
        self.xbc = proj[:, channels : 2 * channels + 2 * state]
        self.turn = lax.axis_index("core") * (LANES // 2)
        dt_raw = pltpu.roll(proj[:, 2 * channels + 2 * state :], self.turn, 1)
        position = lax.broadcasted_iota(jnp.int32, (rows, 1), 0)
        seg_wide = jnp.broadcast_to(seg_col, (rows, LANES))
        self.masks = []
        conv = taps[4:5, :] + taps[3:4, :] * self.xbc
        for offset in (1, 2, 3):
            before = pltpu.roll(seg_wide, offset, 0)[:, :1]
            mask = jnp.where((before == seg_col) & (position >= offset), 1.0, 0.0)
            self.masks.append(mask)
            conv = conv + taps[3 - offset : 4 - offset, :] * (mask * pltpu.roll(self.xbc, offset, 0))
        self.conv = conv
        self.conv_sig = jax.nn.sigmoid(conv)
        act = conv * self.conv_sig
        self.xin = act[:, :channels]
        self.write = act[:, channels : channels + state].astype(BF16)
        self.read = act[:, channels + state :].astype(BF16)
        shifted = dt_raw + heads[0:1, :]
        self.step = jnp.maximum(shifted, 0.0) + jnp.log1p(jnp.exp(-jnp.abs(shifted)))
        self.step_sig = jax.nn.sigmoid(shifted)
        self.speed = heads[1:2, :]
        self.rate = -self.step * self.speed
        row_at = lax.broadcasted_iota(jnp.int32, (rows, rows), 0)
        col_at = lax.broadcasted_iota(jnp.int32, (rows, rows), 1)
        self.causal = row_at >= col_at
        self.keep = self.causal & (seg_col == seg_row)
        self.cum = jnp.dot(self.causal.astype(F32), self.rate, precision=HIGH, preferred_element_type=F32)
        self.cum_t = self.cum.T
        self.scores = jnp.where(self.keep, mm_nt(self.read, self.write), 0.0)

    def groups(self):
        for start in range(0, self.channels, LANES):
            stop = min(start + LANES, self.channels)
            yield start, stop, list(range(start // self.width, (stop - 1) // self.width + 1))

    def spread(self, columns, start, stop, heads):
        lane = lax.broadcasted_iota(jnp.int32, (self.rows, stop - start), 1) + start
        result = jnp.broadcast_to(columns[:, heads[0] : heads[0] + 1], (self.rows, stop - start))
        for head in heads[1:]:
            result = jnp.where(lane >= head * self.width, columns[:, head : head + 1], result)
        return result

    def inside(self, start, stop, head):
        lane = lax.broadcasted_iota(jnp.int32, (self.rows, stop - start), 1) + start
        return (lane >= head * self.width) & (lane < (head + 1) * self.width)

    def decay(self, head):
        gaps = self.cum[:, head : head + 1] - self.cum_t[head : head + 1, :]
        return jnp.exp(jnp.where(self.keep, gaps, 0.0))


def mixer_forward_kernel(
    channels, width, state,
    x_ref, gain_ref, weight_ref, seg_col_ref, seg_row_ref, taps_ref, heads_ref, skip_ref, norm_ref, out_ref,
    part_ref, square_ref, proj_ref,
):
    x = x_ref[...].astype(F32)
    first = (x * rms_rows(x) * gain_ref[...]).astype(BF16)
    proj = mm(first, weight_ref[...])
    proj_ref[...] = proj
    block = Block(proj, seg_col_ref[...], seg_row_ref[...], taps_ref[...], heads_ref[...], channels, width, state)
    rows = block.rows
    mixed = []
    for start, stop, heads in block.groups():
        xin = block.xin[:, start:stop]
        scaled = (xin * block.spread(block.step, start, stop, heads)).astype(BF16)
        y = None
        for head in heads:
            weights = (block.scores * block.decay(head)).astype(BF16)
            term = mm(weights, scaled)
            y = term if y is None else jnp.where(block.inside(start, stop, head), term, y)
        gate = block.gate[:, start:stop]
        mixed.append((y + skip_ref[:, start:stop] * xin) * gate * jax.nn.sigmoid(gate))
    mixed = jnp.concatenate(mixed, axis=1)
    square_ref[...] = row_of(jnp.sum(mixed * mixed, axis=1, keepdims=True), rows)
    part_ref[...] = mm((mixed * norm_ref[...]).astype(BF16), out_ref[...]).astype(BF16)


def mixer_backward_kernel(
    channels, width, state,
    x_ref, gain_ref, weight_ref, seg_col_ref, seg_row_ref, taps_ref, heads_ref, skip_ref, norm_ref, out_ref,
    proj_ref, low_ref, scale_ref,
    back_ref, in_grad_ref, out_grad_ref, taps_grad_ref, heads_grad_ref, wide_grad_ref,
):
    block_at = pl.program_id(0)

    @pl.when(block_at == 0)
    def _():
        in_grad_ref[...] = jnp.zeros_like(in_grad_ref)
        out_grad_ref[...] = jnp.zeros_like(out_grad_ref)
        taps_grad_ref[...] = jnp.zeros_like(taps_grad_ref)
        heads_grad_ref[...] = jnp.zeros_like(heads_grad_ref)
        wide_grad_ref[...] = jnp.zeros_like(wide_grad_ref)

    block = Block(
        proj_ref[...], seg_col_ref[...], seg_row_ref[...], taps_ref[...], heads_ref[...], channels, width, state
    )
    rows = block.rows
    low = low_ref[...]
    scale = column_of(scale_ref[0, 0:1, :], rows)
    pull = column_of(scale_ref[1, 0:1, :], rows)
    normed_grad = mm_nt(low, out_ref[...])
    taps = taps_ref[...]
    gate_grads, x_grads, mixed_all, norm_grads, skip_grads = [], [], [], [], []
    step_grad = jnp.zeros((rows, LANES), F32)
    cum_grad = jnp.zeros((rows, LANES), F32)
    cum_grad_t = jnp.zeros((LANES, rows), F32)
    score_grad = jnp.zeros((rows, rows), F32)
    lane_all = lax.broadcasted_iota(jnp.int32, (rows, LANES), 1)
    sub_all = lax.broadcasted_iota(jnp.int32, (LANES, rows), 0)
    for start, stop, heads in block.groups():
        xin = block.xin[:, start:stop]
        spread = block.spread(block.step, start, stop, heads)
        scaled = (xin * spread).astype(BF16)
        weights, decays = [], []
        y = None
        for head in heads:
            decays.append(block.decay(head))
            weights.append(block.scores * decays[-1])
            term = mm(weights[-1].astype(BF16), scaled)
            y = term if y is None else jnp.where(block.inside(start, stop, head), term, y)
        skip = skip_ref[:, start:stop]
        y = y + skip * xin
        gate = block.gate[:, start:stop]
        gate_sig = jax.nn.sigmoid(gate)
        gate_act = gate * gate_sig
        mixed = y * gate_act
        mixed_all.append(mixed)
        q = normed_grad[:, start:stop]
        norm_grads.append(jnp.sum(mixed * scale * q, axis=0, keepdims=True))
        mixed_grad = scale * norm_ref[:, start:stop] * q - mixed * pull
        gate_grads.append(mixed_grad * y * silu_slope(gate, gate_sig))
        y_grad = mixed_grad * gate_act
        skip_grads.append(jnp.sum(y_grad * xin, axis=0, keepdims=True))
        y_low = y_grad.astype(BF16)
        scaled_grad = None
        for at, head in enumerate(heads):
            inside = block.inside(start, stop, head)
            term = mm_tn(weights[at].astype(BF16), y_low)
            scaled_grad = term if scaled_grad is None else jnp.where(inside, term, scaled_grad)
            pair_grad = mm_nt(jnp.where(inside, y_low, jnp.zeros_like(y_low)), scaled)
            score_grad = score_grad + pair_grad * decays[at]
            exponent_grad = pair_grad * weights[at]
            cum_grad = jnp.where(lane_all == head, jnp.sum(exponent_grad, axis=1, keepdims=True), cum_grad)
            cum_grad_t = jnp.where(sub_all == head, jnp.sum(exponent_grad, axis=0, keepdims=True), cum_grad_t)
        for head in heads:
            inside = block.inside(start, stop, head)
            per_row = jnp.sum(jnp.where(inside, scaled_grad * xin, 0.0), axis=1, keepdims=True)
            step_grad = jnp.where(lane_all == head, per_row, step_grad)
        x_grads.append(scaled_grad * spread + skip * y_grad)
    score_grad = jnp.where(block.keep, score_grad, 0.0).astype(BF16)
    read_grad = mm(score_grad, block.write)
    write_grad = mm_tn(score_grad, block.read)
    cum_grad = cum_grad - cum_grad_t.T
    rate_grad = lax.dot_general(
        block.causal.astype(F32), cum_grad, (((0,), (0,)), ((), ())), precision=HIGH, preferred_element_type=F32
    )
    step_grad = step_grad - block.speed * rate_grad
    dt_grad = step_grad * block.step_sig
    heads_grad_ref[0:1, :] += jnp.sum(dt_grad, axis=0, keepdims=True)
    heads_grad_ref[1:2, :] += jnp.sum(rate_grad * block.rate, axis=0, keepdims=True)
    act_grad = jnp.concatenate(x_grads + [write_grad, read_grad], axis=1)
    conv_grad = act_grad * silu_slope(block.conv, block.conv_sig)
    taps_grad_ref[4:5, :] += jnp.sum(conv_grad, axis=0, keepdims=True)
    taps_grad_ref[3:4, :] += jnp.sum(conv_grad * block.xbc, axis=0, keepdims=True)
    xbc_grad = taps[3:4, :] * conv_grad
    for offset in (1, 2, 3):
        masked = conv_grad * block.masks[offset - 1]
        taps_grad_ref[3 - offset : 4 - offset, :] += jnp.sum(
            masked * pltpu.roll(block.xbc, offset, 0), axis=0, keepdims=True
        )
        xbc_grad = xbc_grad + taps[3 - offset : 4 - offset, :] * pltpu.roll(masked, rows - offset, 0)
    wide_grad_ref[0:1, :] += jnp.concatenate(norm_grads, axis=1)
    wide_grad_ref[1:2, :] += jnp.concatenate(skip_grads, axis=1)
    proj_grad = jnp.concatenate(gate_grads + [xbc_grad, pltpu.roll(dt_grad, block.turn, 1)], axis=1).astype(BF16)
    back_ref[...] = mm_nt(proj_grad, weight_ref[...]).astype(BF16)
    x = x_ref[...].astype(F32)
    first = (x * rms_rows(x) * gain_ref[...]).astype(BF16)
    in_grad_ref[...] += mm_tn(first, proj_grad)
    normed = (jnp.concatenate(mixed_all, axis=1) * scale * norm_ref[...]).astype(BF16)
    out_grad_ref[...] += mm_tn(normed, low)


def whole(shape):
    return pl.BlockSpec(shape, lambda i: (0,) * len(shape))


def by_rows(shape):
    return pl.BlockSpec(shape, lambda i: (i,) + (0,) * (len(shape) - 1))


def mixer_specs(rows, model, channels, state):
    wide = 2 * channels + 2 * state + LANES
    return [
        by_rows((rows, model)),
        whole((1, model)),
        whole((model, wide)),
        by_rows((rows, 1)),
        pl.BlockSpec((None, 1, rows), lambda i: (i, 0, 0)),
        whole((8, channels + 2 * state)),
        whole((8, LANES)),
        whole((1, channels)),
        whole((1, channels)),
        whole((channels, model)),
    ]


def mixer_forward(args, rows, channels, width, state):
    total, model = args[0].shape
    wide = 2 * channels + 2 * state + LANES
    return pl.pallas_call(
        functools.partial(mixer_forward_kernel, channels, width, state),
        grid=(total // rows,),
        in_specs=mixer_specs(rows, model, channels, state),
        out_specs=[
            by_rows((rows, model)),
            pl.BlockSpec((None, 8, rows), lambda i: (i, 0, 0)),
            by_rows((rows, wide)),
        ],
        out_shape=[
            jax.ShapeDtypeStruct((total, model), BF16),
            jax.ShapeDtypeStruct((total // rows, 8, rows), F32),
            jax.ShapeDtypeStruct((total, wide), F32),
        ],
        compiler_params=pltpu.CompilerParams(vmem_limit_bytes=56 * 2**20),
        name="mixer_forward",
    )(*args)


def mixer_backward(args, proj, low, scale, rows, channels, width, state):
    total, model = args[0].shape
    wide = 2 * channels + 2 * state + LANES
    return pl.pallas_call(
        functools.partial(mixer_backward_kernel, channels, width, state),
        grid=(total // rows,),
        in_specs=mixer_specs(rows, model, channels, state)
        + [
            by_rows((rows, wide)),
            by_rows((rows, model)),
            pl.BlockSpec((None, 2, 8, rows), lambda i: (i, 0, 0, 0)),
        ],
        out_specs=[
            by_rows((rows, model)),
            whole((model, wide)),
            whole((channels, model)),
            whole((8, channels + 2 * state)),
            whole((8, LANES)),
            whole((8, channels)),
        ],
        out_shape=[
            jax.ShapeDtypeStruct((total, model), BF16),
            jax.ShapeDtypeStruct((model, wide), F32),
            jax.ShapeDtypeStruct((channels, model), F32),
            jax.ShapeDtypeStruct((8, channels + 2 * state), F32),
            jax.ShapeDtypeStruct((8, LANES), F32),
            jax.ShapeDtypeStruct((8, channels), F32),
        ],
        compiler_params=pltpu.CompilerParams(vmem_limit_bytes=60 * 2**20),
        name="mixer_backward",
    )(*args, proj, low, scale)


MESH_ID = pl.DeviceIdType.MESH


def when(condition, action):
    if condition is True:
        action()
    elif condition is not False:
        pl.when(condition)(action)


class Place:
    def __init__(self, reps, depth):
        self.reps, self.depth = reps, depth
        self.rep, self.z, self.core = lax.axis_index("rep"), lax.axis_index("z"), lax.axis_index("core")
        self.here = {"rep": self.rep, "z": self.z, "core": self.core}
        self.pending = []

    def device(self, **changes):
        return {**self.here, **changes}

    def sibling(self):
        return self.device(core=1 - self.core)

    def rep_at(self, distance):
        return lax.rem(self.rep + distance, self.reps)

    def barrier(self, plane=False, column=False, everyone=False):
        semaphore = pltpu.get_barrier_semaphore()

        def greet(device):
            pl.semaphore_signal(semaphore, inc=1, device_id=device, device_id_type=MESH_ID)

        if everyone:
            count = self.reps * self.depth * 2
            mine = (self.rep * self.depth + self.z) * 2 + self.core

            def step(distance, carry):
                other = lax.rem(mine + distance, count)
                greet({"rep": other // (2 * self.depth), "z": lax.rem(other // 2, self.depth), "core": lax.rem(other, 2)})
                return carry

            lax.fori_loop(1, count, step, 0)
            pl.semaphore_wait(semaphore, count - 1)
            return
        amount = 1
        greet(self.sibling())
        if plane:
            for distance in range(1, self.reps):
                greet(self.device(rep=self.rep_at(distance)))
            amount = amount + self.reps - 1
        if column:
            above, below = self.z < self.depth - 1, self.z > 0
            when(above, lambda: greet(self.device(z=self.z + 1)))
            when(below, lambda: greet(self.device(z=self.z - 1)))
            amount = amount + jnp.where(above, 1, 0) + jnp.where(below, 1, 0)
        pl.semaphore_wait(semaphore, amount)

    def send(self, source, target, send_sem, recv_sem, device, condition=True):
        copy = pltpu.make_async_remote_copy(
            src_ref=source, dst_ref=target, send_sem=send_sem, recv_sem=recv_sem, device_id=device,
            device_id_type=MESH_ID,
        )
        when(condition, copy.start)
        self.pending.append((condition, copy))

    def local(self, source, target, sem):
        copy = pltpu.make_async_copy(source, target, sem)
        copy.start()
        return copy

    def arrived(self, target, recv_sem, condition=True):
        copy = pltpu.make_async_remote_copy(
            src_ref=target, dst_ref=target, send_sem=recv_sem, recv_sem=recv_sem, device_id=self.sibling(),
            device_id_type=MESH_ID,
        )
        when(condition, copy.wait_recv)

    def finish(self):
        for condition, copy in self.pending:
            when(condition, copy.wait_send)
        self.pending = []


class PlaneGather:
    @staticmethod
    def scratch(reps):
        return [pltpu.SemaphoreType.DMA((4, reps)), pltpu.SemaphoreType.DMA((1,))]

    def __init__(self, place, own, out, sems, local_sem):
        self.place, self.out, self.sems = place, out, sems
        p = place
        self.keep = p.local(own, out.at[p.rep, p.core], local_sem.at[0])
        for distance in range(1, p.reps):
            p.send(own, out.at[p.rep, p.core], sems.at[0, distance], sems.at[1, distance],
                   p.device(rep=p.rep_at(distance)))
        p.send(own, out.at[p.rep, p.core], sems.at[2, 0], sems.at[3, 0], p.sibling())

    def relay(self):
        p = self.place
        for distance in range(1, p.reps):
            source = self.out.at[p.rep_at(p.reps - distance), p.core]
            p.arrived(source, self.sems.at[1, distance])
            p.send(source, source, self.sems.at[2, distance], self.sems.at[3, distance], p.sibling())

    def finish(self):
        p = self.place
        self.keep.wait()
        for distance in range(p.reps):
            source = p.rep_at(p.reps - distance) if distance else p.rep
            p.arrived(self.out.at[source, 1 - p.core], self.sems.at[3, distance])


class ColumnGather:
    @staticmethod
    def scratch(depth):
        return [pltpu.SemaphoreType.DMA((8, depth)), pltpu.SemaphoreType.DMA((1,))]

    def __init__(self, place, own, slot, sems, local_sem, shared=None, keep=True):
        self.place, self.slot, self.sems, self.shared = place, slot, sems, shared
        p = place
        self.keep = p.local(own, slot(p.z), local_sem.at[0]) if keep else None
        self.onward(own, slot(p.z), 0, True, True)
        if shared is not None:
            p.send(own, slot(p.z), sems.at[4, 0], sems.at[5, 0], p.sibling())

    def onward(self, source, target, distance, up, down):
        p = self.place
        if up is not False:
            p.send(source, target, self.sems.at[0, distance], self.sems.at[1, distance], p.device(z=p.z + 1),
                   (p.z < p.depth - 1) if up is True else up & (p.z < p.depth - 1))
        if down is not False:
            p.send(source, target, self.sems.at[2, distance], self.sems.at[3, distance], p.device(z=p.z - 1),
                   (p.z > 0) if down is True else down & (p.z > 0))

    def hop(self, distance):
        p = self.place
        below, above = p.z >= distance, p.z + distance < p.depth
        low, high = self.slot(jnp.maximum(p.z - distance, 0)), self.slot(jnp.minimum(p.z + distance, p.depth - 1))
        p.arrived(low, self.sems.at[1, distance - 1], below)
        self.onward(low, low, distance, below, False)
        if self.shared is not None:
            p.send(low, low, self.sems.at[4, distance], self.sems.at[5, distance], p.sibling(), below)
        p.arrived(high, self.sems.at[3, distance - 1], above)
        self.onward(high, high, distance, False, above)
        if self.shared is not None:
            p.send(high, high, self.sems.at[6, distance], self.sems.at[7, distance], p.sibling(), above)

    def finish(self):
        p = self.place
        if self.keep is not None:
            self.keep.wait()
        if self.shared is None:
            return
        p.arrived(self.shared(p.z), self.sems.at[5, 0])
        for distance in range(1, p.depth):
            below, above = p.z >= distance, p.z + distance < p.depth
            p.arrived(self.shared(jnp.maximum(p.z - distance, 0)), self.sems.at[5, distance], below)
            p.arrived(self.shared(jnp.minimum(p.z + distance, p.depth - 1)), self.sems.at[7, distance], above)


def add_up(*terms):
    total = terms[0].astype(F32)
    for term in terms[1:]:
        total = total + term.astype(F32)
    return total


class PlaneSum:
    @staticmethod
    def scratch(reps, shape, dtype):
        return [
            pltpu.VMEM((reps,) + shape, dtype), pltpu.VMEM((reps,) + shape, dtype), pltpu.VMEM((reps,) + shape, dtype),
            pltpu.SemaphoreType.DMA((4, reps)),
        ]

    def __init__(self, place, parts, pair, out, into, sems):
        self.place, self.parts, self.pair, self.out, self.into, self.sems = place, parts, pair, out, into, sems
        p = place
        for distance in list(range(1, p.reps)) + [0]:
            rep = p.rep_at(distance) if distance else p.rep
            p.send(parts.at[rep, 1 - p.core], pair.at[distance], sems.at[0, distance], sems.at[1, distance], p.sibling())

    def relay(self):
        p = self.place
        for distance in range(1, p.reps):
            rep = p.rep_at(distance)
            p.arrived(self.pair.at[distance], self.sems.at[1, distance])
            self.out[distance] = add_up(self.parts[rep, p.core], self.pair[distance]).astype(self.out.dtype)
            p.send(self.out.at[distance], self.into.at[distance], self.sems.at[2, distance], self.sems.at[3, distance],
                   p.device(rep=rep))

    def total(self):
        p = self.place
        p.arrived(self.pair.at[0], self.sems.at[1, 0])
        terms = [self.parts[p.rep, p.core], self.pair[0]]
        for distance in range(1, p.reps):
            p.arrived(self.into.at[distance], self.sems.at[3, distance])
            terms.append(self.into[distance])
        return add_up(*terms)


class ColumnSum:
    @staticmethod
    def scratch(depth, shape, dtype):
        return [
            pltpu.VMEM((depth,) + shape, dtype), pltpu.VMEM((2, depth) + shape, dtype),
            pltpu.VMEM((2, depth) + shape, dtype), pltpu.SemaphoreType.DMA((2, depth)),
            pltpu.SemaphoreType.DMA((4, depth)),
        ]

    def __init__(self, place, parts, pair, out, into, pair_sems, sems):
        self.place, self.parts, self.pair, self.out, self.into = place, parts, pair, out, into
        self.pair_sems, self.sems = pair_sems, sems
        p = place
        for distance in list(range(p.depth - 1, 0, -1)) + [0]:
            at = lax.rem(p.z + distance, p.depth)
            p.send(parts.at[at, 1 - p.core], pair.at[at], pair_sems.at[0, at], pair_sems.at[1, at], p.sibling())
        for distance in list(range(p.depth - 1, 0, -1)) + [0]:
            at = lax.rem(p.z + distance, p.depth)
            p.arrived(pair.at[at], pair_sems.at[1, at])

    def step(self, at):
        p = self.place
        last = p.depth - 1
        for way, towards, goal, first, valid in (
            (0, p.z + 1, last - (at - p.z), p.z == 0, (at >= p.z) & (last - (at - p.z) > p.z)),
            (1, p.z - 1, at - (last - p.z), p.z == last, (at >= last - p.z) & (at - (last - p.z) < p.z)),
        ):
            goal = jnp.clip(goal, 0, last)
            p.arrived(self.into.at[way, goal], self.sems.at[2 * way + 1, goal], valid & jnp.logical_not(first))

            def start(goal=goal, way=way):
                self.out[way, goal] = add_up(self.parts[goal, p.core], self.pair[goal]).astype(self.out.dtype)

            def follow(goal=goal, way=way):
                self.out[way, goal] = add_up(
                    self.parts[goal, p.core], self.pair[goal], self.into[way, goal]
                ).astype(self.out.dtype)

            when(valid & first, start)
            when(valid & jnp.logical_not(first), follow)
            p.send(self.out.at[way, goal], self.into.at[way, goal], self.sems.at[2 * way, goal],
                   self.sems.at[2 * way + 1, goal], p.device(z=towards), valid)

    def total(self, result):
        p = self.place
        result[...] = add_up(self.parts[p.z, p.core], self.pair[p.z])
        for way, condition in ((0, p.z > 0), (1, p.z < p.depth - 1)):
            p.arrived(self.into.at[way, p.z], self.sems.at[2 * way + 1, p.z], condition)

            def add(way=way):
                result[...] += self.into[way, p.z].astype(F32)

            when(condition, add)


def anywhere(count):
    return [pl.BlockSpec(memory_space=pl.ANY)] * count


def in_vmem(count):
    return [pl.BlockSpec(memory_space=pltpu.VMEM)] * count


def remote_params(identity, mebibytes=60):
    return pltpu.CompilerParams(
        collective_id=identity, has_side_effects=True, vmem_limit_bytes=mebibytes * 2**20
    )


def start_gather(tokens, own_pair, other_pair, common, pack, numbers, out_quarters, reps, depth):
    rows, model = tokens.shape
    part, side = own_pair.shape
    wide = side + common.shape[1]

    def kernel(x_ref, own_ref, other_ref, common_ref, pack_ref, numbers_ref, quarters_ref,
               x_out, weight_out, pack_out, numbers_out, out_out, mid_out,
               x_sems, x_local, a_sems, a_local, b_sems, b_local, c_sems, c_local, p_sems, p_local,
               n_sems, n_local, o_sems, o_local, e_sems, swap_sems):
        p = Place(reps, depth)
        p.barrier(everyone=True)

        def left(core):
            return lambda z: weight_out.at[z, core, :, pl.ds(0, side)]

        def right(core):
            return lambda z: weight_out.at[z, core, :, pl.ds(side, wide - side)]

        slot = left(p.core)
        p.send(other_ref, slot(p.z), swap_sems.at[0], swap_sems.at[1], p.sibling())
        pack_job = ColumnGather(p, pack_ref, lambda z: pack_out.at[z, p.core], p_sems, p_local,
                                shared=lambda z: pack_out.at[z, 1 - p.core])
        count = reps * depth * 2
        mine = (p.rep * depth + p.z) * 2 + p.core
        number_keep = p.local(numbers_ref, numbers_out.at[mine], n_local.at[0])

        def number_copy(distance, other):
            return pltpu.make_async_remote_copy(
                src_ref=numbers_ref, dst_ref=numbers_out.at[mine], send_sem=n_sems.at[0, distance],
                recv_sem=n_sems.at[1, distance],
                device_id={"rep": other // (2 * depth), "z": lax.rem(other // 2, depth), "core": lax.rem(other, 2)},
                device_id_type=MESH_ID,
            )

        def number_send(distance, carry):
            number_copy(distance, lax.rem(mine + distance, count)).start()
            return carry

        lax.fori_loop(1, count, number_send, 0)
        job_a = ColumnGather(p, own_ref, slot, a_sems, a_local)
        job_c = ColumnGather(p, common_ref, right(p.core), c_sems, c_local, shared=right(1 - p.core))
        x_job = PlaneGather(p, x_ref, x_out, x_sems, x_local)
        other = left(1 - p.core)
        p.arrived(other(p.z), swap_sems.at[1])
        job_b = ColumnGather(p, other(p.z), other, b_sems, b_local, keep=False)
        job_o = ColumnGather(p, quarters_ref.at[p.rep], lambda z: mid_out.at[z], o_sems, o_local)
        for distance in range(1, depth):
            pack_job.hop(distance)
            job_a.hop(distance)
            job_c.hop(distance)
            job_b.hop(distance)
            if distance == 1:
                x_job.relay()
            job_o.hop(distance)
        job_o.finish()
        for distance in range(1, reps):
            rep = p.rep_at(distance)
            p.send(mid_out.at[rep], out_out.at[p.rep], e_sems.at[0, distance], e_sems.at[1, distance], p.device(rep=rep))
        out_keep = p.local(mid_out.at[p.rep], out_out.at[p.rep], o_local.at[0])
        for job in (x_job, pack_job, job_a, job_b, job_c):
            job.finish()
        number_keep.wait()

        def number_wait(distance, carry):
            copy = number_copy(distance, lax.rem(mine + distance, count))
            copy.wait_send()
            copy.wait_recv()
            return carry

        lax.fori_loop(1, count, number_wait, 0)
        out_keep.wait()
        for distance in range(1, reps):
            p.arrived(out_out.at[p.rep_at(reps - distance)], e_sems.at[1, distance])
        p.finish()

    quarter = out_quarters.shape[1]
    return pl.pallas_call(
        kernel,
        in_specs=anywhere(7),
        out_specs=anywhere(6),
        out_shape=[
            jax.ShapeDtypeStruct((reps, 2, rows, model), BF16),
            jax.ShapeDtypeStruct((depth, 2, part, wide), BF16),
            jax.ShapeDtypeStruct((depth, 2) + pack.shape, BF16),
            jax.ShapeDtypeStruct((reps * depth * 2,) + numbers.shape, jnp.int32),
            jax.ShapeDtypeStruct((reps, quarter, model), BF16),
            jax.ShapeDtypeStruct((depth, quarter, model), BF16),
        ],
        scratch_shapes=PlaneGather.scratch(reps)
        + ColumnGather.scratch(depth) * 4
        + [pltpu.SemaphoreType.DMA((2, reps * depth * 2)), pltpu.SemaphoreType.DMA((1,))]
        + ColumnGather.scratch(depth)
        + [pltpu.SemaphoreType.DMA((2, reps)), pltpu.SemaphoreType.DMA((2,))],
        compiler_params=remote_params(0, 16),
        name="start_gather",
    )(tokens, own_pair, other_pair, common, pack, numbers, out_quarters)


def column_of(row_values, rows):
    return jnp.broadcast_to(row_values, (LANES, rows)).T[:, 0:1]


def row_of(column_values, rows):
    return jnp.broadcast_to(column_values, (rows, LANES)).T[0:8, :]


def join_mixer(parts, squares, tokens, post_gain, inner, reps, depth):
    rows, model = tokens.shape

    def kernel(parts_ref, squares_ref, x_ref, gain_ref, after_ref, mixed_ref, scale_ref, rows_out,
               pair, out, into, sems, s_pair, s_out, s_into, s_sems, second, g_sems, g_local):
        p = Place(reps, depth)
        p.barrier(plane=True, column=True)
        squares_job = PlaneSum(p, squares_ref, s_pair, s_out, s_into, s_sems)
        parts_job = PlaneSum(p, parts_ref, pair, out, into, sems)
        squares_job.relay()
        parts_job.relay()
        square = squares_job.total()
        scale_row = lax.rsqrt(square / inner + EPS)
        scale_ref[...] = scale_row
        mixed = column_of(scale_row[0:1, :], rows) * parts_job.total()
        mixed_ref[...] = mixed
        after = x_ref[...].astype(F32) + mixed
        after_ref[...] = after
        second[...] = (after * rms_rows(after) * gain_ref[...]).astype(BF16)
        job = ColumnGather(p, second, lambda z: rows_out.at[z, p.core], g_sems, g_local,
                           shared=lambda z: rows_out.at[z, 1 - p.core])
        for distance in range(1, depth):
            job.hop(distance)
        job.finish()
        p.finish()

    return pl.pallas_call(
        kernel,
        in_specs=in_vmem(4),
        out_specs=in_vmem(3) + anywhere(1),
        out_shape=[
            jax.ShapeDtypeStruct((rows, model), F32),
            jax.ShapeDtypeStruct((rows, model), F32),
            jax.ShapeDtypeStruct((8, rows), F32),
            jax.ShapeDtypeStruct((depth, 2, rows, model), BF16),
        ],
        scratch_shapes=PlaneSum.scratch(reps, (rows, model), BF16)
        + PlaneSum.scratch(reps, (8, rows), F32)
        + [pltpu.VMEM((rows, model), BF16)]
        + ColumnGather.scratch(depth),
        compiler_params=remote_params(1),
        name="join_mixer",
    )(parts, squares, tokens, post_gain)


def join_experts(parts, cotangent, after, mixed, scale, post_gain, inner, reps, depth):
    rows, model = cotangent.shape

    def kernel(parts_ref, g_ref, after_ref, mixed_ref, scale_ref, gain_ref,
               grad_ref, gain_grad_ref, low_out, scale_out,
               pair, out, into, pair_sems, sems, low, scales, l_sems, l_local, s_sems, s_local):
        p = Place(reps, depth)
        p.barrier(plane=True, column=True)
        job = ColumnSum(p, parts_ref, pair, out, into, pair_sems, sems)
        for at in range(depth - 1):
            job.step(at)
        job.total(grad_ref)
        second_grad = grad_ref[...]
        after_rows = after_ref[...]
        after_scale = rms_rows(after_rows)
        gain_grad_ref[...] = jnp.sum(after_rows * second_grad * after_scale, axis=0, keepdims=True)
        weighted = second_grad * gain_ref[...]
        after_grad = (
            g_ref[...].astype(F32)
            + after_scale * weighted
            - after_rows * after_scale**3 * jnp.mean(after_rows * weighted, axis=1, keepdims=True)
        )
        grad_ref[...] = after_grad
        after_low = after_grad.astype(BF16)
        low[...] = after_low
        scale_row = scale_ref[...]
        dot_row = row_of(jnp.sum(after_low.astype(F32) * mixed_ref[...], axis=1, keepdims=True), rows)
        scales[0] = scale_row
        scales[1] = scale_row**2 * dot_row / inner
        s_job = PlaneGather(p, scales, scale_out, s_sems, s_local)
        l_job = PlaneGather(p, low, low_out, l_sems, l_local)
        s_job.relay()
        l_job.relay()
        s_job.finish()
        l_job.finish()
        p.finish()

    return pl.pallas_call(
        kernel,
        in_specs=in_vmem(6),
        out_specs=in_vmem(2) + anywhere(2),
        out_shape=[
            jax.ShapeDtypeStruct((rows, model), F32),
            jax.ShapeDtypeStruct((1, model), F32),
            jax.ShapeDtypeStruct((reps, 2, rows, model), BF16),
            jax.ShapeDtypeStruct((reps, 2, 2, 8, rows), F32),
        ],
        scratch_shapes=ColumnSum.scratch(depth, (rows, model), BF16)
        + [pltpu.VMEM((rows, model), BF16), pltpu.VMEM((2, 8, rows), F32)]
        + PlaneGather.scratch(reps) * 2,
        compiler_params=remote_params(2),
        name="join_experts",
    )(parts, cotangent, after, mixed, scale, post_gain)


def join_input(parts, tokens, after_grad, in_gain, reps, depth):
    rows, model = tokens.shape

    def kernel(parts_ref, x_ref, grad_ref, gain_ref, tokens_grad_ref, gain_grad_ref, pair, out, into, sems):
        p = Place(reps, depth)
        p.barrier(plane=True)
        job = PlaneSum(p, parts_ref, pair, out, into, sems)
        job.relay()
        first_grad = job.total()
        x = x_ref[...].astype(F32)
        x_scale = rms_rows(x)
        gain_grad_ref[...] = jnp.sum(x * first_grad * x_scale, axis=0, keepdims=True)
        weighted = first_grad * gain_ref[...]
        tokens_grad_ref[...] = (
            grad_ref[...]
            + x_scale * weighted
            - x * x_scale**3 * jnp.mean(x * weighted, axis=1, keepdims=True)
        ).astype(BF16)
        p.finish()

    return pl.pallas_call(
        kernel,
        in_specs=in_vmem(4),
        out_specs=in_vmem(2),
        out_shape=[jax.ShapeDtypeStruct((rows, model), BF16), jax.ShapeDtypeStruct((1, model), F32)],
        scratch_shapes=PlaneSum.scratch(reps, (rows, model), BF16),
        compiler_params=remote_params(3),
        name="join_input",
    )(parts, tokens, after_grad, in_gain)


def gather(values, axes, axis=0):
    return lax.all_gather(values, axes, axis=axis, tiled=True)


def scatter_sum(values, axes, axis=0):
    return lax.psum_scatter(values, axes, scatter_dimension=axis, tiled=True)


def columns_of(values, start, size, axis=1):
    return lax.dynamic_slice_in_dim(values, start, size, axis=axis)


def shards(
    tokens,
    cotangent,
    dealt_to,
    lengths,
    routes,
    slot_index,
    in_norm,
    in_proj,
    conv_weight,
    conv_bias,
    dt_bias,
    decay_log,
    skip_gain,
    mixer_norm,
    out_proj,
    post_norm,
    router,
    shared_in,
    shared_out,
    expert_in,
    expert_out,
):
    reps, depth = lax.axis_size("rep"), lax.axis_size("z")
    group = 2 * depth
    rep, z, core = lax.axis_index("rep"), lax.axis_index("z"), lax.axis_index("core")
    shard = 2 * z + core
    team = 2 * rep + core
    members = 2 * reps
    rows, model = tokens.shape
    top = routes.shape[1]
    local = expert_in.shape[0]
    experts = local * group
    capacity = rows * top * 4 // (3 * experts)
    inner = mixer_norm.shape[0] * group
    convolved = conv_bias.shape[0] * group
    head_count = dt_bias.shape[0] * group
    width = inner // head_count
    state = (convolved - inner) // 2
    channels = inner // members
    heads = head_count // members
    shared = shared_out.shape[0]
    part = in_norm.shape[0]

    expert_ids = jnp.arange(experts, dtype=jnp.int32)
    table = jnp.sum(
        jnp.where(routes[:, None, :] == expert_ids[None, :, None], slot_index[:, None, :] + 1, 0), axis=2
    ).astype(BF16)
    numbers = jnp.pad(jnp.concatenate([lengths[0], dealt_to])[None, :], ((0, 7), (0, LANES - lengths.shape[1] - 1)))
    pieces = [
        table.T.reshape(-1), in_norm, conv_weight.reshape(-1), conv_bias, dt_bias, decay_log, skip_gain,
        mixer_norm, post_norm, router.reshape(-1),
    ]
    sizes = [piece.shape[0] for piece in pieces]
    pack = jnp.concatenate(pieces)
    pack_wide = -(-pack.shape[0] // (16 * LANES)) * LANES
    pack = jnp.pad(pack, (0, 16 * pack_wide - pack.shape[0])).reshape(16, pack_wide)
    pair_heads = 2 * heads
    dt_pair = columns_of(in_proj, inner + convolved + pair_heads * rep, pair_heads)
    blank = jnp.zeros((part, LANES // 2 - heads), BF16)
    common = jnp.concatenate(
        [in_proj[:, 2 * inner : 2 * inner + 2 * state], dt_pair[:, :heads], blank, dt_pair[:, heads:], blank], axis=1
    )

    def pair_of(member):
        return jnp.concatenate(
            [columns_of(in_proj, channels * member, channels), columns_of(in_proj, inner + channels * member, channels)],
            axis=1,
        )

    x_plane, weight, packed, numbers_all, out_own, _ = start_gather(
        tokens, pair_of(team), pair_of(2 * rep + 1 - core), common, pack, numbers,
        out_proj.reshape(reps, channels // reps, model), reps, depth,
    )
    x_plane = x_plane.reshape(members * rows, model)
    weight = weight.reshape(model, -1)
    out_own = out_own.reshape(channels, model)
    numbers_all = numbers_all[:, 0, :4].reshape(reps, group, 4)
    packed = packed.reshape(group, -1)
    unpacked, offset = [], 0
    for size in sizes:
        unpacked.append(packed[:, offset : offset + size])
        offset += size
    table_all = unpacked[0].reshape(group, experts, rows)
    in_gain = unpacked[1].reshape(1, model).astype(F32)
    taps_full = unpacked[2].reshape(group, -1, convolved // group).transpose(1, 0, 2).reshape(-1, convolved)
    taps_full = jnp.concatenate(
        [taps_full, unpacked[3].reshape(1, convolved), jnp.zeros((3, convolved), BF16)], axis=0
    ).astype(F32)
    dt_full, decay_full, skip_full = [unpacked[at].reshape(head_count).astype(F32) for at in (4, 5, 6)]
    mixer_gain = unpacked[7].reshape(1, inner).astype(F32)
    post_gain = unpacked[8].reshape(1, model).astype(F32)
    router_full = unpacked[9].reshape(model, experts)

    g_column = gather(cotangent, COLUMN)
    shared_in_own = lax.all_to_all(
        shared_in.reshape(part, 2, group, shared).transpose(2, 0, 1, 3).reshape(group * part, 2 * shared),
        COLUMN, split_axis=0, concat_axis=0, tiled=True,
    )

    blocks = numbers_all[:, :, 3].reshape(reps, depth, 2)
    dealt_plane = lax.dynamic_index_in_dim(blocks, z, axis=1, keepdims=False)
    lengths_plane = jnp.take_along_axis(numbers_all[:, :, :3], dealt_plane[:, :, None], axis=1).reshape(members, 3)
    ends = jnp.cumsum(lengths_plane, axis=1)
    position = jnp.arange(rows, dtype=jnp.int32)
    seg = jnp.sum((position[None, :, None] >= ends[:, None, :]).astype(jnp.int32), axis=2)

    taps_own = jnp.concatenate(
        [columns_of(taps_full, channels * team, channels), taps_full[:, inner:]], axis=1
    )
    own_heads = [lax.dynamic_slice_in_dim(v, heads * team, heads) for v in (dt_full, decay_full, skip_full)]
    head_rows = jnp.pad(jnp.stack([own_heads[0], jnp.exp(own_heads[1])]), ((0, 6), (0, LANES - heads)))
    skip_own = jnp.repeat(own_heads[2], width)[None, :]
    norm_own = columns_of(mixer_gain, channels * team, channels)
    mixer_args = (
        x_plane, in_gain, weight, seg.reshape(members * rows, 1), seg[:, None, :], taps_own, head_rows, skip_own,
        norm_own, out_own,
    )
    parts, squares, projected = mixer_forward(mixer_args, rows, channels, width, state)
    after, mixer_result, scale, second_column = join_mixer(
        parts.reshape(reps, 2, rows, model), squares.reshape(reps, 2, 8, rows), tokens, post_gain, inner, reps, depth
    )
    second_column = second_column.reshape(group * rows, model)

    second_blocks = second_column.reshape(group, rows, model)
    g_blocks = g_column.reshape(group, rows, model)
    dealt_column = lax.dynamic_index_in_dim(numbers_all[:, :, 3], rep, axis=0, keepdims=False)
    table_dealt = jnp.take(table_all, dealt_column, axis=0)
    logits = mm(second_column, router_full).reshape(group, rows, experts)
    used = table_dealt.transpose(0, 2, 1) > 0
    top_logit = jnp.max(jnp.where(used, logits, -jnp.inf), axis=2, keepdims=True)
    raw = jnp.where(used, jnp.exp(jnp.where(used, logits - top_logit, 0.0)), 0.0)
    gates = raw / jnp.sum(raw, axis=2, keepdims=True)
    slots = columns_of(table_dealt, local * shard, local).astype(jnp.int32) - 1
    onehot_mask = slots[:, :, None, :] == jnp.arange(capacity, dtype=jnp.int32)[None, None, :, None]
    onehot = onehot_mask.astype(BF16)
    gates_own = columns_of(gates, local * shard, local, axis=2).transpose(0, 2, 1)
    gate_slot = jnp.sum(jnp.where(onehot_mask, gates_own[:, :, None, :], 0.0), axis=3)
    gate_slot = gate_slot.transpose(1, 0, 2).reshape(local, group * capacity, 1)

    def to_slots(values):
        return jnp.einsum("qict,qtd->iqcd", onehot, values, preferred_element_type=F32).astype(BF16).reshape(
            local, group * capacity, model
        )

    def to_rows(values):
        return jnp.einsum(
            "qict,iqcd->qtd", onehot, values.reshape(local, group, capacity, model), preferred_element_type=F32
        ).reshape(group * rows, model)

    buffer = to_slots(second_blocks)
    slot_g = to_slots(g_blocks)
    expert_pre = jnp.einsum("ind,idf->inf", buffer, expert_in, preferred_element_type=F32)
    half = expert_pre.shape[2] // 2
    pre_a, pre_b = expert_pre[:, :, :half], expert_pre[:, :, half:]
    sig_a = jax.nn.sigmoid(pre_a)
    hidden = (pre_a * sig_a * pre_b).astype(BF16)
    result = jnp.einsum("inf,ifd->ind", hidden, expert_out, preferred_element_type=F32).astype(BF16)
    shared_pre = mm(second_column, shared_in_own)
    shared_a, shared_b = shared_pre[:, :shared], shared_pre[:, shared:]
    shared_sig = jax.nn.sigmoid(shared_a)
    shared_hidden = (shared_a * shared_sig * shared_b).astype(BF16)

    result_grad = (gate_slot * slot_g.astype(F32)).astype(BF16)
    hidden_grad = jnp.einsum("ind,ifd->inf", result_grad, expert_out, preferred_element_type=F32)
    pre_grad = jnp.concatenate(
        [hidden_grad * pre_b * silu_slope(pre_a, sig_a), hidden_grad * pre_a * sig_a], axis=2
    ).astype(BF16)
    buffer_grad = jnp.einsum("inf,idf->ind", pre_grad, expert_in, preferred_element_type=F32).astype(BF16)
    shared_back = mm_nt(g_column, shared_out)
    shared_grad = jnp.concatenate(
        [shared_back * shared_b * silu_slope(shared_a, shared_sig), shared_back * shared_a * shared_sig], axis=1
    ).astype(BF16)
    slot_dot = jnp.sum(slot_g.astype(F32) * result.astype(F32), axis=2).reshape(local, group, capacity)
    gate_grad = jnp.sum(jnp.where(onehot_mask, slot_dot.transpose(1, 0, 2)[:, :, :, None], 0.0), axis=2)
    gate_sum = jnp.sum(gates_own * gate_grad, axis=1)
    own_expert = (expert_ids[None, :] == (local * shard + jnp.arange(local, dtype=jnp.int32))[:, None]).astype(F32)
    gate_full = jnp.sum(gate_grad[:, :, :, None] * own_expert[None, :, None, :], axis=1)
    logit_grad = (gates * (gate_full - gate_sum[:, :, None])).reshape(group * rows, experts)
    logit_pair = jnp.concatenate(split_two(logit_grad), axis=1)
    second_part = (
        to_rows(buffer_grad)
        + mm_nt(logit_pair, jnp.concatenate([router_full, router_full], axis=1))
        + mm_nt(shared_grad, shared_in_own)
    )

    layer_part = to_rows((gate_slot * result.astype(F32)).astype(BF16)) + mm(shared_hidden, shared_out)
    layer_sum = scatter_sum(layer_part.astype(BF16), COLUMN).astype(F32)
    layer_out = (after + layer_sum).astype(BF16)

    grad_expert_out = jnp.einsum("inf,ind->ifd", hidden, result_grad, preferred_element_type=F32)
    grad_expert_in = jnp.einsum("ind,inf->idf", buffer, pre_grad, preferred_element_type=F32)
    grad_expert_out = lax.psum(grad_expert_out.astype(BF16), "rep").astype(F32)
    grad_expert_in = lax.psum(grad_expert_in.astype(BF16), "rep").astype(F32)
    grad_shared_out = lax.psum(mm_tn(shared_hidden, g_column).astype(BF16), "rep").astype(F32)
    shared_in_columns = mm_tn(second_column, shared_grad).astype(BF16)
    shared_in_rows = lax.all_to_all(shared_in_columns, COLUMN, split_axis=0, concat_axis=0, tiled=True)
    shared_in_rows = shared_in_rows.reshape(group, part, 2, shared).transpose(1, 2, 0, 3).reshape(part, -1)
    grad_shared_in = lax.psum(shared_in_rows, "rep").astype(F32)
    router_pair = mm_tn(second_column, logit_pair)
    router_grad = router_pair[:, :experts] + router_pair[:, experts:]

    after_grad, post_grad, low_plane, scales = join_experts(
        second_part.astype(BF16).reshape(depth, 2, rows, model), cotangent, after, mixer_result, scale, post_gain,
        inner, reps, depth,
    )
    back_parts, in_grad, out_grad, taps_grad, heads_grad, wide_grad = mixer_backward(
        mixer_args, projected, low_plane.reshape(members * rows, model), scales.reshape(members, 2, 8, rows),
        rows, channels, width, state,
    )
    grad_tokens, in_norm_grad = join_input(
        back_parts.reshape(reps, 2, rows, model), tokens, after_grad, in_gain, reps, depth
    )

    in_low = in_grad.astype(BF16)
    first_core = core == 0
    pair = 2 * channels

    def paired(values):
        empty = jnp.zeros_like(values)
        return [jnp.where(first_core, values, empty), jnp.where(first_core, empty, values)]

    in_pair = jnp.concatenate(
        paired(in_low[:, :channels]) + paired(in_low[:, channels:pair]) + [in_low[:, pair:]], axis=1
    )
    in_rows = gather(scatter_sum(in_pair, COLUMN), "rep").reshape(reps, part, -1).transpose(1, 0, 2)
    dt_rows = in_rows[:, :, 2 * pair + 2 * state :].reshape(part, reps, 2, LANES // 2)[:, :, :, :heads]
    grad_in_proj = jnp.concatenate(
        [
            in_rows[:, :, :pair].reshape(part, inner).astype(F32),
            in_rows[:, :, pair : 2 * pair].reshape(part, inner).astype(F32),
            jnp.sum(in_rows[:, :, 2 * pair : 2 * pair + 2 * state].astype(F32), axis=1),
            dt_rows.reshape(part, head_count).astype(F32),
        ],
        axis=1,
    )
    out_chunk = scatter_sum(out_grad.astype(BF16), "z")
    out_chunks = gather(out_chunk[None], "rep")
    out_rows = lax.all_to_all(out_chunks, "z", split_axis=0, concat_axis=0, tiled=True)
    grad_out_proj = out_rows.reshape(channels, model).astype(F32)

    def placed(values, size, start):
        blank_row = jnp.zeros(values.shape[:-1] + (size,), F32)
        return lax.dynamic_update_slice_in_dim(blank_row, values, start, axis=values.ndim - 1)

    taps_full_grad = jnp.concatenate(
        [placed(taps_grad[:5, :channels], inner, channels * team), taps_grad[:5, channels:]], axis=1
    )
    skip_head_grad = jnp.sum(wide_grad[1].reshape(heads, width), axis=1)
    small = [
        in_norm_grad.reshape(group, -1),
        taps_full_grad.reshape(5, group, -1).transpose(1, 0, 2).reshape(group, -1),
        placed(heads_grad[0, :heads], head_count, heads * team).reshape(group, -1),
        placed(heads_grad[1, :heads], head_count, heads * team).reshape(group, -1),
        placed(skip_head_grad, head_count, heads * team).reshape(group, -1),
        placed(wide_grad[0], inner, channels * team).reshape(group, -1),
        post_grad.reshape(group, -1),
        router_grad.reshape(group, -1),
    ]
    small_sizes = [piece.shape[1] for piece in small]
    small_sum = lax.psum(scatter_sum(jnp.concatenate(small, axis=1), COLUMN), "rep")[0]
    small_out, offset = [], 0
    for size in small_sizes:
        small_out.append(small_sum[offset : offset + size])
        offset += size
    taps_out = small_out[1].reshape(5, -1)
    return (
        layer_out,
        grad_tokens,
        small_out[0],
        grad_in_proj,
        taps_out[:4],
        taps_out[4],
        small_out[2],
        small_out[3],
        small_out[4],
        small_out[5],
        grad_out_proj,
        small_out[6],
        small_out[7].reshape(part, experts),
        grad_shared_in,
        grad_shared_out,
        grad_expert_in,
        grad_expert_out,
    )


def solution(mesh):
    reps, group = mesh.shape["rep"], mesh.shape["shard"]
    split = Mesh(mesh.devices.reshape(reps, group // 2, 2), ALL)
    one, row = P(COLUMN), P(COLUMN, None)
    token = P(ALL, None)
    return jax.shard_map(
        shards,
        mesh=split,
        in_specs=(
            token, token, P(ALL), token, token, token, one, row, P(None, COLUMN), one, one, one, one, one, row,
            one, row, row, row, P(COLUMN, None, None), P(COLUMN, None, None),
        ),
        out_specs=(
            token, token, one, row, P(None, COLUMN), one, one, one, one, one, row, one, row, row, row,
            P(COLUMN, None, None), P(COLUMN, None, None),
        ),
        check_vma=False,
    )
```

time: 2740 us -> 1210 us (0.44)
  waiting for transfers between devices: 1470 us -> 370 us
  Pallas kernels: 0 us -> 492 us
  local copies, waits for them, and re-layouts: 500 us -> 84.9 us
  blocking collectives: 305 us -> 16.6 us
  matrix products: 263 us -> 137 us
  other arithmetic: 142 us -> 69 us
    all_to_all x4 -> x3, waiting for transfers between devices: 516 us -> 0.01 us  [the longest x1 0.01 us: shards(): lax.all_to_all(out_chunks, 'z', split_axis=0, concat_axis=0, tiled=True)]
    pallas_call x0 -> x6, Pallas kernels: none -> 492 us  [the longest x1 145 us: start_gather(): pl.pallas_call(kernel, in_specs=anywhere(7), out_specs=anywhere(6), out_s...]
    reduce_scatter x4 -> x3, waiting for transfers between devices: 357 us -> 63.1 us  [scatter_sum(): return lax.psum_scatter(values, axes, scatter_dimension=axis, tiled=True)]
    psum x1, waiting for transfers between devices: 483 us -> 190 us  [shards(): grad_shared_in = lax.psum(shared_in_rows, 'rep').astype(F32)]
    dynamic_update_slice x38 -> x5, local copies, waits for them, and re-layouts: 236 us -> 2.09 us  [placed(): lax.dynamic_update_slice_in_dim(blank_row, values, start, axis=values.ndi...]
    all_gather x3 -> x0, blocking collectives: 227 us -> none  [the longest x1 188 us: shards(): lax.all_gather(router, 'shard', axis=0, tiled=True)]
    dot_general x43 -> x19, matrix products: 256 us -> 137 us  [the longest x3 22 us: mm_nt(): lax.dot_general(left, right, (((1,), (1,)), ((), ())), preferred_element_...]
    unnamed x2 -> x0, blocking collectives: 59.3 us -> none
  transfers between devices with their start and end apart: 18 -> 11, of which waited for: 8 -> 6; matrix products, arithmetic and copies ran while one was open for 32% -> 13% of each run, Pallas kernels for 0% -> 27%
where the time goes in v1:
time: 1210 us; the launch traced here: 1200 us
  Pallas kernels  492 us (41%)
  waiting for transfers between devices  370 us (31%)
  matrix products  137 us (11%)
  local copies, waits for them, and re-layouts  84.9 us (7%)
  other arithmetic  69 us (6%)
  blocking collectives  16.6 us (1%)
  between operations  16.2 us (1%)
  starting transfers between devices  15 us (1%)
    psum x1, waiting for transfers between devices, shards(): grad_shared_in = lax.psum(shared_in_rows, 'rep').astype(F32)  190 us
    pallas_call x1, Pallas kernels, start_gather(): pl.pallas_call(kernel, in_specs=anywhere(7), out_specs=anywhere(6), out_s...  145 us
    pallas_call x1, Pallas kernels, join_experts(): pl.pallas_call(kernel, in_specs=in_vmem(6), out_specs=in_vmem(2) + anywhe...  108 us
    pallas_call x1, Pallas kernels, join_mixer(): pl.pallas_call(kernel, in_specs=in_vmem(4), out_specs=in_vmem(3) + anywhe...  104 us
    unnamed x9, waiting for transfers between devices  65.9 us
    reduce_scatter x3, waiting for transfers between devices, scatter_sum(): return lax.psum_scatter(values, axes, scatter_dimension=axis, tiled=True)  63.1 us
    pallas_call x1, Pallas kernels, mixer_backward(): pl.pallas_call(functools.partial(mixer_backward_kernel, channels, width,...  56.5 us
    all_gather x3, waiting for transfers between devices, gather(): return lax.all_gather(values, axes, axis=axis, tiled=True)  51.1 us
  transfers between devices with their start and end apart: 11, of which 6 were waited for; matrix products, arithmetic and copies ran while one was open for 13% of the time, Pallas kernels for 27%

profile of v1, /device:TPU:0, one launch (start us, length us, event | category | flops | bytes accessed | tf_op | source)
XLA Modules:
  0.0 1200.9 jit_solution(7016336980898354384)
XLA Ops:
  11.1 3.1 all_to_all.17
  14.2 6.3 all-to-all-start
  28.5 145.3 %start_gather.1 = (bf16[4,2,256,1536]{3,2,1,0:T(8,128)(2,1)S(1)}, bf16[4,2,192,1152]{3,2,1,0:T(8,128)(2,1)S(1)}, bf16[4,2,16,640]{3,2,1,0:T(8,128)(2,1)S(1)}, s3...) custom-call(bf16[256,1536]{1,0:T(8,128)(2,1)S(1)} %copy-done.4, ...), custom_call_target="tpu_custom_call" | custom-call | tf_op jit(solution)/shard_map/start_gather/pallas_call | solution.py:660
  200.3 30.0 %mixer_forward.1 = (bf16[2048,1536]{1,0:T(8,128)(2,1)}, f32[8,8,256]{2,1,0:T(8,128)}, f32[2048,1152]{1,0:T(8,128)}) custom-call(bf16[2048,1536]{1,0:T(8,128)(2,1)} %bitcast.185, f32[1,1536]{1,0:T(1,128)} %reshape.445.gain_ref, bf16[1536,1152]{1,0:T(8,128)(2,1)} %bitcast.187, s32[2048,1]{1,0:T(8,128)} %bitcast.206, ...), custom_call_target="tpu_custom_call" | custom-call | tf_op jit(solution)/shard_map/mixer_forward/pallas_call | solution.py:262
  230.2 104.0 %join_mixer.1 = (f32[256,1536]{1,0:T(8,128)}, f32[256,1536]{1,0:T(8,128)}, f32[8,256]{1,0:T(8,128)}, bf16[4,2,256,1536]{3,2,1,0:T(8,128)(2,1)}) custom-call(bf16[4,2,256,1536]{3,2,1,0:T(8,128)(2,1)} %bitcast.211, f32[4,2,8,256]{3,2,1,0:T(8,128)} %bitcast.241, bf16[256,1536]{1,0:T(8,128)(2,1)} %x_ref.5, f32[1,1536]{1,0:T(1,128)} %reshape.450.gain_ref), custom_call_target="tpu_custom_call" | custom-call | tf_op jit(solution)/shard_map/join_mixer/pallas_call | solution.py:716
  334.3 5.8 convert_bitcast_fusion.1
  340.2 3.8 copy.175
  348.3 10.9 fusion.46
  362.2 6.2 multiply_convert_fusion.2
  368.4 6.1 fusion.47
  374.5 9.0 convert_bitcast_fusion
  383.5 10.8 copy.181
  394.3 7.7 fusion.2
  404.3 11.6 fusion.6
  415.9 8.5 multiply_convert_fusion.1
  424.5 13.6 %convolution_convert_fusion.2 = bf16[2,1024,1536]{2,1,0:T(8,128)(2,1)} fusion(bf16[2,1536,1024]{2,1,0:T(8,128)(2,1)} %param.40, bf16[2,1024,512]{1,2,0:T(8,128)(2,1)S(1)} %get-tuple-element.144, bf16[2,1024,512]{1,2,0:T(8,128)(2,1)S(1)} %get-tuple-element.143), kind=kOutput, calls=%fused_computation.22 | convolution fusion | flops 6453985280 | bytes 16777216 | tf_op jit(solution)/shard_map/inf,idf->ind/dot_general | solution.py:1001
  438.1 7.8 fusion.7
  445.9 6.6 fusion.23
  452.5 3.1 multiply_convert_fusion.4
  455.7 12.3 %fusion.4 = bf16[2048,1536]{1,0:T(8,128)(2,1)} fusion(f32[2048,1536]{1,0:T(8,128)} %fusion.23, f32[8,256,1536,1]{2,1,3,0:T(8,128)} %fusion.7, bf16[1536,256]{1,0:T(8,128)(2,1)} %bitcast.34, bf16[2048,128]{0,1:T(8,128)(2,1)S(1)} %get-tuple-element.148, bf16[2048,128]{0,1:T(8,128)(2,1)S(1)} %get-tuple-element.147), kind=kOutput, calls=%fused_computation.9 | convolution fusion | flops 1622147072 | bytes 33292288 | tf_op jit(solution)/shard_map/dot_general | solution.py:30
  467.9 108.3 %join_experts.1 = (f32[256,1536]{1,0:T(8,128)}, f32[1,1536]{1,0:T(1,128)}, bf16[4,2,256,1536]{3,2,1,0:T(8,128)(2,1)}, f32[4,2,2,8,256]{4,3,2,1,0:T(8,128)}) custom-call(bf16[4,2,256,1536]{3,2,1,0:T(8,128)(2,1)} %bitcast.202, bf16[256,1536]{1,0:T(8,128)(2,1)} %g_ref.1, f32[256,1536]{1,0:T(8,128)} %get-tuple-element.48.after_ref, ...), custom_call_target="tpu_custom_call" | custom-call | tf_op jit(solution)/shard_map/join_experts/pallas_call | solution.py:772
  576.3 56.5 %mixer_backward.1 = (bf16[2048,1536]{1,0:T(8,128)(2,1)}, f32[1536,1152]{1,0:T(8,128)}, f32[384,1536]{1,0:T(8,128)}, f32[8,640]{1,0:T(8,128)}, f32[8,128]{1,0:T(8,128)}, /*index=5*/f32[8,384]{1,0:T(8,128)}) custom-call(bf16[2048,1536]{1,0:T(8,128)(2,1)} %bitcast.186, f32[1,1536]{1,0:T(1,128)} %reshape.445.gain_ref, bf16[1536,1152]{1,0:T(8,128)(2,1)} %bitcast.188, ...), custom_call_target="tpu_custom_call" | custom-call | tf_op jit(solution)/shard_map/mixer_backward/pallas_call | solution.py:284
  632.8 2.8 convert_element_type.238
  635.7 3.4 convert_element_type.230
  645.2 5.5 convolution_convert_fusion.4
  650.7 3.7 all-to-all-start.2
  654.5 3.9 fusion.27
  660.9 5.8 reduce-scatter.8.cloned.1.call-done
  666.8 12.9 %convolution_convert_fusion.1 = bf16[2,1536,1024]{2,1,0:T(8,128)(2,1)} fusion(bf16[2,1024,1536]{2,1,0:T(8,128)(2,1)} %bitcast.208, bf16[2,1024,512]{1,2,0:T(8,128)(2,1)} %copy-done.40, bf16[2,1024,512]{1,2,0:T(8,128)(2,1)} %copy-done.39), kind=kOutput, calls=%fused_computation.21 | convolution fusion | flops 6453985280 | bytes 16777216 | tf_op jit(solution)/shard_map/ind,inf->idf/dot_general | solution.py:1024
  681.3 47.5 %join_input.1 = (bf16[256,1536]{1,0:T(8,128)(2,1)}, f32[1,1536]{1,0:T(1,128)}) custom-call(bf16[4,2,256,1536]{3,2,1,0:T(8,128)(2,1)} %bitcast.210, bf16[256,1536]{1,0:T(8,128)(2,1)} %x_ref.5, f32[256,1536]{1,0:T(8,128)} %get-tuple-element.56.grad_ref, f32[1,1536]{1,0:T(1,128)} %reshape.445.gain_ref), custom_call_target="tpu_custom_call" | custom-call | tf_op jit(solution)/shard_map/join_input/pallas_call | solution.py:810
  730.8 7.7 convolution_convert_fusion.3
  738.5 4.5 convolution_convert_fusion.5
  745.3 5.2 fusion.9
  750.5 4.5 fusion.5
  755.7 10.7 all-gather.9.cloned.1.call-done
  766.5 4.6 all-to-all-start.1
  771.7 64.5 %all-reduce.8.cloned.1.call-done = f32[8,5938]{1,0:T(8,128)} async-done(((f32[8,5938]{1,0:T(8,128)}), f32[8,5938]{1,0:T(8,128)}) %all-reduce.8.cloned.1.call-update) | async-done | bytes 190032
  837.8 16.6 %psum.35 = f32[1,5938]{1,0:T(1,128)S(1)} all-reduce(f32[1,5938]{1,0:T(1,128)S(1)} %constant_dynamic-slice_fusion.10), channel_id=1, replica_groups=mesh['rep'=4,'z'=4,'core'=2] {'rep'}, use_global_device_ids=true, to_apply=%region_13.14 | all-reduce | flops 5938 | bytes 47504 | tf_op jit(solution)/shard_map/psum | solution.py:1093
  860.4 190.1 %all-reduce.10.cloned.1.call-done = (bf16[192,2048]{1,0:T(8,128)(2,1)}, bf16[128,1536]{1,0:T(8,128)(2,1)}, bf16[2,1536,1024]{2,1,0:T(8,128)(2,1)}, bf16[2,512,1536]{2,1,0:T(8,128)(2,1)}) async-done(((bf16[192,2048]{1,0:T(8,128)(2,1)}, bf16[128,1536]{1,0:T(8,128)(2,1)}, bf16[2,1536,1024]{2,1,0:T(8,128)(2,1)}, bf16[2,512,1536]{2,1,0:T(8,128)(2,1)}), (bf16[192,2048]{1,0:T(8,128)(2,1)}, ...) | async-done | bytes 10616848 | tf_op jit(solution)/shard_map/psum | solution.py:1031
  1055.3 3.6 convert_element_type.248
  1058.9 6.3 convert_element_type.246
  1065.3 57.3 %reduce-scatter.4.cloned.1.call-done = bf16[256,1536]{1,0:T(8,128)(2,1)} async-done(((bf16[2048,1536]{1,0:T(8,128)(2,1)}), bf16[256,1536]{1,0:T(8,128)(2,1)}) %reduce-scatter.4.cloned.1.call-update) | async-done | bytes 786448 | tf_op jit(solution)/shard_map/reduce_scatter | solution.py:826
  1124.8 40.4 %all-gather.7.cloned.1.call-done = bf16[768,1920]{1,0:T(8,128)(2,1)} async-done(((bf16[192,1920]{1,0:T(8,128)(2,1)}), bf16[768,1920]{1,0:T(8,128)(2,1)}) %all-gather.7.cloned.1.call-update) | async-done | bytes 2949136 | tf_op jit(solution)/shard_map/all_gather | solution.py:822
  1165.2 5.7 copy.190
  1172.9 3.7 fusion.43
  1180.8 3.3 bitcast_convert_fusion
  1184.1 3.6 copy.192
  1187.6 5.1 pad_maximum_fusion
  (267 shorter events, 84.4 us)
Async XLA Ops:
  7.2 387.1 %copy-start = (bf16[2,512,1536]{2,1,0:T(8,128)(2,1)S(1)}, bf16[2,512,1536]{2,1,0:T(8,128)(2,1)}, u32[]{:S(2)}) copy-start(bf16[2,512,1536]{2,1,0:T(8,128)(2,1)} %param.41) | copy-start | bytes 9437188
  7.2 14.1 %copy-start.36 = (s32[1,3]{1,0:T(1,128)S(1)}, s32[1,3]{1,0:T(1,128)}, u32[]{:S(2)}) copy-start(s32[1,3]{1,0:T(1,128)} %param.24) | copy-start | bytes 40
  7.2 14.1 %copy-start.27 = (bf16[4,416]{1,0:T(4,128)(2,1)S(1)}, bf16[4,416]{1,0:T(4,128)(2,1)}, u32[]{:S(2)}) copy-start(bf16[4,416]{1,0:T(4,128)(2,1)} %param.29) | copy-start | bytes 9988
  7.2 14.2 %copy-start.24 = (s32[256,6]{0,1:T(8,128)S(1)}, s32[256,6]{0,1:T(8,128)}, u32[]{:S(2)}) copy-start(s32[256,6]{0,1:T(8,128)} %param.26) | copy-start | bytes 18436
  7.2 14.2 %copy-start.25 = (s32[256,6]{0,1:T(8,128)S(1)}, s32[256,6]{0,1:T(8,128)}, u32[]{:S(2)}) copy-start(s32[256,6]{0,1:T(8,128)} %param.25) | copy-start | bytes 18436
  7.3 14.3 %copy-start.23 = (bf16[192,16]{0,1:T(8,128)(2,1)S(1)}, bf16[192,16]{0,1:T(8,128)(2,1)}, u32[]{:S(2)}) copy-start(bf16[192,16]{0,1:T(8,128)(2,1)} %param.37) | copy-start | bytes 18436
  7.3 14.5 %copy-start.35 = (bf16[192]{0:T(256)(128)(2,1)S(1)}, bf16[192]{0:T(256)(128)(2,1)}, u32[]{:S(2)}) copy-start(bf16[192]{0:T(256)(128)(2,1)} %param.36) | copy-start | bytes 1156
  7.3 14.5 %copy-start.30 = (bf16[384]{0:T(512)(128)(2,1)S(1)}, bf16[384]{0:T(512)(128)(2,1)}, u32[]{:S(2)}) copy-start(bf16[384]{0:T(512)(128)(2,1)} %param.34) | copy-start | bytes 2308
  7.3 14.5 %copy-start.34 = (bf16[6]{0:T(256)(128)(2,1)S(1)}, bf16[6]{0:T(256)(128)(2,1)}, u32[]{:S(2)}) copy-start(bf16[6]{0:T(256)(128)(2,1)} %param.33) | copy-start | bytes 40
  7.3 14.5 %copy-start.33 = (bf16[6]{0:T(256)(128)(2,1)S(1)}, bf16[6]{0:T(256)(128)(2,1)}, u32[]{:S(2)}) copy-start(bf16[6]{0:T(256)(128)(2,1)} %param.32) | copy-start | bytes 40
  7.3 14.5 %copy-start.32 = (bf16[6]{0:T(256)(128)(2,1)S(1)}, bf16[6]{0:T(256)(128)(2,1)}, u32[]{:S(2)}) copy-start(bf16[6]{0:T(256)(128)(2,1)} %param.31) | copy-start | bytes 40
  7.3 14.5 %copy-start.29 = (bf16[416]{0:T(512)(128)(2,1)S(1)}, bf16[416]{0:T(512)(128)(2,1)}, u32[]{:S(2)}) copy-start(bf16[416]{0:T(512)(128)(2,1)} %param.30) | copy-start | bytes 2500
  7.3 14.5 %copy-start.31 = (bf16[192]{0:T(256)(128)(2,1)S(1)}, bf16[192]{0:T(256)(128)(2,1)}, u32[]{:S(2)}) copy-start(bf16[192]{0:T(256)(128)(2,1)} %param.27) | copy-start | bytes 1156
  7.3 16.3 %slice-start.4 = ((bf16[192,6448]{1,0:T(8,128)(2,1)}), bf16[192,256]{1,0:T(8,128)(2,1)S(1)}, s32[]{:S(2)}) async-start(bf16[192,6448]{1,0:T(8,128)(2,1)} %param.28), calls=%async_computation.18 | async-start | bytes 196608 | tf_op jit(solution)/shard_map/slice | solution.py:894
  7.3 367.1 %all-gather.5.cloned.1.call-start = ((), (), s32[]{:S(2)}) async-start(), calls=%async_computation.7 | async-start | bytes 7077888 | tf_op jit(solution)/shard_map/all_gather | solution.py:822
  14.2 354.2 %all-to-all-start = ((bf16[8,192,256]{2,1,0:T(8,128)(2,1)}), bf16[8,192,256]{2,1,0:T(8,128)(2,1)}, u32[]{:S(2)}, u32[]{:S(2)}) async-start(bf16[8,192,256]{2,1,0:T(8,128)(2,1)} %all_to_all.17), calls=%async_computation | async-start | bytes 1572864 | tf_op jit(solution)/shard_map/all_to_all | solution.py:928
  20.6 646.1 %reduce-scatter.8.cloned.1.call-start = ((), (), s32[]{:S(2)}) async-start(), calls=%async_computation.10 | async-start | bytes 1474560 | tf_op jit(solution)/shard_map/reduce_scatter | solution.py:826
  230.2 104.0 %copy-start.18 = (bf16[8,16,256]{2,1,0:T(8,128)(2,1)S(1)}, bf16[8,16,256]{2,1,0:T(8,128)(2,1)}, u32[]{:S(2)}) copy-start(bf16[8,16,256]{2,1,0:T(8,128)(2,1)} %gather_fusion) | copy-start | bytes 196612
  340.2 5.1 copy-start.7
  394.3 9.9 copy-start.15
  394.3 10.0 copy-start.21
  415.9 36.6 %slice-start = ((s8[6291456]{0:T(1024)(128)(4,1)}), s8[2097152]{0:T(1024)(128)(4,1)S(1)}, s32[]{:S(2)}) async-start(s8[6291456]{0:T(1024)(128)(4,1)} %bitcast.199), calls=%async_computation.14 | async-start | bytes 4194304
  424.4 13.6 %copy-start.39 = (bf16[2,1024,512]{1,2,0:T(8,128)(2,1)}, bf16[2,1024,512]{1,2,0:T(8,128)(2,1)S(1)}, u32[]{:S(2)}) copy-start(bf16[2,1024,512]{1,2,0:T(8,128)(2,1)S(1)} %get-tuple-element.143) | copy-start | bytes 6291460
  424.4 13.6 %copy-start.40 = (bf16[2,1024,512]{1,2,0:T(8,128)(2,1)}, bf16[2,1024,512]{1,2,0:T(8,128)(2,1)S(1)}, u32[]{:S(2)}) copy-start(bf16[2,1024,512]{1,2,0:T(8,128)(2,1)S(1)} %get-tuple-element.144) | copy-start | bytes 6291460
  424.5 28.1 %slice-start.1 = ((s8[6291456]{0:T(1024)(128)(4,1)}), s8[4194304]{0:T(1024)(128)(4,1)S(1)}, s32[]{:S(2)}) async-start(s8[6291456]{0:T(1024)(128)(4,1)} %bitcast.199), calls=%async_computation.15 | async-start | bytes 8388608
  438.1 7.8 copy-start.19
  445.9 6.6 copy-start.16
  445.9 6.6 copy-start.38
  635.7 119.4 %reduce-scatter.6.cloned.1.call-start = ((), (), s32[]{:S(2)}) async-start(), calls=%async_computation.8 | async-start | bytes 6635520 | tf_op jit(solution)/shard_map/reduce_scatter | solution.py:826
  650.7 92.3 %all-to-all-start.2 = ((bf16[8,192,256]{2,1,0:T(8,128)(2,1)}), bf16[8,192,256]{2,1,0:T(8,128)(2,1)S(1)}, u32[]{:S(2)}, u32[]{:S(2)}) async-start(bf16[8,192,256]{2,1,0:T(8,128)(2,1)} %bitcast.66), calls=%async_computation.5 | async-start | bytes 1572864 | tf_op jit(solution)/shard_map/all_to_all | solution.py:1029
  654.5 6.4 copy-start.22
  654.5 112.0 %all-gather.9.cloned.1.call-start = ((), (), s32[]{:S(2)}) async-start(), calls=%async_computation.11 | async-start | bytes 1474560 | tf_op jit(solution)/shard_map/all_gather | solution.py:822
  666.7 169.4 %all-reduce.8.cloned.1.call-start = ((), (), s32[]{:S(2)}) async-start(), calls=%async_computation.12 | async-start | bytes 385024
  681.3 48.3 %copy-start.26 = (f32[1,1536]{1,0:T(1,128)S(1)}, f32[1,1536]{1,0:T(1,128)}, u32[]{:S(2)}) copy-start(f32[1,1536]{1,0:T(1,128)} %get-tuple-element.62) | copy-start | bytes 18436
  681.3 49.5 %copy-start.8 = (bf16[2,1024,512]{1,2,0:T(8,128)(2,1)S(1)}, bf16[2,1024,512]{1,2,0:T(8,128)(2,1)}, u32[]{:S(2)}) copy-start(bf16[2,1024,512]{1,2,0:T(8,128)(2,1)} %multiply_convert_fusion.2) | copy-start | bytes 6291460
  730.7 319.7 %all-reduce.10.cloned.1.call-start = ((), (), s32[]{:S(2)}) async-start(), calls=%async_computation.13 | async-start | bytes 21233664 | tf_op jit(solution)/shard_map/psum | solution.py:1031
  730.8 7.7 copy-start.12
  745.2 377.4 %reduce-scatter.4.cloned.1.call-start = ((), (), s32[]{:S(2)}) async-start(), calls=%async_computation.6 | async-start | bytes 7077888 | tf_op jit(solution)/shard_map/reduce_scatter | solution.py:826
  745.3 5.2 copy-start.13
  745.3 5.2 copy-start.17
  755.0 16.1 %copy-start.37 = (u32[32]{0:T(128)S(1)}, u32[32]{0:T(128)}, u32[]{:S(2)}) copy-start(u32[32]{0:T(128)} %constant.128) | copy-start | bytes 388
  755.0 410.2 %all-gather.7.cloned.1.call-start = ((), (), s32[]{:S(2)}) async-start(), calls=%async_computation.9 | async-start | bytes 3686400 | tf_op jit(solution)/shard_map/all_gather | solution.py:822
  766.5 92.1 %all-to-all-start.1 = ((bf16[4,96,1536]{2,1,0:T(8,128)(2,1)}), bf16[4,96,1536]{2,1,0:T(8,128)(2,1)S(1)}, u32[]{:S(2)}, u32[]{:S(2)}) async-start(bf16[4,96,1536]{2,1,0:T(8,128)(2,1)} %bitcast.221), calls=%async_computation.4 | async-start | bytes 2359296 | tf_op jit(solution)/shard_map/all_to_all | solution.py:1071
  1050.4 4.9 copy-start.11
  1050.5 8.5 slice-start.2
  1058.9 63.7 %copy-start.10 = (f32[256,1536]{1,0:T(8,128)S(1)}, f32[256,1536]{1,0:T(8,128)}, u32[]{:S(2)}) copy-start(f32[256,1536]{1,0:T(8,128)} %get-tuple-element.48.after_ref) | copy-start | bytes 4718596
  1184.1 9.5 copy-start.1
  1187.6 5.1 copy-start.14
  (9 other events, 19.8 us)
Sparse Core Ops, SparseCore 0:
  9.8 100.6 all-gather.4
  635.8 30.8 reduce-scatter.7
  669.6 68.8 reduce-scatter.5
  740.4 26.0 all-gather.8
  769.3 66.7 all-reduce.7
  841.7 208.7 all-reduce.9
  1052.7 69.7 reduce-scatter.3
  1124.4 40.6 all-gather.6

commit v2 on v1

--- a/solution.py
+++ b/solution.py
@@ -64,8 +64,8 @@
         self.conv_sig = jax.nn.sigmoid(conv)
         act = conv * self.conv_sig
         self.xin = act[:, :channels]
-        self.write = act[:, channels : channels + state].astype(BF16)
-        self.read = act[:, channels + state :].astype(BF16)
+        self.write = act[:, channels : channels + state]
+        self.read = act[:, channels + state :]
         shifted = dt_raw + heads[0:1, :]
         self.step = jnp.maximum(shifted, 0.0) + jnp.log1p(jnp.exp(-jnp.abs(shifted)))
         self.step_sig = jax.nn.sigmoid(shifted)
@@ -77,7 +77,10 @@
         self.keep = self.causal & (seg_col == seg_row)
         self.cum = jnp.dot(self.causal.astype(F32), self.rate, precision=HIGH, preferred_element_type=F32)
         self.cum_t = self.cum.T
-        self.scores = jnp.where(self.keep, mm_nt(self.read, self.write), 0.0)
+        scores = lax.dot_general(
+            self.read, self.write, (((1,), (1,)), ((), ())), precision=HIGH, preferred_element_type=F32
+        )
+        self.scores = jnp.where(self.keep, scores, 0.0)
 
     def groups(self):
         for start in range(0, self.channels, LANES):
@@ -162,7 +165,8 @@
     for start, stop, heads in block.groups():
         xin = block.xin[:, start:stop]
         spread = block.spread(block.step, start, stop, heads)
-        scaled = (xin * spread).astype(BF16)
+        scaled, scaled_rest = split_two(xin * spread)
+        scaled_wide = jnp.concatenate([scaled, scaled, scaled_rest], axis=1)
         weights, decays = [], []
         y = None
         for head in heads:
@@ -183,13 +187,17 @@
         gate_grads.append(mixed_grad * y * silu_slope(gate, gate_sig))
         y_grad = mixed_grad * gate_act
         skip_grads.append(jnp.sum(y_grad * xin, axis=0, keepdims=True))
-        y_low = y_grad.astype(BF16)
+        y_low, y_rest = split_two(y_grad)
         scaled_grad = None
         for at, head in enumerate(heads):
             inside = block.inside(start, stop, head)
             term = mm_tn(weights[at].astype(BF16), y_low)
             scaled_grad = term if scaled_grad is None else jnp.where(inside, term, scaled_grad)
-            pair_grad = mm_nt(jnp.where(inside, y_low, jnp.zeros_like(y_low)), scaled)
+            blank = jnp.zeros_like(y_low)
+            y_own = jnp.where(inside, y_low, blank)
+            pair_grad = mm_nt(
+                jnp.concatenate([y_own, jnp.where(inside, y_rest, blank), y_own], axis=1), scaled_wide
+            )
             score_grad = score_grad + pair_grad * decays[at]
             exponent_grad = pair_grad * weights[at]
             cum_grad = jnp.where(lane_all == head, jnp.sum(exponent_grad, axis=1, keepdims=True), cum_grad)
@@ -200,8 +208,8 @@
             step_grad = jnp.where(lane_all == head, per_row, step_grad)
         x_grads.append(scaled_grad * spread + skip * y_grad)
     score_grad = jnp.where(block.keep, score_grad, 0.0).astype(BF16)
-    read_grad = mm(score_grad, block.write)
-    write_grad = mm_tn(score_grad, block.read)
+    read_grad = mm(score_grad, block.write.astype(BF16))
+    write_grad = mm_tn(score_grad, block.read.astype(BF16))
     cum_grad = cum_grad - cum_grad_t.T
     rate_grad = lax.dot_general(
         block.causal.astype(F32), cum_grad, (((0,), (0,)), ((), ())), precision=HIGH, preferred_element_type=F32
@@ -478,59 +486,61 @@
     return total
 
 
+class PairSwap:
+    @staticmethod
+    def scratch(count, shape, dtype):
+        return [pltpu.VMEM((count,) + shape, dtype), pltpu.SemaphoreType.DMA((2, count))]
+
+    def __init__(self, place, parts, pair, sems, order):
+        self.place, self.parts, self.pair, self.sems = place, parts, pair, sems
+        for at in order:
+            place.send(parts.at[at, 1 - place.core], pair.at[at], sems.at[0, at], sems.at[1, at], place.sibling())
+
+    def wait(self, at):
+        self.place.arrived(self.pair.at[at], self.sems.at[1, at])
+
+    def terms(self, at):
+        return [self.parts[at, self.place.core], self.pair[at]]
+
+
 class PlaneSum:
     @staticmethod
     def scratch(reps, shape, dtype):
-        return [
-            pltpu.VMEM((reps,) + shape, dtype), pltpu.VMEM((reps,) + shape, dtype), pltpu.VMEM((reps,) + shape, dtype),
-            pltpu.SemaphoreType.DMA((4, reps)),
+        return PairSwap.scratch(reps, shape, dtype) + [
+            pltpu.VMEM((reps,) + shape, dtype), pltpu.SemaphoreType.DMA((2, reps)),
         ]
 
-    def __init__(self, place, parts, pair, out, into, sems):
-        self.place, self.parts, self.pair, self.out, self.into, self.sems = place, parts, pair, out, into, sems
-        p = place
-        for distance in list(range(1, p.reps)) + [0]:
-            rep = p.rep_at(distance) if distance else p.rep
-            p.send(parts.at[rep, 1 - p.core], pair.at[distance], sems.at[0, distance], sems.at[1, distance], p.sibling())
+    def __init__(self, place, parts, pair, pair_sems, into, sems):
+        self.place, self.pair, self.into, self.sems = place, pair, into, sems
+        order = [place.rep_at(distance) for distance in range(1, place.reps)] + [place.rep]
+        self.swap = PairSwap(place, parts, pair, pair_sems, order)
 
     def relay(self):
         p = self.place
         for distance in range(1, p.reps):
             rep = p.rep_at(distance)
-            p.arrived(self.pair.at[distance], self.sems.at[1, distance])
-            self.out[distance] = add_up(self.parts[rep, p.core], self.pair[distance]).astype(self.out.dtype)
-            p.send(self.out.at[distance], self.into.at[distance], self.sems.at[2, distance], self.sems.at[3, distance],
+            self.swap.wait(rep)
+            self.pair[rep] = add_up(*self.swap.terms(rep)).astype(self.pair.dtype)
+            p.send(self.pair.at[rep], self.into.at[distance], self.sems.at[0, distance], self.sems.at[1, distance],
                    p.device(rep=rep))
 
     def total(self):
         p = self.place
-        p.arrived(self.pair.at[0], self.sems.at[1, 0])
-        terms = [self.parts[p.rep, p.core], self.pair[0]]
+        self.swap.wait(p.rep)
+        terms = self.swap.terms(p.rep)
         for distance in range(1, p.reps):
-            p.arrived(self.into.at[distance], self.sems.at[3, distance])
+            p.arrived(self.into.at[distance], self.sems.at[1, distance])
             terms.append(self.into[distance])
         return add_up(*terms)
 
 
-class ColumnSum:
+class LineSum:
     @staticmethod
     def scratch(depth, shape, dtype):
-        return [
-            pltpu.VMEM((depth,) + shape, dtype), pltpu.VMEM((2, depth) + shape, dtype),
-            pltpu.VMEM((2, depth) + shape, dtype), pltpu.SemaphoreType.DMA((2, depth)),
-            pltpu.SemaphoreType.DMA((4, depth)),
-        ]
-
-    def __init__(self, place, parts, pair, out, into, pair_sems, sems):
-        self.place, self.parts, self.pair, self.out, self.into = place, parts, pair, out, into
-        self.pair_sems, self.sems = pair_sems, sems
-        p = place
-        for distance in list(range(p.depth - 1, 0, -1)) + [0]:
-            at = lax.rem(p.z + distance, p.depth)
-            p.send(parts.at[at, 1 - p.core], pair.at[at], pair_sems.at[0, at], pair_sems.at[1, at], p.sibling())
-        for distance in list(range(p.depth - 1, 0, -1)) + [0]:
-            at = lax.rem(p.z + distance, p.depth)
-            p.arrived(pair.at[at], pair_sems.at[1, at])
+        return [pltpu.VMEM((depth + 1,) + shape, dtype), pltpu.SemaphoreType.DMA((4, depth))]
+
+    def __init__(self, place, terms, out, into, sems):
+        self.place, self.terms, self.out, self.into, self.sems = place, terms, out, into, sems
 
     def step(self, at):
         p = self.place
@@ -540,31 +550,56 @@
             (1, p.z - 1, at - (last - p.z), p.z == last, (at >= last - p.z) & (at - (last - p.z) < p.z)),
         ):
             goal = jnp.clip(goal, 0, last)
-            p.arrived(self.into.at[way, goal], self.sems.at[2 * way + 1, goal], valid & jnp.logical_not(first))
-
-            def start(goal=goal, way=way):
-                self.out[way, goal] = add_up(self.parts[goal, p.core], self.pair[goal]).astype(self.out.dtype)
-
-            def follow(goal=goal, way=way):
-                self.out[way, goal] = add_up(
-                    self.parts[goal, p.core], self.pair[goal], self.into[way, goal]
-                ).astype(self.out.dtype)
+            inner = valid & jnp.logical_not(first)
+            p.arrived(self.into.at[goal], self.sems.at[2 * way + 1, goal], inner)
+
+            def start(goal=goal):
+                self.out[goal] = add_up(*self.terms(goal)).astype(self.out.dtype)
+
+            def follow(goal=goal):
+                self.out[goal] = add_up(*self.terms(goal), self.into[goal]).astype(self.out.dtype)
 
             when(valid & first, start)
-            when(valid & jnp.logical_not(first), follow)
-            p.send(self.out.at[way, goal], self.into.at[way, goal], self.sems.at[2 * way, goal],
-                   self.sems.at[2 * way + 1, goal], p.device(z=towards), valid)
+            when(inner, follow)
+            target = self.into.at[goal]
+            if way:
+                target = self.into.at[jnp.where(goal == towards, p.depth, goal)]
+            p.send(self.out.at[goal], target, self.sems.at[2 * way, goal], self.sems.at[2 * way + 1, goal],
+                   p.device(z=towards), valid)
 
     def total(self, result):
         p = self.place
-        result[...] = add_up(self.parts[p.z, p.core], self.pair[p.z])
-        for way, condition in ((0, p.z > 0), (1, p.z < p.depth - 1)):
-            p.arrived(self.into.at[way, p.z], self.sems.at[2 * way + 1, p.z], condition)
-
-            def add(way=way):
-                result[...] += self.into[way, p.z].astype(F32)
+        result[...] = add_up(*self.terms(p.z))
+        for way, slot, condition in ((0, p.z, p.z > 0), (1, p.depth, p.z < p.depth - 1)):
+            p.arrived(self.into.at[slot], self.sems.at[2 * way + 1, p.z], condition)
+
+            def add(slot=slot):
+                result[...] += self.into[slot].astype(F32)
 
             when(condition, add)
+
+
+class ColumnSum:
+    @staticmethod
+    def scratch(depth, shape, dtype):
+        return PairSwap.scratch(depth, shape, dtype) + LineSum.scratch(depth, shape, dtype)
+
+    def __init__(self, place, parts, pair, pair_sems, into, sems):
+        self.place = place
+        order = [lax.rem(place.z + distance, place.depth) for distance in list(range(place.depth - 1, 0, -1)) + [0]]
+        self.order = order
+        self.swap = PairSwap(place, parts, pair, pair_sems, order)
+        self.line = LineSum(place, self.swap.terms, pair, into, sems)
+
+    def ready(self):
+        for at in self.order:
+            self.swap.wait(at)
+
+    def step(self, at):
+        self.line.step(at)
+
+    def total(self, result):
+        self.line.total(result)
 
 
 def anywhere(count):
@@ -691,18 +726,19 @@
     rows, model = tokens.shape
 
     def kernel(parts_ref, squares_ref, x_ref, gain_ref, after_ref, mixed_ref, scale_ref, rows_out,
-               pair, out, into, sems, s_pair, s_out, s_into, s_sems, second, g_sems, g_local):
+               *scratch):
         p = Place(reps, depth)
         p.barrier(plane=True, column=True)
-        squares_job = PlaneSum(p, squares_ref, s_pair, s_out, s_into, s_sems)
-        parts_job = PlaneSum(p, parts_ref, pair, out, into, sems)
+        second, g_sems, g_local = scratch[8:]
+        squares_job = PlaneSum(p, squares_ref, *scratch[4:8])
+        parts_job = PlaneSum(p, parts_ref, *scratch[:4])
         squares_job.relay()
         parts_job.relay()
         square = squares_job.total()
         scale_row = lax.rsqrt(square / inner + EPS)
         scale_ref[...] = scale_row
         mixed = column_of(scale_row[0:1, :], rows) * parts_job.total()
-        mixed_ref[...] = mixed
+        mixed_ref[...] = mixed.astype(BF16)
         after = x_ref[...].astype(F32) + mixed
         after_ref[...] = after
         second[...] = (after * rms_rows(after) * gain_ref[...]).astype(BF16)
@@ -719,7 +755,7 @@
         out_specs=in_vmem(3) + anywhere(1),
         out_shape=[
             jax.ShapeDtypeStruct((rows, model), F32),
-            jax.ShapeDtypeStruct((rows, model), F32),
+            jax.ShapeDtypeStruct((rows, model), BF16),
             jax.ShapeDtypeStruct((8, rows), F32),
             jax.ShapeDtypeStruct((depth, 2, rows, model), BF16),
         ],
@@ -732,18 +768,22 @@
     )(parts, squares, tokens, post_gain)
 
 
-def join_experts(parts, cotangent, after, mixed, scale, post_gain, inner, reps, depth):
+def join_experts(parts, layer_parts, cotangent, after, mixed, scale, post_gain, inner, reps, depth):
     rows, model = cotangent.shape
 
-    def kernel(parts_ref, g_ref, after_ref, mixed_ref, scale_ref, gain_ref,
-               grad_ref, gain_grad_ref, low_out, scale_out,
-               pair, out, into, pair_sems, sems, low, scales, l_sems, l_local, s_sems, s_local):
+    def kernel(parts_ref, layer_ref, g_ref, after_ref, mixed_ref, scale_ref, gain_ref,
+               grad_ref, gain_grad_ref, layer_out_ref, low_out, scale_out, *scratch):
+        scales, total, l_sems, l_local, s_sems, s_local = scratch[8:]
         p = Place(reps, depth)
         p.barrier(plane=True, column=True)
-        job = ColumnSum(p, parts_ref, pair, out, into, pair_sems, sems)
+        job = ColumnSum(p, parts_ref, *scratch[:4])
+        layer_job = ColumnSum(p, layer_ref, *scratch[4:8])
+        job.ready()
         for at in range(depth - 1):
             job.step(at)
+        layer_job.ready()
         job.total(grad_ref)
+        layer_job.step(0)
         second_grad = grad_ref[...]
         after_rows = after_ref[...]
         after_scale = rms_rows(after_rows)
@@ -756,66 +796,404 @@
         )
         grad_ref[...] = after_grad
         after_low = after_grad.astype(BF16)
-        low[...] = after_low
+        pair = scratch[0]
+        pair[p.z] = after_low
+        l_job = PlaneGather(p, pair.at[p.z], low_out, l_sems, l_local)
         scale_row = scale_ref[...]
-        dot_row = row_of(jnp.sum(after_low.astype(F32) * mixed_ref[...], axis=1, keepdims=True), rows)
+        dot_row = row_of(jnp.sum(after_low.astype(F32) * mixed_ref[...].astype(F32), axis=1, keepdims=True), rows)
         scales[0] = scale_row
         scales[1] = scale_row**2 * dot_row / inner
         s_job = PlaneGather(p, scales, scale_out, s_sems, s_local)
-        l_job = PlaneGather(p, low, low_out, l_sems, l_local)
+        for at in range(1, depth - 1):
+            layer_job.step(at)
         s_job.relay()
         l_job.relay()
+        layer_job.total(total)
+        layer_out_ref[...] = (total[...] + after_ref[...]).astype(BF16)
         s_job.finish()
         l_job.finish()
         p.finish()
 
     return pl.pallas_call(
         kernel,
-        in_specs=in_vmem(6),
-        out_specs=in_vmem(2) + anywhere(2),
+        in_specs=in_vmem(7),
+        out_specs=in_vmem(3) + anywhere(2),
         out_shape=[
             jax.ShapeDtypeStruct((rows, model), F32),
             jax.ShapeDtypeStruct((1, model), F32),
+            jax.ShapeDtypeStruct((rows, model), BF16),
             jax.ShapeDtypeStruct((reps, 2, rows, model), BF16),
             jax.ShapeDtypeStruct((reps, 2, 2, 8, rows), F32),
         ],
-        scratch_shapes=ColumnSum.scratch(depth, (rows, model), BF16)
-        + [pltpu.VMEM((rows, model), BF16), pltpu.VMEM((2, 8, rows), F32)]
+        scratch_shapes=ColumnSum.scratch(depth, (rows, model), BF16) * 2
+        + [pltpu.VMEM((2, 8, rows), F32), pltpu.VMEM((rows, model), F32)]
         + PlaneGather.scratch(reps) * 2,
         compiler_params=remote_params(2),
         name="join_experts",
-    )(parts, cotangent, after, mixed, scale, post_gain)
-
-
-def join_input(parts, tokens, after_grad, in_gain, reps, depth):
+    )(parts, layer_parts, cotangent, after, mixed, scale, post_gain)
+
+
+def finish_input(parts, tokens, after_grad, in_gain, side, common, out_grad, small, reps, depth):
     rows, model = tokens.shape
-
-    def kernel(parts_ref, x_ref, grad_ref, gain_ref, tokens_grad_ref, gain_grad_ref, pair, out, into, sems):
+    part, width = side.shape[2:]
+    common_width = common.shape[3]
+    quarter = out_grad.shape[1]
+    small_width = small.shape[3]
+    gain_width = -(-part // LANES) * LANES
+    x_scratch = PlaneSum.scratch(reps, (rows, model), BF16)
+    c_scratch = ColumnSum.scratch(depth, (part, common_width), BF16)
+    s_scratch = ColumnSum.scratch(depth, small.shape[2:], F32)
+    n_scratch = ColumnSum.scratch(depth, (8, gain_width), F32)
+    a_scratch = [pltpu.VMEM((depth, 2, part, width), BF16)] + LineSum.scratch(depth, (2, part, width), BF16)
+    o_scratch = [
+        pltpu.VMEM((reps, quarter, model), BF16), pltpu.SemaphoreType.DMA((2, reps)),
+        pltpu.VMEM((depth, quarter, model), BF16),
+    ] + LineSum.scratch(depth, (quarter, model), BF16)
+
+    def kernel(parts_ref, x_ref, grad_ref, gain_ref, side_ref, common_ref, out_ref, small_ref,
+               tokens_grad_ref, side_out, common_out, out_out, small_out, gain_out, *scratch):
+        x_work, c_work, s_work, n_work, a_work, o_work = (
+            scratch[:4], scratch[4:8], scratch[8:12], scratch[12:16], scratch[16:19], scratch[19:24]
+        )
+        (side_total, side_pair, swap_sems, common_total, common_low, out_total, out_low, small_total, small_all,
+         gain_parts, gain_total, gain_all, end_sems, local_sems) = scratch[24:]
         p = Place(reps, depth)
-        p.barrier(plane=True)
-        job = PlaneSum(p, parts_ref, pair, out, into, sems)
-        job.relay()
-        first_grad = job.total()
+        p.barrier(plane=True, column=True)
+        side_job = LineSum(p, lambda at: [side_ref[at]], *a_work)
+        side_job.step(0)
+        common_job = ColumnSum(p, common_ref, *c_work)
+        small_job = ColumnSum(p, small_ref, *s_work)
+        x_job = PlaneSum(p, parts_ref, *x_work)
+        out_mid, o_sems = o_work[:2]
+        for distance in range(1, reps):
+            rep = p.rep_at(distance)
+            p.send(out_ref.at[rep], out_mid.at[p.rep], o_sems.at[0, distance], o_sems.at[1, distance], p.device(rep=rep))
+        out_mid[p.rep] = out_ref[p.rep]
+        common_job.ready()
+        small_job.ready()
+        common_job.step(0)
+        small_job.step(0)
+        x_job.relay()
+        for distance in range(1, reps):
+            p.arrived(out_mid.at[p.rep_at(reps - distance)], o_sems.at[1, distance])
+        out_job = LineSum(p, lambda at: [out_mid[at]], *o_work[2:])
+        out_job.step(0)
+        for at in range(1, depth - 1):
+            for job in (side_job, common_job, small_job, out_job):
+                job.step(at)
+
+        def to_reps(source, target, at):
+            for distance in range(1, reps):
+                p.send(source, target.at[p.rep], end_sems.at[0, at, distance], end_sems.at[1, at, distance],
+                       p.device(rep=p.rep_at(distance)))
+
+        def from_reps(target, at):
+            for distance in range(1, reps):
+                p.arrived(target.at[p.rep_at(reps - distance)], end_sems.at[1, at, distance])
+
+        side_job.total(side_total)
+        side_pair[p.core] = side_total[p.core].astype(BF16)
+        side_low = a_work[0].at[p.z, 1 - p.core]
+        a_work[0][p.z, 1 - p.core] = side_total[1 - p.core].astype(BF16)
+        p.send(side_low, side_pair.at[p.core], swap_sems.at[0], swap_sems.at[1], p.sibling())
+        out_job.total(out_total)
+        out_low[...] = out_total[...].astype(BF16)
+        to_reps(out_low, out_out, 0)
+        out_keep = p.local(out_low, out_out.at[p.rep], local_sems.at[0])
+        p.arrived(side_pair.at[1 - p.core], swap_sems.at[1])
+        to_reps(side_pair, side_out, 1)
+        side_keep = p.local(side_pair, side_out.at[p.rep], local_sems.at[1])
+        common_job.total(common_total)
+        common_low[...] = common_total[...].astype(BF16)
+        to_reps(common_low, common_out, 2)
+        common_keep = p.local(common_low, common_out.at[p.rep], local_sems.at[2])
+        small_job.total(small_total)
+        small_all[p.rep] = small_total[...]
+        to_reps(small_total, small_all, 3)
+
+        first_grad = x_job.total()
         x = x_ref[...].astype(F32)
         x_scale = rms_rows(x)
-        gain_grad_ref[...] = jnp.sum(x * first_grad * x_scale, axis=0, keepdims=True)
+        gain_grad = jnp.sum(x * first_grad * x_scale, axis=0, keepdims=True)
+        gain_parts[...] = jnp.zeros_like(gain_parts)
+        for z in range(depth):
+            for core in range(2):
+                at = (2 * z + core) * part
+                gain_parts[z, core, 0:1, 0:part] = gain_grad[:, at : at + part]
+        gain_job = ColumnSum(p, gain_parts, *n_work)
         weighted = first_grad * gain_ref[...]
         tokens_grad_ref[...] = (
             grad_ref[...]
             + x_scale * weighted
             - x * x_scale**3 * jnp.mean(x * weighted, axis=1, keepdims=True)
         ).astype(BF16)
+        gain_job.ready()
+        for at in range(depth - 1):
+            gain_job.step(at)
+        gain_job.total(gain_total)
+        gain_all[p.rep] = gain_total[...]
+        to_reps(gain_total, gain_all, 4)
+        from_reps(small_all, 3)
+        small_out[...] = add_up(*[small_all[at] for at in range(reps)])
+        from_reps(gain_all, 4)
+        gain_out[...] = add_up(*[gain_all[at] for at in range(reps)])
+        for at, target, keep in ((0, out_out, out_keep), (1, side_out, side_keep), (2, common_out, common_keep)):
+            from_reps(target, at)
+            keep.wait()
         p.finish()
 
     return pl.pallas_call(
         kernel,
-        in_specs=in_vmem(4),
-        out_specs=in_vmem(2),
-        out_shape=[jax.ShapeDtypeStruct((rows, model), BF16), jax.ShapeDtypeStruct((1, model), F32)],
-        scratch_shapes=PlaneSum.scratch(reps, (rows, model), BF16),
+        in_specs=in_vmem(8),
+        out_specs=in_vmem(1) + anywhere(3) + in_vmem(2),
+        out_shape=[
+            jax.ShapeDtypeStruct((rows, model), BF16),
+            jax.ShapeDtypeStruct((reps, 2, part, width), BF16),
+            jax.ShapeDtypeStruct((reps, part, common_width), BF16),
+            jax.ShapeDtypeStruct((reps, quarter, model), BF16),
+            jax.ShapeDtypeStruct(small.shape[2:], F32),
+            jax.ShapeDtypeStruct((8, gain_width), F32),
+        ],
+        scratch_shapes=x_scratch + c_scratch + s_scratch + n_scratch + a_scratch + o_scratch
+        + [
+            pltpu.VMEM((2, part, width), F32), pltpu.VMEM((2, part, width), BF16), pltpu.SemaphoreType.DMA((2,)),
+            pltpu.VMEM((part, common_width), F32), pltpu.VMEM((part, common_width), BF16),
+            pltpu.VMEM((quarter, model), F32), pltpu.VMEM((quarter, model), BF16),
+            pltpu.VMEM(small.shape[2:], F32), pltpu.VMEM((reps,) + small.shape[2:], F32),
+            pltpu.VMEM((depth, 2, 8, gain_width), F32), pltpu.VMEM((8, gain_width), F32),
+            pltpu.VMEM((reps, 8, gain_width), F32),
+            pltpu.SemaphoreType.DMA((2, 5, reps)), pltpu.SemaphoreType.DMA((3,)),
+        ],
         compiler_params=remote_params(3),
-        name="join_input",
-    )(parts, tokens, after_grad, in_gain)
+        name="finish_input",
+    )(parts, tokens, after_grad, in_gain, side, common, out_grad, small)
+
+
+def slot_match(table_row, capacity, rows):
+    slot = lax.broadcasted_iota(jnp.int32, (capacity, rows), 0).astype(F32) + 1.0
+    return table_row == slot
+
+
+def dispatch_kernel(
+    local, capacity, half,
+    table_ref, own_ref, second_ref, g_ref, router_ref, in_ref, out_ref,
+    buffer_ref, slot_g_ref, gate_slot_ref, gates_ref, hidden_ref, grad_ref, in_grad_ref, out_grad_ref,
+    in_total, out_total,
+):
+    at = pl.program_id(0)
+    second, g = second_ref[...], g_ref[...]
+    rows = second.shape[0]
+    table = table_ref[...].astype(F32)
+    used = table > 0.0
+    logits = mm_nt(router_ref[...], second)
+    top = jnp.max(jnp.where(used, logits, -jnp.inf), axis=0, keepdims=True)
+    raw = jnp.where(used, jnp.exp(jnp.where(used, logits - top, 0.0)), 0.0)
+    gates = raw / jnp.sum(raw, axis=0, keepdims=True)
+    gates_ref[...] = gates
+    expert = lax.broadcasted_iota(jnp.int32, gates.shape, 0)
+    shard = 2 * lax.axis_index("z") + lax.axis_index("core")
+    for i in range(local):
+        match = slot_match(own_ref[i : i + 1, :].astype(F32), capacity, rows)
+        onehot = match.astype(BF16)
+        buffer_ref[i] = mm(onehot, second).astype(BF16)
+        slot_g_ref[i] = mm(onehot, g).astype(BF16)
+        gate_row = jnp.sum(jnp.where(expert == local * shard + i, gates, 0.0), axis=0, keepdims=True)
+        gate_slot = jnp.sum(jnp.where(match, gate_row, 0.0), axis=1, keepdims=True)
+        gate_slot_ref[i] = jnp.broadcast_to(gate_slot, (capacity, LANES))
+    pre = mm(second, in_ref[...])
+    a, b = pre[:, :half], pre[:, half:]
+    sig = jax.nn.sigmoid(a)
+    hidden = (a * sig * b).astype(BF16)
+    hidden_ref[...] = hidden
+    back = mm_nt(g, out_ref[...])
+    grad = jnp.concatenate([back * b * silu_slope(a, sig), back * a * sig], axis=1).astype(BF16)
+    grad_ref[...] = grad
+
+    @pl.when(at == 0)
+    def _():
+        in_total[...] = jnp.zeros_like(in_total)
+        out_total[...] = jnp.zeros_like(out_total)
+
+    in_total[...] += mm_tn(second, grad)
+    out_total[...] += mm_tn(hidden, g)
+
+    @pl.when(at == pl.num_programs(0) - 1)
+    def _():
+        in_grad_ref[...] = in_total[...].astype(BF16)
+        out_grad_ref[...] = out_total[...].astype(BF16)
+
+
+def dispatch(table, own, second, g, router_t, shared_in, shared_out, capacity):
+    group, experts, rows = table.shape
+    local = own.shape[1]
+    model = second.shape[1]
+    half = shared_out.shape[0]
+    slots = group * capacity
+
+    def by_block(*shape):
+        return pl.BlockSpec((None,) + shape, lambda q: (q,) + (0,) * len(shape))
+
+    def by_slots(width):
+        return pl.BlockSpec((local, capacity, width), lambda q: (0, q, 0))
+
+    return pl.pallas_call(
+        functools.partial(dispatch_kernel, local, capacity, half),
+        grid=(group,),
+        in_specs=[
+            by_block(experts, rows), by_block(local, rows), by_rows((rows, model)), by_rows((rows, model)),
+            whole((experts, model)), whole((model, 2 * half)), whole((half, model)),
+        ],
+        out_specs=[
+            by_slots(model), by_slots(model), by_slots(LANES), by_block(experts, rows), by_rows((rows, half)),
+            by_rows((rows, 2 * half)), whole((model, 2 * half)), whole((half, model)),
+        ],
+        out_shape=[
+            jax.ShapeDtypeStruct((local, slots, model), BF16),
+            jax.ShapeDtypeStruct((local, slots, model), BF16),
+            jax.ShapeDtypeStruct((local, slots, LANES), F32),
+            jax.ShapeDtypeStruct((group, experts, rows), F32),
+            jax.ShapeDtypeStruct((group * rows, half), BF16),
+            jax.ShapeDtypeStruct((group * rows, 2 * half), BF16),
+            jax.ShapeDtypeStruct((model, 2 * half), BF16),
+            jax.ShapeDtypeStruct((half, model), BF16),
+        ],
+        scratch_shapes=[pltpu.VMEM((model, 2 * half), F32), pltpu.VMEM((half, model), F32)],
+        compiler_params=pltpu.CompilerParams(vmem_limit_bytes=56 * 2**20),
+        name="dispatch",
+    )(table, own, second, g, router_t, shared_in, shared_out)
+
+
+def experts_kernel(
+    buffer_ref, slot_g_ref, gate_ref, in_ref, out_ref,
+    weighted_ref, back_ref, dot_ref, in_grad_ref, out_grad_ref, in_total, out_total,
+):
+    at = pl.program_id(1)
+    buffer, weight_in, weight_out = buffer_ref[...], in_ref[...], out_ref[...]
+    half = weight_out.shape[0]
+    pre = mm(buffer, weight_in)
+    a, b = pre[:, :half], pre[:, half:]
+    sig = jax.nn.sigmoid(a)
+    act = a * sig
+    hidden = (act * b).astype(BF16)
+    gate = gate_ref[:, 0:1]
+    slot_g = slot_g_ref[...].astype(F32)
+    result = mm(hidden, weight_out).astype(BF16).astype(F32)
+    weighted_ref[...] = (gate * result).astype(BF16)
+    dot_ref[...] = jnp.broadcast_to(jnp.sum(slot_g * result, axis=1, keepdims=True), dot_ref.shape)
+    result_grad = (gate * slot_g).astype(BF16)
+    hidden_grad = mm_nt(result_grad, weight_out)
+    pre_grad = jnp.concatenate([hidden_grad * b * silu_slope(a, sig), hidden_grad * act], axis=1).astype(BF16)
+    back_ref[...] = mm_nt(pre_grad, weight_in).astype(BF16)
+
+    @pl.when(at == 0)
+    def _():
+        in_total[...] = jnp.zeros_like(in_total)
+        out_total[...] = jnp.zeros_like(out_total)
+
+    in_total[...] += mm_tn(buffer, pre_grad)
+    out_total[...] += mm_tn(hidden, result_grad)
+
+    @pl.when(at == pl.num_programs(1) - 1)
+    def _():
+        in_grad_ref[...] = in_total[...].astype(BF16)
+        out_grad_ref[...] = out_total[...].astype(BF16)
+
+
+def run_experts(buffer, slot_g, gate_slot, expert_in, expert_out, step):
+    local, slots, model = buffer.shape
+    half = expert_out.shape[1]
+
+    def by_step(width):
+        return pl.BlockSpec((None, step, width), lambda i, m: (i, m, 0))
+
+    def by_expert(*shape):
+        return pl.BlockSpec((None,) + shape, lambda i, m: (i, 0, 0))
+
+    return pl.pallas_call(
+        experts_kernel,
+        grid=(local, slots // step),
+        in_specs=[
+            by_step(model), by_step(model), by_step(LANES), by_expert(model, 2 * half), by_expert(half, model),
+        ],
+        out_specs=[
+            by_step(model), by_step(model), by_step(LANES), by_expert(model, 2 * half), by_expert(half, model),
+        ],
+        out_shape=[
+            jax.ShapeDtypeStruct((local, slots, model), BF16),
+            jax.ShapeDtypeStruct((local, slots, model), BF16),
+            jax.ShapeDtypeStruct((local, slots, LANES), F32),
+            jax.ShapeDtypeStruct((local, model, 2 * half), BF16),
+            jax.ShapeDtypeStruct((local, half, model), BF16),
+        ],
+        scratch_shapes=[pltpu.VMEM((model, 2 * half), F32), pltpu.VMEM((half, model), F32)],
+        compiler_params=pltpu.CompilerParams(vmem_limit_bytes=62 * 2**20),
+        name="run_experts",
+    )(buffer, slot_g, gate_slot, expert_in, expert_out)
+
+
+def combine_kernel(
+    local, capacity,
+    own_ref, gates_ref, dot_ref, weighted_ref, back_ref, second_ref, hidden_ref, grad_ref, router_ref, in_ref, out_ref,
+    second_part_ref, layer_part_ref, router_grad_ref,
+):
+    gates = gates_ref[...]
+    rows = gates.shape[1]
+    expert = lax.broadcasted_iota(jnp.int32, gates.shape, 0)
+    shard = 2 * lax.axis_index("z") + lax.axis_index("core")
+    gate_grad = jnp.zeros_like(gates)
+    second_part = mm_nt(grad_ref[...], in_ref[...])
+    layer_part = mm(hidden_ref[...], out_ref[...])
+    for i in range(local):
+        match = slot_match(own_ref[i : i + 1, :].astype(F32), capacity, rows)
+        onehot = match.astype(BF16)
+        second_part = second_part + mm_tn(onehot, back_ref[i])
+        layer_part = layer_part + mm_tn(onehot, weighted_ref[i])
+        row = jnp.sum(jnp.where(match, dot_ref[i, :, 0:1], 0.0), axis=0, keepdims=True)
+        gate_grad = jnp.where(expert == local * shard + i, row, gate_grad)
+    logit_grad = gates * (gate_grad - jnp.sum(gates * gate_grad, axis=0, keepdims=True))
+    high, low = split_two(logit_grad)
+    router = router_ref[...]
+    second_part = second_part + mm_tn(high, router) + mm_tn(low, router)
+    second_part_ref[...] = second_part.astype(BF16)
+    layer_part_ref[...] = layer_part.astype(BF16)
+    second = second_ref[...]
+
+    @pl.when(pl.program_id(0) == 0)
+    def _():
+        router_grad_ref[...] = jnp.zeros_like(router_grad_ref)
+
+    router_grad_ref[...] += mm(high, second) + mm(low, second)
+
+
+def combine(own, gates, dots, weighted, back, second, hidden, grad, router_t, shared_in, shared_out, capacity):
+    group, experts, rows = gates.shape
+    local = own.shape[1]
+    model = second.shape[1]
+    half = shared_out.shape[0]
+
+    def by_block(*shape):
+        return pl.BlockSpec((None,) + shape, lambda q: (q,) + (0,) * len(shape))
+
+    def by_slots(width):
+        return pl.BlockSpec((local, capacity, width), lambda q: (0, q, 0))
+
+    return pl.pallas_call(
+        functools.partial(combine_kernel, local, capacity),
+        grid=(group,),
+        in_specs=[
+            by_block(local, rows), by_block(experts, rows), by_slots(LANES), by_slots(model), by_slots(model),
+            by_rows((rows, model)), by_rows((rows, half)), by_rows((rows, 2 * half)),
+            whole((experts, model)), whole((model, 2 * half)), whole((half, model)),
+        ],
+        out_specs=[by_rows((rows, model)), by_rows((rows, model)), whole((experts, model))],
+        out_shape=[
+            jax.ShapeDtypeStruct((group * rows, model), BF16),
+            jax.ShapeDtypeStruct((group * rows, model), BF16),
+            jax.ShapeDtypeStruct((experts, model), F32),
+        ],
+        compiler_params=pltpu.CompilerParams(vmem_limit_bytes=56 * 2**20),
+        name="combine",
+    )(own, gates, dots, weighted, back, second, hidden, grad, router_t, shared_in, shared_out)
 
 
 def gather(values, axes, axis=0):
@@ -924,11 +1302,15 @@
     post_gain = unpacked[8].reshape(1, model).astype(F32)
     router_full = unpacked[9].reshape(model, experts)
 
-    g_column = gather(cotangent, COLUMN)
+    g_column = gather(lax.optimization_barrier((cotangent, x_plane))[0], COLUMN)
     shared_in_own = lax.all_to_all(
         shared_in.reshape(part, 2, group, shared).transpose(2, 0, 1, 3).reshape(group * part, 2 * shared),
         COLUMN, split_axis=0, concat_axis=0, tiled=True,
     )
+
+    dealt_column = lax.dynamic_index_in_dim(numbers_all[:, :, 3], rep, axis=0, keepdims=False)
+    table_dealt = jnp.take(table_all, dealt_column, axis=0)
+    table_own = columns_of(table_dealt, local * shard, local)
 
     blocks = numbers_all[:, :, 3].reshape(reps, depth, 2)
     dealt_plane = lax.dynamic_index_in_dim(blocks, z, axis=1, keepdims=False)
@@ -954,123 +1336,33 @@
     )
     second_column = second_column.reshape(group * rows, model)
 
-    second_blocks = second_column.reshape(group, rows, model)
-    g_blocks = g_column.reshape(group, rows, model)
-    dealt_column = lax.dynamic_index_in_dim(numbers_all[:, :, 3], rep, axis=0, keepdims=False)
-    table_dealt = jnp.take(table_all, dealt_column, axis=0)
-    logits = mm(second_column, router_full).reshape(group, rows, experts)
-    used = table_dealt.transpose(0, 2, 1) > 0
-    top_logit = jnp.max(jnp.where(used, logits, -jnp.inf), axis=2, keepdims=True)
-    raw = jnp.where(used, jnp.exp(jnp.where(used, logits - top_logit, 0.0)), 0.0)
-    gates = raw / jnp.sum(raw, axis=2, keepdims=True)
-    slots = columns_of(table_dealt, local * shard, local).astype(jnp.int32) - 1
-    onehot_mask = slots[:, :, None, :] == jnp.arange(capacity, dtype=jnp.int32)[None, None, :, None]
-    onehot = onehot_mask.astype(BF16)
-    gates_own = columns_of(gates, local * shard, local, axis=2).transpose(0, 2, 1)
-    gate_slot = jnp.sum(jnp.where(onehot_mask, gates_own[:, :, None, :], 0.0), axis=3)
-    gate_slot = gate_slot.transpose(1, 0, 2).reshape(local, group * capacity, 1)
-
-    def to_slots(values):
-        return jnp.einsum("qict,qtd->iqcd", onehot, values, preferred_element_type=F32).astype(BF16).reshape(
-            local, group * capacity, model
-        )
-
-    def to_rows(values):
-        return jnp.einsum(
-            "qict,iqcd->qtd", onehot, values.reshape(local, group, capacity, model), preferred_element_type=F32
-        ).reshape(group * rows, model)
-
-    buffer = to_slots(second_blocks)
-    slot_g = to_slots(g_blocks)
-    expert_pre = jnp.einsum("ind,idf->inf", buffer, expert_in, preferred_element_type=F32)
-    half = expert_pre.shape[2] // 2
-    pre_a, pre_b = expert_pre[:, :, :half], expert_pre[:, :, half:]
-    sig_a = jax.nn.sigmoid(pre_a)
-    hidden = (pre_a * sig_a * pre_b).astype(BF16)
-    result = jnp.einsum("inf,ifd->ind", hidden, expert_out, preferred_element_type=F32).astype(BF16)
-    shared_pre = mm(second_column, shared_in_own)
-    shared_a, shared_b = shared_pre[:, :shared], shared_pre[:, shared:]
-    shared_sig = jax.nn.sigmoid(shared_a)
-    shared_hidden = (shared_a * shared_sig * shared_b).astype(BF16)
-
-    result_grad = (gate_slot * slot_g.astype(F32)).astype(BF16)
-    hidden_grad = jnp.einsum("ind,ifd->inf", result_grad, expert_out, preferred_element_type=F32)
-    pre_grad = jnp.concatenate(
-        [hidden_grad * pre_b * silu_slope(pre_a, sig_a), hidden_grad * pre_a * sig_a], axis=2
-    ).astype(BF16)
-    buffer_grad = jnp.einsum("inf,idf->ind", pre_grad, expert_in, preferred_element_type=F32).astype(BF16)
-    shared_back = mm_nt(g_column, shared_out)
-    shared_grad = jnp.concatenate(
-        [shared_back * shared_b * silu_slope(shared_a, shared_sig), shared_back * shared_a * shared_sig], axis=1
-    ).astype(BF16)
-    slot_dot = jnp.sum(slot_g.astype(F32) * result.astype(F32), axis=2).reshape(local, group, capacity)
-    gate_grad = jnp.sum(jnp.where(onehot_mask, slot_dot.transpose(1, 0, 2)[:, :, :, None], 0.0), axis=2)
-    gate_sum = jnp.sum(gates_own * gate_grad, axis=1)
-    own_expert = (expert_ids[None, :] == (local * shard + jnp.arange(local, dtype=jnp.int32))[:, None]).astype(F32)
-    gate_full = jnp.sum(gate_grad[:, :, :, None] * own_expert[None, :, None, :], axis=1)
-    logit_grad = (gates * (gate_full - gate_sum[:, :, None])).reshape(group * rows, experts)
-    logit_pair = jnp.concatenate(split_two(logit_grad), axis=1)
-    second_part = (
-        to_rows(buffer_grad)
-        + mm_nt(logit_pair, jnp.concatenate([router_full, router_full], axis=1))
-        + mm_nt(shared_grad, shared_in_own)
-    )
-
-    layer_part = to_rows((gate_slot * result.astype(F32)).astype(BF16)) + mm(shared_hidden, shared_out)
-    layer_sum = scatter_sum(layer_part.astype(BF16), COLUMN).astype(F32)
-    layer_out = (after + layer_sum).astype(BF16)
-
-    grad_expert_out = jnp.einsum("inf,ind->ifd", hidden, result_grad, preferred_element_type=F32)
-    grad_expert_in = jnp.einsum("ind,inf->idf", buffer, pre_grad, preferred_element_type=F32)
-    grad_expert_out = lax.psum(grad_expert_out.astype(BF16), "rep").astype(F32)
-    grad_expert_in = lax.psum(grad_expert_in.astype(BF16), "rep").astype(F32)
-    grad_shared_out = lax.psum(mm_tn(shared_hidden, g_column).astype(BF16), "rep").astype(F32)
-    shared_in_columns = mm_tn(second_column, shared_grad).astype(BF16)
-    shared_in_rows = lax.all_to_all(shared_in_columns, COLUMN, split_axis=0, concat_axis=0, tiled=True)
+    router_t = router_full.T
+    buffer, slot_g, gate_slot, gates, shared_hidden, shared_grad, shared_in_grad, shared_out_grad = dispatch(
+        table_dealt, table_own, second_column, g_column, router_t, shared_in_own, shared_out, capacity
+    )
+    weighted, buffer_grad, dots, grad_expert_in, grad_expert_out = run_experts(
+        buffer, slot_g, gate_slot, expert_in, expert_out, group * capacity // 2
+    )
+    second_part, layer_part, router_grad = combine(
+        table_own, gates, dots, weighted, buffer_grad, second_column, shared_hidden, shared_grad, router_t,
+        shared_in_own, shared_out, capacity,
+    )
+    shared_in_rows = lax.all_to_all(shared_in_grad, COLUMN, split_axis=0, concat_axis=0, tiled=True)
     shared_in_rows = shared_in_rows.reshape(group, part, 2, shared).transpose(1, 2, 0, 3).reshape(part, -1)
-    grad_shared_in = lax.psum(shared_in_rows, "rep").astype(F32)
-    router_pair = mm_tn(second_column, logit_pair)
-    router_grad = router_pair[:, :experts] + router_pair[:, experts:]
-
-    after_grad, post_grad, low_plane, scales = join_experts(
-        second_part.astype(BF16).reshape(depth, 2, rows, model), cotangent, after, mixer_result, scale, post_gain,
-        inner, reps, depth,
+    grad_expert_in, grad_expert_out, grad_shared_out, grad_shared_in = [
+        values.astype(F32)
+        for values in lax.psum((grad_expert_in, grad_expert_out, shared_out_grad, shared_in_rows), "rep")
+    ]
+    router_grad = router_grad.T
+
+    after_grad, post_grad, layer_out, low_plane, scales = join_experts(
+        second_part.reshape(depth, 2, rows, model), layer_part.reshape(depth, 2, rows, model), cotangent, after,
+        mixer_result, scale, post_gain, inner, reps, depth,
     )
     back_parts, in_grad, out_grad, taps_grad, heads_grad, wide_grad = mixer_backward(
         mixer_args, projected, low_plane.reshape(members * rows, model), scales.reshape(members, 2, 8, rows),
         rows, channels, width, state,
     )
-    grad_tokens, in_norm_grad = join_input(
-        back_parts.reshape(reps, 2, rows, model), tokens, after_grad, in_gain, reps, depth
-    )
-
-    in_low = in_grad.astype(BF16)
-    first_core = core == 0
-    pair = 2 * channels
-
-    def paired(values):
-        empty = jnp.zeros_like(values)
-        return [jnp.where(first_core, values, empty), jnp.where(first_core, empty, values)]
-
-    in_pair = jnp.concatenate(
-        paired(in_low[:, :channels]) + paired(in_low[:, channels:pair]) + [in_low[:, pair:]], axis=1
-    )
-    in_rows = gather(scatter_sum(in_pair, COLUMN), "rep").reshape(reps, part, -1).transpose(1, 0, 2)
-    dt_rows = in_rows[:, :, 2 * pair + 2 * state :].reshape(part, reps, 2, LANES // 2)[:, :, :, :heads]
-    grad_in_proj = jnp.concatenate(
-        [
-            in_rows[:, :, :pair].reshape(part, inner).astype(F32),
-            in_rows[:, :, pair : 2 * pair].reshape(part, inner).astype(F32),
-            jnp.sum(in_rows[:, :, 2 * pair : 2 * pair + 2 * state].astype(F32), axis=1),
-            dt_rows.reshape(part, head_count).astype(F32),
-        ],
-        axis=1,
-    )
-    out_chunk = scatter_sum(out_grad.astype(BF16), "z")
-    out_chunks = gather(out_chunk[None], "rep")
-    out_rows = lax.all_to_all(out_chunks, "z", split_axis=0, concat_axis=0, tiled=True)
-    grad_out_proj = out_rows.reshape(channels, model).astype(F32)
-
     def placed(values, size, start):
         blank_row = jnp.zeros(values.shape[:-1] + (size,), F32)
         return lax.dynamic_update_slice_in_dim(blank_row, values, start, axis=values.ndim - 1)
@@ -1080,7 +1372,6 @@
     )
     skip_head_grad = jnp.sum(wide_grad[1].reshape(heads, width), axis=1)
     small = [
-        in_norm_grad.reshape(group, -1),
         taps_full_grad.reshape(5, group, -1).transpose(1, 0, 2).reshape(group, -1),
         placed(heads_grad[0, :heads], head_count, heads * team).reshape(group, -1),
         placed(heads_grad[1, :heads], head_count, heads * team).reshape(group, -1),
@@ -1090,26 +1381,46 @@
         router_grad.reshape(group, -1),
     ]
     small_sizes = [piece.shape[1] for piece in small]
-    small_sum = lax.psum(scatter_sum(jnp.concatenate(small, axis=1), COLUMN), "rep")[0]
+    small = jnp.concatenate(small, axis=1)
+    small_wide = -(-small.shape[1] // (8 * LANES)) * LANES
+    small = jnp.pad(small, ((0, 0), (0, 8 * small_wide - small.shape[1]))).reshape(depth, 2, 8, small_wide)
+    pair = 2 * channels
+    in_low = in_grad.astype(BF16).reshape(depth, 2, part, -1)
+    grad_tokens, side_rows, common_rows, out_rows, small_sum, gain_sum = finish_input(
+        back_parts.reshape(reps, 2, rows, model), tokens, after_grad, in_gain, in_low[:, :, :, :pair],
+        in_low[:, :, :, pair:], out_grad.astype(BF16).reshape(reps, channels // reps, model), small, reps, depth,
+    )
+    small_sum = small_sum.reshape(-1)
+    dt_rows = common_rows[:, :, 2 * state :].reshape(reps, part, 2, LANES // 2)[:, :, :, :heads]
+    grad_in_proj = jnp.concatenate(
+        [
+            side_rows[:, :, :, :channels].transpose(2, 0, 1, 3).reshape(part, inner).astype(F32),
+            side_rows[:, :, :, channels:].transpose(2, 0, 1, 3).reshape(part, inner).astype(F32),
+            jnp.sum(common_rows[:, :, : 2 * state].astype(F32), axis=0),
+            dt_rows.transpose(1, 0, 2, 3).reshape(part, head_count).astype(F32),
+        ],
+        axis=1,
+    )
+    grad_out_proj = out_rows.reshape(channels, model).astype(F32)
     small_out, offset = [], 0
     for size in small_sizes:
         small_out.append(small_sum[offset : offset + size])
         offset += size
-    taps_out = small_out[1].reshape(5, -1)
+    taps_out = small_out[0].reshape(5, -1)
     return (
         layer_out,
         grad_tokens,
-        small_out[0],
+        gain_sum[0, :part],
         grad_in_proj,
         taps_out[:4],
         taps_out[4],
+        small_out[1],
         small_out[2],
         small_out[3],
         small_out[4],
+        grad_out_proj,
         small_out[5],
-        grad_out_proj,
-        small_out[6],
-        small_out[7].reshape(part, experts),
+        small_out[6].reshape(part, experts),
         grad_shared_in,
         grad_shared_out,
         grad_expert_in,

time: 1210 us -> 768 us (0.63)
  waiting for transfers between devices: 370 us -> 0.04 us
  matrix products: 137 us -> 0 us
  Pallas kernels: 492 us -> 627 us
  other arithmetic: 69 us -> 35.6 us
  local copies, waits for them, and re-layouts: 84.9 us -> 67 us
  blocking collectives: 16.6 us -> 0 us
    psum x1, waiting for transfers between devices: 190 us -> 0.01 us  [shards(): lax.psum((grad_expert_in, grad_expert_out, shared_out_grad, shared_in_row...]
    pallas_call x2 -> x5, Pallas kernels: 156 us -> 327 us  [the longest x1 127 us: join_experts(): pl.pallas_call(kernel, in_specs=in_vmem(7), out_specs=in_vmem(3) + anywhe...]
    dot_general x19 -> x0, matrix products: 137 us -> none  [the longest x3 22 us: mm_nt(): lax.dot_general(left, right, (((1,), (1,)), ((), ())), preferred_element_...]
    unnamed x9 -> x2, waiting for transfers between devices: 65.9 us -> 0.03 us
    reduce_scatter x3 -> x0, waiting for transfers between devices: 63.1 us -> none  [scatter_sum(): return lax.psum_scatter(values, axes, scatter_dimension=axis, tiled=True)]
    all_gather x3 -> x1, waiting for transfers between devices: 51.1 us -> 0.01 us  [gather(): return lax.all_gather(values, axes, axis=axis, tiled=True)]
    pallas_call x1, Pallas kernels: 145 us -> 95.4 us  [start_gather(): pl.pallas_call(kernel, in_specs=anywhere(7), out_specs=anywhere(6), out_s...]
    convert_element_type x15 -> x8, other arithmetic: 46.7 us -> 25.7 us  [the longest x4 17.2 us: shards(): values.astype(F32)]
  transfers between devices with their start and end apart: 11 -> 4, of which waited for: 6 -> 0; matrix products, arithmetic and copies ran while one was open for 13% -> 8% of each run, Pallas kernels for 27% -> 68%
where the time goes in v2:
time: 768 us; the launch traced here: 753 us
  Pallas kernels  627 us (82%)
  local copies, waits for them, and re-layouts  67 us (9%)
  other arithmetic  35.6 us (5%)
  between operations  15.4 us (2%)
    pallas_call x1, Pallas kernels, join_experts(): pl.pallas_call(kernel, in_specs=in_vmem(7), out_specs=in_vmem(3) + anywhe...  127 us
    pallas_call x1, Pallas kernels, finish_input(): pl.pallas_call(kernel, in_specs=in_vmem(8), out_specs=in_vmem(1) + anywhe...  118 us
    pallas_call x1, Pallas kernels, join_mixer(): pl.pallas_call(kernel, in_specs=in_vmem(4), out_specs=in_vmem(3) + anywhe...  116 us
    pallas_call x1, Pallas kernels, start_gather(): pl.pallas_call(kernel, in_specs=anywhere(7), out_specs=anywhere(6), out_s...  95.4 us
    pallas_call x1, Pallas kernels, mixer_backward(): pl.pallas_call(functools.partial(mixer_backward_kernel, channels, width,...  59.3 us
    pallas_call x1, Pallas kernels, run_experts(): pl.pallas_call(experts_kernel, grid=(local, slots // step), in_specs=[by_...  41.5 us
    pallas_call x1, Pallas kernels, mixer_forward(): pl.pallas_call(functools.partial(mixer_forward_kernel, channels, width, s...  30.2 us
    pallas_call x1, Pallas kernels, combine(): pl.pallas_call(functools.partial(combine_kernel, local, capacity), grid=(...  21.3 us
  transfers between devices with their start and end apart: 4, of which 0 were waited for; matrix products, arithmetic and copies ran while one was open for 8% of the time, Pallas kernels for 68%

profile of v2, /device:TPU:0, one launch (start us, length us, event | category | flops | bytes accessed | tf_op | source)
XLA Modules:
  0.0 752.5 jit_solution(9407498036257094002)
XLA Ops:
  7.3 1.1 constant_dynamic-slice_fusion.6
  10.6 0.8 copy.90
  11.5 4.8 concatenate.33
  17.7 1.5 constant_dynamic-slice_fusion.8
  19.5 95.4 %start_gather.1 = (bf16[4,2,256,1536]{3,2,1,0:T(8,128)(2,1)S(1)}, bf16[4,2,192,1152]{3,2,1,0:T(8,128)(2,1)S(1)}, bf16[4,2,16,640]{3,2,1,0:T(8,128)(2,1)S(1)}, s3...) custom-call(bf16[256,1536]{1,0:T(8,128)(2,1)S(1)} %copy-done.2, ...), custom_call_target="tpu_custom_call" | custom-call | tf_op jit(solution)/shard_map/start_gather/pallas_call | solution.py:695
  114.9 2.7 copy-done
  117.6 1.8 copy-done.1
  119.4 1.0 copy-done.3
  120.5 1.3 copy.120
  122.4 1.4 all_to_all.13
  123.8 3.6 all-to-all-start
  131.3 1.3 copy.118
  138.0 30.2 %mixer_forward.1 = (bf16[2048,1536]{1,0:T(8,128)(2,1)}, f32[8,8,256]{2,1,0:T(8,128)}, f32[2048,1152]{1,0:T(8,128)}) custom-call(bf16[2048,1536]{1,0:T(8,128)(2,1)} %bitcast.94, f32[1,1536]{1,0:T(1,128)} %reshape.379.gain_ref, bf16[1536,1152]{1,0:T(8,128)(2,1)} %bitcast.96, s32[2048,1]{1,0:T(8,128)} %bitcast.106, s32[8,1,256]{2,1,0:T(1,128)} %broadcast_in_dim.66.seg_row_ref, ...), custom_call_target="tpu_custom_call" | custom-call | tf_op jit(solution)/shard_map/mixer_forward/pallas_call | solution.py:270
  168.2 115.7 %join_mixer.1 = (f32[256,1536]{1,0:T(8,128)}, bf16[256,1536]{1,0:T(8,128)(2,1)}, f32[8,256]{1,0:T(8,128)}, bf16[4,2,256,1536]{3,2,1,0:T(8,128)(2,1)}) custom-call(bf16[4,2,256,1536]{3,2,1,0:T(8,128)(2,1)} %bitcast.113, f32[4,2,8,256]{3,2,1,0:T(8,128)} %bitcast.142, bf16[256,1536]{1,0:T(8,128)(2,1)} %x_ref.5, f32[1,1536]{1,0:T(1,128)} %reshape.384.gain_ref), custom_call_target="tpu_custom_call" | custom-call | tf_op jit(solution)/shard_map/join_mixer/pallas_call | solution.py:752
  284.7 0.9 copy-done.6
  285.5 18.9 %dispatch.1 = (bf16[2,1024,1536]{2,1,0:T(8,128)(2,1)}, bf16[2,1024,1536]{2,1,0:T(8,128)(2,1)}, f32[2,1024,128]{2,1,0:T(8,128)}, f32[8,16,256]{2,1,0:T(8,128)}, b...) custom-call(bf16[8,16,256]{2,1,0:T(8,128)(2,1)} %copy-done.13, ...), custom_call_target="tpu_custom_call" | custom-call | tf_op jit(solution)/shard_map/dispatch/pallas_call | solution.py:1039
  304.4 3.6 all-to-all-start.1
  308.1 41.5 %run_experts.1 = (bf16[2,1024,1536]{2,1,0:T(8,128)(2,1)}, bf16[2,1024,1536]{2,1,0:T(8,128)(2,1)}, f32[2,1024,128]{2,1,0:T(8,128)}, bf16[2,1536,1024]{2,1,0:T(8,128)(2,1)}, bf16[2,512,1536]{2,1,0:T(8,128)(2,1)}) custom-call(bf16[2,1024,1536]{2,1,0:T(8,128)(2,1)} %get-tuple-element.73.buffer_ref, bf16[2,1024,1536]{2,1,0:T(8,128)(2,1)} %get-tuple-element.74.slot_g_ref, ...), custom_call_target="tpu_custom_call" | custom-call | tf_op jit(solution)/shard_map/run_experts/pallas_call | solution.py:1112
  349.8 0.9 copy.108
  350.7 1.1 copy.126
  351.8 21.3 %combine.1 = (bf16[2048,1536]{1,0:T(8,128)(2,1)}, bf16[2048,1536]{1,0:T(8,128)(2,1)}, f32[16,1536]{1,0:T(8,128)}) custom-call(bf16[8,2,256]{2,1,0:T(2,128)(2,1)} %constant_dynamic-slice_fusion.3.own_ref, f32[8,16,256]{2,1,0:T(8,128)} %get-tuple-element.72.gates_ref, f32[2,1024,128]{2,1,0:T(8,128)} %get-tuple-element.76.dot_ref, ...), custom_call_target="tpu_custom_call" | custom-call | tf_op jit(solution)/shard_map/combine/pallas_call | solution.py:1180
  373.1 126.9 %join_experts.1 = (f32[256,1536]{1,0:T(8,128)}, f32[1,1536]{1,0:T(1,128)}, bf16[256,1536]{1,0:T(8,128)(2,1)}, bf16[4,2,256,1536]{3,2,1,0:T(8,128)(2,1)}, f32[4,2,2,8,256]{4,3,2,1,0:T(8,128)}) custom-call(bf16[4,2,256,1536]{3,2,1,0:T(8,128)(2,1)} %bitcast.111, bf16[4,2,256,1536]{3,2,1,0:T(8,128)(2,1)} %bitcast.112, bf16[256,1536]{1,0:T(8,128)(2,1)} %g_ref.1, ...), custom_call_target="tpu_custom_call" | custom-call | tf_op jit(solution)/shard_map/join_experts/pallas_call | solution.py:817
  500.0 59.3 %mixer_backward.1 = (bf16[2048,1536]{1,0:T(8,128)(2,1)}, f32[1536,1152]{1,0:T(8,128)}, f32[384,1536]{1,0:T(8,128)}, f32[8,640]{1,0:T(8,128)}, f32[8,128]{1,0:T(8,128)}, /*index=5*/f32[8,384]{1,0:T(8,128)}) custom-call(bf16[2048,1536]{1,0:T(8,128)(2,1)} %bitcast.95, f32[1,1536]{1,0:T(1,128)} %reshape.379.gain_ref, bf16[1536,1152]{1,0:T(8,128)(2,1)} %bitcast.97, ...), custom_call_target="tpu_custom_call" | custom-call | tf_op jit(solution)/shard_map/mixer_backward/pallas_call | solution.py:292
  559.4 3.8 convert_element_type.131
  563.2 1.6 slice.184.side_ref
  564.7 1.1 slice.185.common_ref
  565.9 1.1 convert_element_type.132
  569.1 0.8 slice_reduce_fusion
  572.3 117.9 %finish_input.1 = (bf16[256,1536]{1,0:T(8,128)(2,1)}, bf16[4,2,192,768]{3,2,1,0:T(8,128)(2,1)}, bf16[4,192,384]{2,1,0:T(8,128)(2,1)}, bf16[4,96,1536]{2,1,0:T(8,...) custom-call(bf16[4,2,256,1536]{3,2,1,0:T(8,128)(2,1)} %bitcast.110, bf16[256,1536]{1,0:T(8,128)(2,1)} %x_ref.5, ...), custom_call_target="tpu_custom_call" | custom-call | tf_op jit(solution)/shard_map/finish_input/pallas_call | solution.py:945
  693.5 1.3 slice.152
  694.7 0.9 slice.156
  696.6 3.5 convert_bitcast_fusion.1
  700.1 3.2 copy.105
  703.4 3.2 reshape.386
  706.6 4.9 copy.104
  711.5 4.2 reshape.385
  716.4 1.4 reshape.376
  717.8 1.6 copy.109
  719.4 1.2 convert_reduce_fusion
  720.6 1.4 fusion.4
  722.0 1.8 bitcast_convert_fusion
  723.8 2.7 pad_maximum_fusion
  726.5 2.5 convert_element_type.145
  728.9 2.0 convert_element_type.146
  730.9 9.3 %convert_element_type.147 = f32[2,1536,1024]{2,1,0:T(8,128)} convert(bf16[2,1536,1024]{2,1,0:T(8,128)(2,1)} %get-tuple-element.164) | non-fusion elementwise | flops 3145728 | bytes 18874368 | tf_op jit(solution)/shard_map/convert_element_type | solution.py:1353
  740.1 3.6 convert_element_type.148
  743.7 0.9 copy.143
  744.6 0.9 copy.144
  (155 shorter events, 23.4 us)
Async XLA Ops:
  7.2 12.1 %slice-start = ((bf16[192,6448]{1,0:T(8,128)(2,1)}), bf16[192,256]{1,0:T(8,128)(2,1)S(1)}, s32[]{:S(2)}) async-start(bf16[192,6448]{1,0:T(8,128)(2,1)} %param.28), calls=%async_computation.4 | async-start | bytes 196608 | tf_op jit(solution)/shard_map/slice | solution.py:1272
  7.2 12.3 %copy-start.2 = (bf16[256,1536]{1,0:T(8,128)(2,1)S(1)}, bf16[256,1536]{1,0:T(8,128)(2,1)}, u32[]{:S(2)}) copy-start(bf16[256,1536]{1,0:T(8,128)(2,1)} %x_ref.5) | copy-start | bytes 2359300
  7.2 12.3 %copy-start.4 = (bf16[384,1536]{1,0:T(8,128)(2,1)S(1)}, bf16[384,1536]{1,0:T(8,128)(2,1)}, u32[]{:S(2)}) copy-start(bf16[384,1536]{1,0:T(8,128)(2,1)} %param.35) | copy-start | bytes 3538948
  7.2 277.4 %all-gather.2.cloned.1.call-start = ((), (), s32[]{:S(2)}) async-start(), calls=%async_computation.2 | async-start | bytes 7077888 | tf_op jit(solution)/shard_map/all_gather | solution.py:1200
  114.9 2.7 copy-start
  117.6 1.8 copy-start.1
  119.4 1.0 copy-start.3
  123.8 160.9 %all-to-all-start = ((bf16[8,192,256]{2,1,0:T(8,128)(2,1)}), bf16[8,192,256]{2,1,0:T(8,128)(2,1)S(1)}, u32[]{:S(2)}, u32[]{:S(2)}) async-start(bf16[8,192,256]{2,1,0:T(8,128)(2,1)} %all_to_all.13), calls=%async_computation | async-start | bytes 1572864 | tf_op jit(solution)/shard_map/all_to_all | solution.py:1306
  284.0 0.6 copy-start.13
  284.6 0.9 copy-start.6
  304.4 45.2 %all-to-all-start.1 = ((bf16[8,192,256]{2,1,0:T(8,128)(2,1)}), bf16[8,192,256]{2,1,0:T(8,128)(2,1)S(1)}, u32[]{:S(2)}, u32[]{:S(2)}) async-start(bf16[8,192,256]{2,1,0:T(8,128)(2,1)} %bitcast.120), calls=%async_computation.1 | async-start | bytes 1572864 | tf_op jit(solution)/shard_map/all_to_all | solution.py:1350
  308.0 418.5 %all-reduce.7.cloned.1.call-start = ((), (), s32[]{:S(2)}) async-start(), calls=%async_computation.3 | async-start | bytes 21233664 | tf_op jit(solution)/shard_map/psum | solution.py:1354
  563.2 2.7 copy-start.8
  564.7 2.3 copy-start.16
  564.7 5.9 copy-start.17
  564.7 6.0 copy-start.15
  690.9 3.8 copy-start.14
  711.5 4.2 slice-start.1
  711.5 10.5 %copy-start.9 = (bf16[4,96,1536]{2,1,0:T(8,128)(2,1)S(1)}, bf16[4,96,1536]{2,1,0:T(8,128)(2,1)}, u32[]{:S(2)}) copy-start(bf16[4,96,1536]{2,1,0:T(8,128)(2,1)} %get-tuple-element.104) | copy-start | bytes 3538948
  719.4 4.4 copy-start.5
  719.4 4.4 copy-start.12
  730.9 9.3 %copy-start.7 = (bf16[2,512,1536]{2,1,0:T(8,128)(2,1)S(1)}, bf16[2,512,1536]{2,1,0:T(8,128)(2,1)}, u32[]{:S(2)}) copy-start(bf16[2,512,1536]{2,1,0:T(8,128)(2,1)} %get-tuple-element.165) | copy-start | bytes 9437188
  740.1 3.6 copy-start.10
  740.1 4.5 copy-start.11
Sparse Core Ops, SparseCore 0:
  120.6 79.9 all-gather.1
  352.0 267.0 all-reduce.6

commit v3 on v2

v3 whole, which is shorter than its diff:
```python
import functools

import jax
import jax.numpy as jnp
from jax import lax
from jax.experimental import pallas as pl
from jax.experimental.pallas import tpu as pltpu
from jax.sharding import Mesh
from jax.sharding import PartitionSpec as P

EPS = 1e-05
HIGH = lax.Precision.HIGHEST
F32 = jnp.float32
BF16 = jnp.bfloat16
ALL = ("rep", "z", "core")
COLUMN = ("z", "core")
PLANE = ("rep", "core")
LANES = 128


def rms_rows(values):
    return lax.rsqrt(jnp.mean(values * values, axis=-1, keepdims=True) + EPS)


def mm(left, right):
    return jnp.dot(left, right, preferred_element_type=F32)


def mm_nt(left, right):
    return lax.dot_general(left, right, (((1,), (1,)), ((), ())), preferred_element_type=F32)


def mm_tn(left, right):
    return lax.dot_general(left, right, (((0,), (0,)), ((), ())), preferred_element_type=F32)


def silu_slope(values, sig):
    return sig * (1.0 + values * (1.0 - sig))


def split_two(values):
    high = values.astype(BF16)
    return high, (values - high.astype(F32)).astype(BF16)


def segments(lengths_row, sequences, rows):
    column = lax.broadcasted_iota(jnp.int32, (rows, 1), 0).astype(F32)
    line = lax.broadcasted_iota(jnp.int32, (1, rows), 1).astype(F32)
    end = jnp.zeros((1, 1), F32)
    seg_column, seg_line = jnp.zeros_like(column), jnp.zeros_like(line)
    for at in range(sequences):
        end = end + lengths_row[:, at : at + 1]
        seg_column = seg_column + jnp.where(column >= end, 1.0, 0.0)
        seg_line = seg_line + jnp.where(line >= end, 1.0, 0.0)
    return seg_column, seg_line


class Block:
    def __init__(self, proj, seg_col, seg_row, taps, heads, channels, width, state):
        rows = proj.shape[0]
        self.rows, self.channels, self.width, self.state = rows, channels, width, state
        self.gate = proj[:, :channels]
        self.xbc = proj[:, channels : 2 * channels + 2 * state]
        self.turn = lax.axis_index("core") * (LANES // 2)
        dt_raw = pltpu.roll(proj[:, 2 * channels + 2 * state :], self.turn, 1)
        position = lax.broadcasted_iota(jnp.int32, (rows, 1), 0)
        seg_wide = jnp.broadcast_to(seg_col, (rows, LANES))
        self.masks = []
        conv = taps[4:5, :] + taps[3:4, :] * self.xbc
        for offset in (1, 2, 3):
            before = pltpu.roll(seg_wide, offset, 0)[:, :1]
            mask = jnp.where((before == seg_col) & (position >= offset), 1.0, 0.0)
            self.masks.append(mask)
            conv = conv + taps[3 - offset : 4 - offset, :] * (mask * pltpu.roll(self.xbc, offset, 0))
        self.conv = conv
        self.conv_sig = jax.nn.sigmoid(conv)
        act = conv * self.conv_sig
        self.xin = act[:, :channels]
        self.write = act[:, channels : channels + state]
        self.read = act[:, channels + state :]
        shifted = dt_raw + heads[0:1, :]
        self.step = jnp.maximum(shifted, 0.0) + jnp.log1p(jnp.exp(-jnp.abs(shifted)))
        self.step_sig = jax.nn.sigmoid(shifted)
        self.speed = heads[1:2, :]
        self.rate = -self.step * self.speed
        row_at = lax.broadcasted_iota(jnp.int32, (rows, rows), 0)
        col_at = lax.broadcasted_iota(jnp.int32, (rows, rows), 1)
        self.causal = row_at >= col_at
        self.keep = self.causal & (seg_col == seg_row)
        self.cum = jnp.dot(self.causal.astype(F32), self.rate, precision=HIGH, preferred_element_type=F32)
        self.cum_t = self.cum.T
        scores = lax.dot_general(
            self.read, self.write, (((1,), (1,)), ((), ())), precision=HIGH, preferred_element_type=F32
        )
        self.scores = jnp.where(self.keep, scores, 0.0)

    def groups(self):
        for start in range(0, self.channels, LANES):
            stop = min(start + LANES, self.channels)
            yield start, stop, list(range(start // self.width, (stop - 1) // self.width + 1))

    def spread(self, columns, start, stop, heads):
        lane = lax.broadcasted_iota(jnp.int32, (self.rows, stop - start), 1) + start
        result = jnp.broadcast_to(columns[:, heads[0] : heads[0] + 1], (self.rows, stop - start))
        for head in heads[1:]:
            result = jnp.where(lane >= head * self.width, columns[:, head : head + 1], result)
        return result

    def inside(self, start, stop, head):
        lane = lax.broadcasted_iota(jnp.int32, (self.rows, stop - start), 1) + start
        return (lane >= head * self.width) & (lane < (head + 1) * self.width)

    def decay(self, head):
        gaps = self.cum[:, head : head + 1] - self.cum_t[head : head + 1, :]
        return jnp.exp(jnp.where(self.keep, gaps, 0.0))


def block_back(block, low, scale, pull, taps_ref, skip_ref, norm_ref, weight, out_weight):
    rows, channels = block.rows, block.channels
    normed_grad = mm_nt(low, out_weight)
    taps = taps_ref[...]
    gate_grads, x_grads, norm_grads, skip_grads = [], [], [], []
    step_grad = jnp.zeros((rows, LANES), F32)
    cum_grad = jnp.zeros((rows, LANES), F32)
    cum_grad_t = jnp.zeros((LANES, rows), F32)
    score_grad = jnp.zeros((rows, rows), F32)
    lane_all = lax.broadcasted_iota(jnp.int32, (rows, LANES), 1)
    sub_all = lax.broadcasted_iota(jnp.int32, (LANES, rows), 0)
    for start, stop, heads in block.groups():
        xin = block.xin[:, start:stop]
        spread = block.spread(block.step, start, stop, heads)
        scaled, scaled_rest = split_two(xin * spread)
        scaled_wide = jnp.concatenate([scaled, scaled, scaled_rest], axis=1)
        weights, decays = [], []
        y = None
        for head in heads:
            decays.append(block.decay(head))
            weights.append(block.scores * decays[-1])
            term = mm(weights[-1].astype(BF16), scaled)
            y = term if y is None else jnp.where(block.inside(start, stop, head), term, y)
        skip = skip_ref[:, start:stop]
        y = y + skip * xin
        gate = block.gate[:, start:stop]
        gate_sig = jax.nn.sigmoid(gate)
        gate_act = gate * gate_sig
        mixed = y * gate_act
        q = normed_grad[:, start:stop]
        norm_grads.append(jnp.sum(mixed * scale * q, axis=0, keepdims=True))
        mixed_grad = scale * norm_ref[:, start:stop] * q - mixed * pull
        gate_grads.append(mixed_grad * y * silu_slope(gate, gate_sig))
        y_grad = mixed_grad * gate_act
        skip_grads.append(jnp.sum(y_grad * xin, axis=0, keepdims=True))
        y_low, y_rest = split_two(y_grad)
        scaled_grad = None
        for at, head in enumerate(heads):
            inside = block.inside(start, stop, head)
            term = mm_tn(weights[at].astype(BF16), y_low)
            scaled_grad = term if scaled_grad is None else jnp.where(inside, term, scaled_grad)
            blank = jnp.zeros_like(y_low)
            y_own = jnp.where(inside, y_low, blank)
            pair_grad = mm_nt(
                jnp.concatenate([y_own, jnp.where(inside, y_rest, blank), y_own], axis=1), scaled_wide
            )
            score_grad = score_grad + pair_grad * decays[at]
            exponent_grad = pair_grad * weights[at]
            cum_grad = jnp.where(lane_all == head, jnp.sum(exponent_grad, axis=1, keepdims=True), cum_grad)
            cum_grad_t = jnp.where(sub_all == head, jnp.sum(exponent_grad, axis=0, keepdims=True), cum_grad_t)
        for head in heads:
            inside = block.inside(start, stop, head)
            per_row = jnp.sum(jnp.where(inside, scaled_grad * xin, 0.0), axis=1, keepdims=True)
            step_grad = jnp.where(lane_all == head, per_row, step_grad)
        x_grads.append(scaled_grad * spread + skip * y_grad)
    score_grad = jnp.where(block.keep, score_grad, 0.0).astype(BF16)
    read_grad = mm(score_grad, block.write.astype(BF16))
    write_grad = mm_tn(score_grad, block.read.astype(BF16))
    cum_grad = cum_grad - cum_grad_t.T
    rate_grad = lax.dot_general(
        block.causal.astype(F32), cum_grad, (((0,), (0,)), ((), ())), precision=HIGH, preferred_element_type=F32
    )
    dt_grad = (step_grad - block.speed * rate_grad) * block.step_sig
    head_rows = [jnp.sum(dt_grad, axis=0, keepdims=True), jnp.sum(rate_grad * block.rate, axis=0, keepdims=True)]
    act_grad = jnp.concatenate(x_grads + [write_grad, read_grad], axis=1)
    conv_grad = act_grad * silu_slope(block.conv, block.conv_sig)
    tap_rows = {4: jnp.sum(conv_grad, axis=0, keepdims=True), 3: jnp.sum(conv_grad * block.xbc, axis=0, keepdims=True)}
    xbc_grad = taps[3:4, :] * conv_grad
    for offset in (1, 2, 3):
        masked = conv_grad * block.masks[offset - 1]
        tap_rows[3 - offset] = jnp.sum(masked * pltpu.roll(block.xbc, offset, 0), axis=0, keepdims=True)
        xbc_grad = xbc_grad + taps[3 - offset : 4 - offset, :] * pltpu.roll(masked, rows - offset, 0)
    proj_grad = jnp.concatenate(gate_grads + [xbc_grad, pltpu.roll(dt_grad, block.turn, 1)], axis=1).astype(BF16)
    tap_grads = jnp.concatenate([tap_rows[at] for at in range(5)], axis=0)
    wide_grads = jnp.concatenate(
        [jnp.concatenate(norm_grads, axis=1), jnp.concatenate(skip_grads, axis=1)], axis=0
    )
    return proj_grad, tap_grads, head_rows, wide_grads


def whole(shape):
    return pl.BlockSpec(shape, lambda i: (0,) * len(shape))


def by_rows(shape):
    return pl.BlockSpec(shape, lambda i: (i,) + (0,) * (len(shape) - 1))


MESH_ID = pl.DeviceIdType.MESH


def when(condition, action):
    if condition is True:
        action()
    elif condition is not False:
        pl.when(condition)(action)


class Place:
    def __init__(self, reps, depth):
        self.reps, self.depth = reps, depth
        self.rep, self.z, self.core = lax.axis_index("rep"), lax.axis_index("z"), lax.axis_index("core")
        self.here = {"rep": self.rep, "z": self.z, "core": self.core}
        self.pending = []

    def device(self, **changes):
        return {**self.here, **changes}

    def sibling(self):
        return self.device(core=1 - self.core)

    def rep_at(self, distance):
        result, place = 0, 1
        while place < self.reps:
            mine, other = lax.rem(self.rep // place, 2), lax.rem(distance // place, 2)
            result = result + place * (mine + other - 2 * mine * other)
            place *= 2
        return result

    def barrier(self, plane=False, column=False, everyone=False):
        semaphore = pltpu.get_barrier_semaphore()

        def greet(device):
            pl.semaphore_signal(semaphore, inc=1, device_id=device, device_id_type=MESH_ID)

        if everyone:
            count = self.reps * self.depth * 2
            mine = (self.rep * self.depth + self.z) * 2 + self.core

            def step(distance, carry):
                other = lax.rem(mine + distance, count)
                greet({"rep": other // (2 * self.depth), "z": lax.rem(other // 2, self.depth), "core": lax.rem(other, 2)})
                return carry

            lax.fori_loop(1, count, step, 0)
            pl.semaphore_wait(semaphore, count - 1)
            return
        amount = 1
        greet(self.sibling())
        if plane:
            for distance in range(1, self.reps):
                greet(self.device(rep=self.rep_at(distance)))
            amount = amount + self.reps - 1
        if column:
            above, below = self.z < self.depth - 1, self.z > 0
            when(above, lambda: greet(self.device(z=self.z + 1)))
            when(below, lambda: greet(self.device(z=self.z - 1)))
            amount = amount + jnp.where(above, 1, 0) + jnp.where(below, 1, 0)
        pl.semaphore_wait(semaphore, amount)

    def send(self, source, target, send_sem, recv_sem, device, condition=True):
        copy = pltpu.make_async_remote_copy(
            src_ref=source, dst_ref=target, send_sem=send_sem, recv_sem=recv_sem, device_id=device,
            device_id_type=MESH_ID,
        )
        when(condition, copy.start)
        self.pending.append((condition, copy))

    def local(self, source, target, sem):
        copy = pltpu.make_async_copy(source, target, sem)
        copy.start()
        return copy

    def arrived(self, target, recv_sem, condition=True):
        copy = pltpu.make_async_remote_copy(
            src_ref=target, dst_ref=target, send_sem=recv_sem, recv_sem=recv_sem, device_id=self.sibling(),
            device_id_type=MESH_ID,
        )
        when(condition, copy.wait_recv)

    def finish(self):
        for condition, copy in self.pending:
            when(condition, copy.wait_send)
        self.pending = []


class PlaneGather:
    @staticmethod
    def scratch(reps):
        return [pltpu.SemaphoreType.DMA((4, reps)), pltpu.SemaphoreType.DMA((1,))]

    def __init__(self, place, own, out, sems, local_sem):
        self.place, self.out, self.sems = place, out, sems
        p = place
        self.keep = p.local(own, out.at[p.rep, p.core], local_sem.at[0])
        for distance in range(1, p.reps):
            p.send(own, out.at[p.rep, p.core], sems.at[0, distance], sems.at[1, distance],
                   p.device(rep=p.rep_at(distance)))
        p.send(own, out.at[p.rep, p.core], sems.at[2, 0], sems.at[3, 0], p.sibling())

    def relay(self):
        p = self.place
        for distance in range(1, p.reps):
            source = self.out.at[p.rep_at(distance), p.core]
            p.arrived(source, self.sems.at[1, distance])
            p.send(source, source, self.sems.at[2, distance], self.sems.at[3, distance], p.sibling())

    def finish(self):
        p = self.place
        self.keep.wait()
        for distance in range(p.reps):
            source = p.rep_at(distance) if distance else p.rep
            p.arrived(self.out.at[source, 1 - p.core], self.sems.at[3, distance])


class ColumnGather:
    @staticmethod
    def scratch(depth):
        return [pltpu.SemaphoreType.DMA((8, depth)), pltpu.SemaphoreType.DMA((1,))]

    def __init__(self, place, own, slot, sems, local_sem, shared=None, keep=True):
        self.place, self.slot, self.sems, self.shared = place, slot, sems, shared
        p = place
        self.keep = p.local(own, slot(p.z), local_sem.at[0]) if keep else None
        self.onward(own, slot(p.z), 0, True, True)
        if shared is not None:
            p.send(own, slot(p.z), sems.at[4, 0], sems.at[5, 0], p.sibling())

    def onward(self, source, target, distance, up, down):
        p = self.place
        if up is not False:
            p.send(source, target, self.sems.at[0, distance], self.sems.at[1, distance], p.device(z=p.z + 1),
                   (p.z < p.depth - 1) if up is True else up & (p.z < p.depth - 1))
        if down is not False:
            p.send(source, target, self.sems.at[2, distance], self.sems.at[3, distance], p.device(z=p.z - 1),
                   (p.z > 0) if down is True else down & (p.z > 0))

    def hop(self, distance):
        p = self.place
        below, above = p.z >= distance, p.z + distance < p.depth
        low, high = self.slot(jnp.maximum(p.z - distance, 0)), self.slot(jnp.minimum(p.z + distance, p.depth - 1))
        p.arrived(low, self.sems.at[1, distance - 1], below)
        self.onward(low, low, distance, below, False)
        if self.shared is not None:
            p.send(low, low, self.sems.at[4, distance], self.sems.at[5, distance], p.sibling(), below)
        p.arrived(high, self.sems.at[3, distance - 1], above)
        self.onward(high, high, distance, False, above)
        if self.shared is not None:
            p.send(high, high, self.sems.at[6, distance], self.sems.at[7, distance], p.sibling(), above)

    def finish(self):
        p = self.place
        if self.keep is not None:
            self.keep.wait()
        if self.shared is None:
            return
        p.arrived(self.shared(p.z), self.sems.at[5, 0])
        for distance in range(1, p.depth):
            below, above = p.z >= distance, p.z + distance < p.depth
            p.arrived(self.shared(jnp.maximum(p.z - distance, 0)), self.sems.at[5, distance], below)
            p.arrived(self.shared(jnp.minimum(p.z + distance, p.depth - 1)), self.sems.at[7, distance], above)


def add_up(*terms):
    total = terms[0].astype(F32)
    for term in terms[1:]:
        total = total + term.astype(F32)
    return total


class PairSwap:
    @staticmethod
    def scratch(count, shape, dtype):
        return [pltpu.VMEM((count,) + shape, dtype), pltpu.SemaphoreType.DMA((2, count))]

    def __init__(self, place, parts, pair, sems, order, own=None):
        self.place, self.parts, self.pair, self.sems, self.own = place, parts, pair, sems, own
        for at in order:
            place.send(parts.at[at, 1 - place.core], pair.at[at], sems.at[0, at], sems.at[1, at], place.sibling())

    def wait(self, at):
        self.place.arrived(self.pair.at[at], self.sems.at[1, at])

    def terms(self, at):
        if self.own is None:
            return [self.parts[at, self.place.core], self.pair[at]]
        slot, sem = self.own
        self.place.local(self.parts.at[at, self.place.core], slot, sem.at[0]).wait()
        return [slot[...], self.pair[at]]


class PlaneSum:
    @staticmethod
    def scratch(reps, shape, dtype):
        return PairSwap.scratch(reps, shape, dtype) + [
            pltpu.VMEM((reps,) + shape, dtype), pltpu.SemaphoreType.DMA((2, reps)),
        ]

    def __init__(self, place, parts, pair, pair_sems, into, sems):
        self.place, self.pair, self.into, self.sems = place, pair, into, sems
        order = [place.rep_at(distance) for distance in range(1, place.reps)] + [place.rep]
        self.swap = PairSwap(place, parts, pair, pair_sems, order)

    def relay(self):
        p = self.place
        for distance in range(1, p.reps):
            rep = p.rep_at(distance)
            self.swap.wait(rep)
            self.pair[rep] = add_up(*self.swap.terms(rep)).astype(self.pair.dtype)
            p.send(self.pair.at[rep], self.into.at[distance], self.sems.at[0, distance], self.sems.at[1, distance],
                   p.device(rep=rep))

    def total(self):
        p = self.place
        self.swap.wait(p.rep)
        terms = self.swap.terms(p.rep)
        for distance in range(1, p.reps):
            p.arrived(self.into.at[distance], self.sems.at[1, distance])
            terms.append(self.into[distance])
        return add_up(*terms)


class LineSum:
    @staticmethod
    def scratch(depth, shape, dtype):
        return [pltpu.VMEM((depth + 1,) + shape, dtype), pltpu.SemaphoreType.DMA((4, depth))]

    def __init__(self, place, terms, out, into, sems):
        self.place, self.terms, self.out, self.into, self.sems = place, terms, out, into, sems

    def moves(self, at):
        p = self.place
        last = p.depth - 1
        for way, towards, goal, first, valid in (
            (0, p.z + 1, last - (at - p.z), p.z == 0, (at >= p.z) & (last - (at - p.z) > p.z)),
            (1, p.z - 1, at - (last - p.z), p.z == last, (at >= last - p.z) & (at - (last - p.z) < p.z)),
        ):
            goal = jnp.clip(goal, 0, last)
            slot = jnp.where(goal == towards, p.depth, goal) if way else goal
            copy = pltpu.make_async_remote_copy(
                src_ref=self.out.at[goal], dst_ref=self.into.at[slot], send_sem=self.sems.at[2 * way, goal],
                recv_sem=self.sems.at[2 * way + 1, goal], device_id=p.device(z=towards), device_id_type=MESH_ID,
            )
            yield way, goal, first, valid, copy

    def step(self, at):
        p = self.place
        for way, goal, first, valid, copy in self.moves(at):
            inner = valid & jnp.logical_not(first)
            p.arrived(self.into.at[goal], self.sems.at[2 * way + 1, goal], inner)

            def start(goal=goal):
                self.out[goal] = add_up(*self.terms(goal)).astype(self.out.dtype)

            def follow(goal=goal):
                self.out[goal] = add_up(*self.terms(goal), self.into[goal]).astype(self.out.dtype)

            when(valid & first, start)
            when(inner, follow)
            when(valid, copy.start)

    def finish(self):
        for at in range(self.place.depth - 1):
            for _, _, _, valid, copy in self.moves(at):
                when(valid, copy.wait_send)

    def total(self, result):
        result[...] = add_up(*self.terms(self.place.z))
        self.gather(result)
        self.finish()

    def gather(self, result):
        p = self.place
        for way, slot, condition in ((0, p.z, p.z > 0), (1, p.depth, p.z < p.depth - 1)):
            p.arrived(self.into.at[slot], self.sems.at[2 * way + 1, p.z], condition)

            def add(slot=slot):
                result[...] += self.into[slot].astype(F32)

            when(condition, add)


class ColumnSum:
    @staticmethod
    def scratch(depth, shape, dtype):
        return PairSwap.scratch(depth, shape, dtype) + LineSum.scratch(depth, shape, dtype)

    def __init__(self, place, parts, pair, pair_sems, into, sems, own=None):
        self.place = place
        order = [lax.rem(place.z + distance, place.depth) for distance in list(range(place.depth - 1, 0, -1)) + [0]]
        self.order = order
        self.swap = PairSwap(place, parts, pair, pair_sems, order, own)
        self.line = LineSum(place, self.swap.terms, pair, into, sems)

    def ready(self):
        for at in self.order:
            self.swap.wait(at)

    def step(self, at):
        self.line.step(at)

    def total(self, result):
        self.line.total(result)


def anywhere(count):
    return [pl.BlockSpec(memory_space=pl.ANY)] * count


def in_vmem(count):
    return [pl.BlockSpec(memory_space=pltpu.VMEM)] * count


def remote_params(identity, mebibytes=60):
    return pltpu.CompilerParams(
        collective_id=identity, has_side_effects=True, vmem_limit_bytes=mebibytes * 2**20
    )


def column_of(row_values, rows):
    return jnp.broadcast_to(row_values, (LANES, rows)).T[:, 0:1]


def row_of(column_values, rows):
    return jnp.broadcast_to(column_values, (rows, LANES)).T[0:8, :]


def forward_mixer(tokens, cotangent, own_pair, other_pair, common, vectors, table, out_quarters, sizes):
    reps, depth, channels, width, state, sequences, inner, convolved = sizes
    rows, model = tokens.shape
    part, side = own_pair.shape
    wide = side + common.shape[1]
    quarter = out_quarters.shape[1]
    vector_width = vectors.shape[1]
    heads = channels // width
    per_shard = convolved // (2 * depth)

    x_scratch = [pltpu.VMEM((reps, 2, rows, model), BF16)] + PlaneGather.scratch(reps)
    w_scratch = [pltpu.VMEM((depth, 2, part, wide), BF16)] + ColumnGather.scratch(depth) * 3
    v_scratch = [pltpu.VMEM((depth, 2) + vectors.shape, BF16)] + ColumnGather.scratch(depth) * 2
    o_scratch = [
        pltpu.VMEM((depth, quarter, model), BF16), pltpu.VMEM((reps, quarter, model), BF16),
    ] + ColumnGather.scratch(depth) + [pltpu.SemaphoreType.DMA((2, reps)), pltpu.SemaphoreType.DMA((2,))]
    n_scratch = [pltpu.VMEM((8, LANES), F32)] + PlaneGather.scratch(reps)
    sum_scratch = [
        pltpu.VMEM((reps, rows, model), BF16), pltpu.VMEM((reps, 2, 8, rows), F32),
    ] + PlaneSum.scratch(reps, (rows, model), BF16) + PlaneSum.scratch(reps, (8, rows), F32)
    groups = [x_scratch, w_scratch, v_scratch, o_scratch, n_scratch, sum_scratch]

    def kernel(x_ref, g_ref, own_ref, other_ref, common_ref, vectors_ref, table_ref, quarters_ref,
               after_ref, mixed_ref, scale_ref, lengths_ref, in_gain_ref, post_gain_ref, taps_ref, heads_ref, skip_ref,
               norm_ref, table_out, second_out, g_out, first_out, weight_out, out_out, proj_out, mixed_out, *scratch):
        cut = [0]
        for group in groups:
            cut.append(cut[-1] + len(group))
        x_work, w_work, v_work, o_work, n_work, sum_work = [scratch[i:j] for i, j in zip(cut, cut[1:])]
        (second, second_sems, second_local, g_sems, g_local, proj_buffer, proj_sems, keep_sems,
         own_part, mixed_buffer, mixed_sems) = scratch[cut[-1]:]
        p = Place(reps, depth)
        p.barrier(plane=True, column=True)

        x_all, weight_all, vectors_all = x_work[0], w_work[0], v_work[0]

        def left(core):
            return lambda z: weight_all.at[z, core, :, pl.ds(0, side)]

        def right(core):
            return lambda z: weight_all.at[z, core, :, pl.ds(side, wide - side)]

        vector_job = ColumnGather(p, vectors_ref, lambda z: vectors_all.at[z, p.core], v_work[1], v_work[2],
                                  shared=lambda z: vectors_all.at[z, 1 - p.core])
        own_slot, other_slot = left(p.core), left(1 - p.core)
        p.send(other_ref, own_slot(p.z), keep_sems.at[0], keep_sems.at[1], p.sibling())
        job_a = ColumnGather(p, own_ref, own_slot, w_work[1], w_work[2])
        job_c = ColumnGather(p, common_ref, right(p.core), w_work[3], w_work[4], shared=right(1 - p.core))
        x_job = PlaneGather(p, x_ref, x_all, x_work[1], x_work[2])
        p.arrived(other_slot(p.z), keep_sems.at[1])
        job_b = ColumnGather(p, other_slot(p.z), other_slot, w_work[5], w_work[6], keep=False)
        mid, out_all = o_work[0], o_work[1]
        job_o = ColumnGather(p, quarters_ref.at[p.rep], lambda z: mid.at[z], o_work[2], o_work[3])
        table_job = ColumnGather(p, table_ref, lambda z: table_out.at[z, p.core], v_work[3], v_work[4],
                                 shared=lambda z: table_out.at[z, 1 - p.core])
        for distance in range(1, depth):
            vector_job.hop(distance)
        vector_job.finish()

        own_row = vectors_all[p.z, p.core].astype(F32)[11:12, :LANES]
        dealt = own_row[:, sequences : sequences + 1]
        lengths_row = jnp.zeros((1, LANES), F32)
        for z in range(depth):
            for core in range(2):
                row = vectors_all[z, core].astype(F32)[11:12, :LANES]
                lengths_row = jnp.where(dealt == float(2 * z + core), row, lengths_row)
        n_work[0][...] = jnp.broadcast_to(lengths_row, (8, LANES))
        n_job = PlaneGather(p, n_work[0], lengths_ref, n_work[1], n_work[2])

        pieces = [vectors_all[z, core].astype(F32) for z in range(depth) for core in range(2)]
        in_gain_ref[...] = jnp.concatenate([piece[0:1, :part] for piece in pieces], axis=1)
        post_gain_ref[...] = jnp.concatenate([piece[10:11, :part] for piece in pieces], axis=1)
        taps_full = jnp.concatenate([piece[0:8, :per_shard] for piece in pieces], axis=1)
        taps_full = jnp.concatenate([taps_full[1:6, :], jnp.zeros((3, convolved), F32)], axis=0)
        team = 2 * p.rep + p.core
        taps_own = taps_full[:, :channels]
        for member in range(1, 2 * reps):
            taps_own = jnp.where(team == member, taps_full[:, channels * member : channels * (member + 1)], taps_own)
        taps_ref[...] = jnp.concatenate([taps_own, taps_full[:, inner:]], axis=1)
        own = vectors_all[p.rep, p.core].astype(F32)
        lane = lax.broadcasted_iota(jnp.int32, (1, LANES), 1)
        speed = jnp.where(lane < heads, jnp.exp(jnp.where(lane < heads, own[7:8, :LANES], 0.0)), 0.0)
        heads_ref[...] = jnp.concatenate([own[6:7, :LANES], speed, jnp.zeros((6, LANES), F32)], axis=0)
        norm_ref[...] = own[9:10, :channels]
        wide_lane = lax.broadcasted_iota(jnp.int32, (1, channels), 1)
        skip = jnp.broadcast_to(own[8:9, 0:1], (1, channels))
        for head in range(1, heads):
            skip = jnp.where(wide_lane >= head * width, own[8:9, head : head + 1], skip)
        skip_ref[...] = skip

        n_job.relay()
        for distance in range(1, depth):
            for job in (job_a, job_c, job_b, job_o, table_job):
                job.hop(distance)
            if distance == 1:
                x_job.relay()
        for job in (n_job, x_job, job_a, job_b, job_c, job_o, table_job):
            job.finish()
        e_sems, e_local = o_work[4], o_work[5]
        for distance in range(1, reps):
            rep = p.rep_at(distance)
            p.send(mid.at[rep], out_all.at[p.rep], e_sems.at[0, distance], e_sems.at[1, distance], p.device(rep=rep))
        out_all[p.rep] = mid[p.rep]
        g_job = ColumnGather(p, g_ref, lambda z: g_out.at[z, p.core], g_sems, g_local,
                             shared=lambda z: g_out.at[z, 1 - p.core])
        for distance in range(1, reps):
            p.arrived(out_all.at[p.rep_at(distance)], e_sems.at[1, distance])
        weight_keep = p.local(weight_all, weight_out, e_local.at[0])
        out_keep = p.local(out_all, out_out, e_local.at[1])

        p.finish()
        parts, squares = sum_work[0], sum_work[1]
        pair, pair_sems, into, into_sems = sum_work[2:6]
        s_pair, s_pair_sems, s_into, s_into_sems = sum_work[6:10]

        def swap(rep, start):
            for source, target, sems in (
                (parts.at[rep], pair, pair_sems), (squares.at[rep, 1 - p.core], s_pair, s_pair_sems)
            ):
                copy = pltpu.make_async_remote_copy(
                    src_ref=source, dst_ref=target.at[rep], send_sem=sems.at[0, rep],
                    recv_sem=sems.at[1, rep], device_id=p.sibling(), device_id_type=MESH_ID,
                )
                if start:
                    copy.start()
                else:
                    copy.wait_send()

        def onward(distance, rep, start):
            for values, target, sems in ((pair, into, into_sems), (s_pair, s_into, s_into_sems)):
                copy = pltpu.make_async_remote_copy(
                    src_ref=values.at[rep], dst_ref=target.at[distance], send_sem=sems.at[0, distance],
                    recv_sem=sems.at[1, distance], device_id=p.device(rep=rep), device_id_type=MESH_ID,
                )
                if start:
                    copy.start()
                else:
                    copy.wait_send()

        def proj_copy(slot, rep, core):
            return pltpu.make_async_copy(proj_buffer.at[slot], proj_out.at[rep, core], proj_sems.at[slot])

        def mixed_copy(slot, rep, core):
            return pltpu.make_async_copy(mixed_buffer.at[slot], mixed_out.at[rep, core], mixed_sems.at[slot])

        def visit(at, carry):
            distance = lax.rem(at // 2 + 1, reps)
            rep = p.rep_at(distance)
            turn = lax.rem(at, 2)
            core = jnp.where(turn == 0, 1 - p.core, p.core)
            x = x_all[rep, core].astype(F32)
            first = (x * rms_rows(x) * in_gain_ref[...]).astype(BF16)
            x_all[rep, core] = first
            proj = mm(first, weight_all[...].reshape(model, wide))

            @pl.when(at >= 2)
            def _():
                proj_copy(turn, rep, core).wait()

            proj_buffer[turn] = proj
            proj_copy(turn, rep, core).start()
            seg_column, seg_line = segments(lengths_ref[rep, core][0:1, :], sequences, rows)
            block = Block(proj, seg_column, seg_line, taps_ref[...], heads_ref[...], channels, width, state)
            mixed = []
            for start, stop, inside in block.groups():
                xin = block.xin[:, start:stop]
                scaled, rest = split_two(xin * block.spread(block.step, start, stop, inside))
                scaled = jnp.concatenate([scaled, scaled, rest], axis=0)
                y = None
                for head in inside:
                    weights, weights_rest = split_two(block.scores * block.decay(head))
                    term = mm(jnp.concatenate([weights, weights_rest, weights], axis=1), scaled)
                    y = term if y is None else jnp.where(block.inside(start, stop, head), term, y)
                gate = block.gate[:, start:stop]
                mixed.append((y + skip_ref[:, start:stop] * xin) * gate * jax.nn.sigmoid(gate))
            mixed = jnp.concatenate(mixed, axis=1)
            squares[rep, core] = row_of(jnp.sum(mixed * mixed, axis=1, keepdims=True), rows)
            mixed = mixed * norm_ref[...]

            @pl.when(at >= 2)
            def _():
                mixed_copy(turn, rep, core).wait()

            mixed_buffer[turn] = mixed
            mixed_copy(turn, rep, core).start()
            mixed, mixed_rest = split_two(mixed)
            out_weight = out_all[...].reshape(channels, model)
            part_rows = mm(mixed, out_weight) + mm(mixed_rest, out_weight)

            @pl.when(turn == 0)
            def _():
                parts[rep] = part_rows.astype(BF16)
                swap(rep, True)

            @pl.when((turn == 1) & (distance == 0))
            def _():
                own_part[...] = part_rows

            @pl.when((turn == 1) & (distance > 0))
            def _():
                p.arrived(pair.at[rep], pair_sems.at[1, rep])
                pair[rep] = add_up(part_rows, pair[rep]).astype(BF16)
                p.arrived(s_pair.at[rep], s_pair_sems.at[1, rep])
                s_pair[rep] = add_up(squares[rep, p.core], s_pair[rep])
                onward(distance, rep, True)

            return carry

        lax.fori_loop(0, reps, visit, 0)
        g_job.hop(1)
        lax.fori_loop(reps, 2 * reps, visit, 0)
        first_keep = p.local(x_all, first_out, keep_sems.at[2])
        if depth > 2:
            g_job.hop(2)
        p.arrived(pair.at[p.rep], pair_sems.at[1, p.rep])
        p.arrived(s_pair.at[p.rep], s_pair_sems.at[1, p.rep])
        terms, square_terms = [own_part[...], pair[p.rep]], [squares[p.rep, p.core], s_pair[p.rep]]
        for distance in range(1, reps):
            p.arrived(s_into.at[distance], s_into_sems.at[1, distance])
            square_terms.append(s_into[distance])
            p.arrived(into.at[distance], into_sems.at[1, distance])
            terms.append(into[distance])
        scale_row = lax.rsqrt(add_up(*square_terms) / inner + EPS)
        scale_ref[...] = scale_row
        mixed = column_of(scale_row[0:1, :], rows) * add_up(*terms)
        mixed_ref[...] = mixed.astype(BF16)
        after = x_ref[...].astype(F32) + mixed
        after_ref[...] = after
        second[...] = (after * rms_rows(after) * post_gain_ref[...]).astype(BF16)
        job = ColumnGather(p, second, lambda z: second_out.at[z, p.core], second_sems, second_local,
                           shared=lambda z: second_out.at[z, 1 - p.core])
        for distance in range(3, depth):
            g_job.hop(distance)
        for distance in range(1, depth):
            job.hop(distance)
        job.finish()
        g_job.finish()
        for distance in range(reps):
            rep = p.rep_at(distance) if distance else p.rep
            swap(rep, False)
            if distance:
                onward(distance, rep, False)
        for slot in range(2):
            proj_copy(slot, p.rep, p.core).wait()
            mixed_copy(slot, p.rep, p.core).wait()
        for keep in (weight_keep, out_keep, first_keep):
            keep.wait()
        p.finish()

    return pl.pallas_call(
        kernel,
        in_specs=in_vmem(1) + anywhere(7),
        out_specs=in_vmem(10) + anywhere(8),
        out_shape=[
            jax.ShapeDtypeStruct((rows, model), F32),
            jax.ShapeDtypeStruct((rows, model), BF16),
            jax.ShapeDtypeStruct((8, rows), F32),
            jax.ShapeDtypeStruct((reps, 2, 8, LANES), F32),
            jax.ShapeDtypeStruct((1, model), F32),
            jax.ShapeDtypeStruct((1, model), F32),
            jax.ShapeDtypeStruct((8, channels + 2 * state), F32),
            jax.ShapeDtypeStruct((8, LANES), F32),
            jax.ShapeDtypeStruct((1, channels), F32),
            jax.ShapeDtypeStruct((1, channels), F32),
            jax.ShapeDtypeStruct((depth, 2) + table.shape, BF16),
            jax.ShapeDtypeStruct((depth, 2, rows, model), BF16),
            jax.ShapeDtypeStruct((depth, 2, rows, model), BF16),
            jax.ShapeDtypeStruct((reps, 2, rows, model), BF16),
            jax.ShapeDtypeStruct((depth, 2, part, wide), BF16),
            jax.ShapeDtypeStruct((reps, quarter, model), BF16),
            jax.ShapeDtypeStruct((reps, 2, rows, wide), F32),
            jax.ShapeDtypeStruct((reps, 2, rows, channels), F32),
        ],
        scratch_shapes=[item for group in groups for item in group]
        + [pltpu.VMEM((rows, model), BF16)]
        + ColumnGather.scratch(depth) * 2
        + [pltpu.VMEM((2, rows, wide), F32), pltpu.SemaphoreType.DMA((2,)), pltpu.SemaphoreType.DMA((3,)),
           pltpu.VMEM((rows, model), F32), pltpu.VMEM((2, rows, channels), F32), pltpu.SemaphoreType.DMA((2,))],
        compiler_params=remote_params(0),
        name="forward_mixer",
    )(tokens, cotangent, own_pair, other_pair, common, vectors, table, out_quarters)


def join_experts(
    own, gates, dots, hidden, shared_grad, router_t, shared_in, shared_out, cotangent, after, mixed, scale, post_gain,
    back, weighted, second, inner, reps, depth, capacity,
):
    rows, model = cotangent.shape
    local = own.shape[1]
    experts = gates.shape[1]
    half_rows = rows // 2
    stack = (rows, model)
    halves = (slice(0, half_rows), slice(half_rows, rows))
    groups = {
        "stream": [
            pltpu.VMEM((2, local, capacity, model), BF16), pltpu.SemaphoreType.DMA((2,)),
            pltpu.VMEM((2,) + stack, BF16), pltpu.SemaphoreType.DMA((2,)),
        ],
        "parts": [
            pltpu.VMEM((2,) + stack, BF16), pltpu.VMEM(stack, F32), pltpu.VMEM((depth, 2, half_rows, model), BF16),
            pltpu.SemaphoreType.DMA((2, depth)),
        ],
        "line": LineSum.scratch(depth, (half_rows, model), BF16) * 2,
        "low": [pltpu.VMEM((2, half_rows, model), BF16), pltpu.VMEM((2, 8, rows), F32)] + PlaneGather.scratch(reps) * 3,
        "logits": [pltpu.VMEM((2 * depth, 2 * experts, rows), BF16), pltpu.VMEM((2,) + stack, BF16),
                   pltpu.SemaphoreType.DMA((2,))],
    }

    def kernel(own_ref, gates_ref, dots_ref, hidden_ref, shared_ref, router_ref, in_ref, out_ref, g_ref, after_ref,
               mixed_ref, scale_ref, gain_ref, back_ref, weighted_ref, second_ref,
               grad_ref, gain_grad_ref, router_grad_ref, layer_out, low_out, scale_out, *scratch):
        work, cut = {}, 0
        for name, items in groups.items():
            work[name] = scratch[cut : cut + len(items)]
            cut += len(items)
        p = Place(reps, depth)
        slots, slot_sems, second_slots, second_sems = work["stream"]
        parts, own_part, pair, pair_sems = work["parts"]
        logits_all, layer_slots, layer_sems = work["logits"]
        lower = p.z < depth // 2

        def goal_at(index):
            distance = lax.rem(depth - 1 - index + depth, depth)
            return jnp.where(lower, lax.rem(p.z + distance, depth), lax.rem(p.z - distance + depth, depth))

        def block_at(at):
            return goal_at(at // 2), jnp.where(lax.rem(at, 2) == 0, 1 - p.core, p.core)

        def load(source, at):
            goal, core = block_at(at)
            start = pl.multiple_of((2 * goal + core) * capacity, capacity)
            return pltpu.make_async_copy(
                source.at[:, pl.ds(start, capacity)], slots.at[lax.rem(at, 2)], slot_sems.at[lax.rem(at, 2)]
            )

        def swap(goal, slot, start):
            for at, piece in enumerate(halves):
                copy = pltpu.make_async_remote_copy(
                    src_ref=parts.at[slot, pl.ds(half_rows * at, half_rows)], dst_ref=pair.at[goal, at],
                    send_sem=pair_sems.at[0, goal] if at == 0 else pair_sems_late.at[0, goal],
                    recv_sem=pair_sems.at[1, goal] if at == 0 else pair_sems_late.at[1, goal],
                    device_id=p.sibling(), device_id_type=MESH_ID,
                )
                copy.start() if start else copy.wait_send()

        pair_sems_late = work["late"][0]
        load(back_ref, 0).start()
        p.barrier(plane=True, column=True)
        expert = lax.broadcasted_iota(jnp.int32, (experts, rows), 0)
        shard = 2 * p.z + p.core

        def matches(q):
            table = own_ref[q].astype(F32)
            return [slot_match(table[i : i + 1, :], capacity, rows) for i in range(local)]

        def visit(at, carry):
            goal, core = block_at(at)
            q = 2 * goal + core
            turn = lax.rem(at, 2)
            load(back_ref, at).wait()

            @pl.when(at + 1 < 2 * depth)
            def _():
                load(back_ref, at + 1).start()

            start = pl.multiple_of(q * rows, rows)
            gates = gates_ref[q]
            gate_grad = jnp.zeros_like(gates)
            total = mm_nt(shared_ref[pl.ds(start, rows), :], in_ref[...])
            for i, match in enumerate(matches(q)):
                total = total + mm_tn(match.astype(BF16), slots[turn, i])
                dot = dots_ref[i, pl.ds(pl.multiple_of(q * capacity, capacity), capacity), 0:1]
                row = jnp.sum(jnp.where(match, dot, 0.0), axis=0, keepdims=True)
                gate_grad = jnp.where(expert == local * shard + i, row, gate_grad)
            logit_grad = gates * (gate_grad - jnp.sum(gates * gate_grad, axis=0, keepdims=True))
            logit_pair = jnp.concatenate(split_two(logit_grad), axis=0)
            logits_all[q] = logit_pair
            total = total + mm_tn(logit_pair, jnp.concatenate([router_ref[...], router_ref[...]], axis=0))

            @pl.when(turn == 0)
            def _():
                slot = lax.rem(at // 2, 2)

                @pl.when(at >= 4)
                def _():
                    swap(goal_at(at // 2 - 2), slot, False)

                parts[slot] = total.astype(BF16)
                swap(goal, slot, True)

            @pl.when(turn == 1)
            def _():
                p.arrived(pair.at[goal, 0], pair_sems.at[1, goal])
                p.arrived(pair.at[goal, 1], pair_sems_late.at[1, goal])

                @pl.when(goal == p.z)
                def _():
                    for index, piece in enumerate(halves):
                        own_part[piece, :] = add_up(total[piece, :], pair[goal, index])

                @pl.when(goal != p.z)
                def _():
                    for index, piece in enumerate(halves):
                        pair[goal, index] = add_up(total[piece, :], pair[goal, index]).astype(BF16)

            return carry

        lines = []
        for index in range(2):
            view = pair.at[:, index]
            into, sems = work["line"][2 * index : 2 * index + 2]

            def terms(goal, view=view, index=index):
                return [view[goal]]

            lines.append(LineSum(p, terms, view, into, sems))

        for step in range(depth - 1):
            lax.fori_loop(2 * step, 2 * step + 2, visit, 0)
            lines[0].step(step)
        for step in range(depth - 1):
            lines[1].step(step)
        lax.fori_loop(2 * depth - 2, 2 * depth, visit, 0)

        low, scales = work["low"][:2]
        gather_sems = work["low"][2:]
        gain_grad_ref[...] = jnp.zeros_like(gain_grad_ref)
        row_dots = []

        def norm_back(index):
            piece = halves[index]
            into = lines[index].into
            grad_ref[piece, :] = own_part[piece, :]
            lines[index].gather(grad_ref.at[pl.ds(half_rows * index, half_rows)])
            second_grad = grad_ref[piece, :]
            after_rows = after_ref[piece, :]
            after_scale = rms_rows(after_rows)
            gain_grad_ref[...] += jnp.sum(after_rows * second_grad * after_scale, axis=0, keepdims=True)
            weighted = second_grad * gain_ref[...]
            after_grad = (
                g_ref[piece, :].astype(F32)
                + after_scale * weighted
                - after_rows * after_scale**3 * jnp.mean(after_rows * weighted, axis=1, keepdims=True)
            )
            grad_ref[piece, :] = after_grad
            after_low = after_grad.astype(BF16)
            low[index] = after_low
            row_dots.append(
                jnp.sum(after_low.astype(F32) * mixed_ref[piece, :].astype(F32), axis=1, keepdims=True)
            )
            return PlaneGather(p, low.at[index], low_out.at[:, :, pl.ds(half_rows * index, half_rows)],
                               *gather_sems[2 * index : 2 * index + 2])

        first_job = norm_back(0)

        def layer_load(at):
            q = block_at(at)
            start = pl.multiple_of((2 * q[0] + q[1]) * rows, rows)
            return pltpu.make_async_copy(
                second_ref.at[pl.ds(start, rows)], second_slots.at[lax.rem(at, 2)], second_sems.at[lax.rem(at, 2)]
            )

        def layer_store(at):
            goal, core = block_at(at)
            return pltpu.make_async_copy(
                layer_slots.at[lax.rem(at, 2)], layer_out.at[goal, core], layer_sems.at[lax.rem(at, 2)]
            )

        def layer_visit(at, carry):
            goal, core = block_at(at)
            q = 2 * goal + core
            turn = lax.rem(at, 2)
            load(weighted_ref, at).wait()
            layer_load(at).wait()

            @pl.when(at + 1 < 2 * depth)
            def _():
                load(weighted_ref, at + 1).start()
                layer_load(at + 1).start()

            total = mm(hidden_ref[pl.ds(pl.multiple_of(q * rows, rows), rows), :], out_ref[...])
            for i, match in enumerate(matches(q)):
                total = total + mm_tn(match.astype(BF16), slots[turn, i])

            @pl.when(at >= 2)
            def _():
                layer_store(at).wait()

            layer_slots[turn] = total.astype(BF16)
            layer_store(at).start()
            both = mm(logits_all[q], second_slots[turn])
            router_grad_ref[...] += both[:experts, :] + both[experts:, :]
            return carry

        router_grad_ref[...] = jnp.zeros_like(router_grad_ref)
        load(weighted_ref, 0).start()
        layer_load(0).start()
        lax.fori_loop(0, depth, layer_visit, 0)
        first_job.relay()
        second_job = norm_back(1)
        dot_row = row_of(jnp.concatenate(row_dots, axis=0), rows)
        scale_row = scale_ref[...]
        scales[0] = scale_row
        scales[1] = scale_row**2 * dot_row / inner
        scale_job = PlaneGather(p, scales, scale_out, *gather_sems[4:6])
        lax.fori_loop(depth, 2 * depth, layer_visit, 0)
        scale_job.relay()
        second_job.relay()
        for job in (first_job, scale_job, second_job):
            job.finish()
        for slot in range(2):
            layer_store(slot).wait()
        for at in range(max(depth - 2, 0), depth):
            swap(goal_at(at), at % 2, False)
        for line in lines:
            line.finish()
        p.finish()

    groups["late"] = [pltpu.SemaphoreType.DMA((2, depth))]
    group = 2 * depth
    return pl.pallas_call(
        kernel,
        in_specs=in_vmem(13) + anywhere(3),
        out_specs=in_vmem(3) + anywhere(3),
        out_shape=[
            jax.ShapeDtypeStruct((rows, model), F32),
            jax.ShapeDtypeStruct((1, model), F32),
            jax.ShapeDtypeStruct((experts, model), F32),
            jax.ShapeDtypeStruct((depth, 2, rows, model), BF16),
            jax.ShapeDtypeStruct((reps, 2, rows, model), BF16),
            jax.ShapeDtypeStruct((reps, 2, 2, 8, rows), F32),
        ],
        scratch_shapes=[item for items in groups.values() for item in items],
        compiler_params=remote_params(2),
        name="join_experts",
    )(
        own, gates, dots, hidden, shared_grad, router_t, shared_in, shared_out, cotangent, after, mixed, scale,
        post_gain, back, weighted, second,
    )


def backward_mixer(
    scales, after, after_grad, tokens, in_gain, post_grad, router_parts, lengths, taps, head_rows, skip, norm, weight,
    out_weight, low, layer_parts, first, proj, gained, sizes,
):
    reps, depth, channels, width, state, sequences, inner, convolved = sizes
    rows, model = tokens.shape
    part = model // (2 * depth)
    wide = weight.shape[1]
    side = 2 * channels
    heads = channels // width
    per_shard = convolved // (2 * depth)
    quarter = channels // reps
    experts, router_width = router_parts.shape[2:]
    small_width = -(-max(per_shard, channels, router_width) // LANES) * LANES
    small_shape = (16 + experts, small_width)
    stack = (rows, model)
    groups = {
        "early": [pltpu.VMEM((2, rows, channels), F32), pltpu.SemaphoreType.DMA((2,))],
        "layer": [pltpu.SemaphoreType.DMA((1,))]
        + ColumnSum.scratch(depth, stack, BF16),
        "stream": [
            pltpu.VMEM(stack, BF16), pltpu.VMEM((2, rows, wide), F32), pltpu.VMEM((2,) + stack, BF16),
            pltpu.SemaphoreType.DMA((3, 2)),
        ],
        "sum": [
            pltpu.VMEM((2,) + stack, BF16), pltpu.VMEM(stack, F32),
            pltpu.VMEM((reps,) + stack, BF16), pltpu.SemaphoreType.DMA((2, reps)),
            pltpu.VMEM((reps - 1,) + stack, BF16), pltpu.SemaphoreType.DMA((2, reps)),
        ],
        "grads": [
            pltpu.VMEM((depth, 2, part, wide), F32), pltpu.VMEM((channels, model), F32),
            pltpu.VMEM((8, channels + 2 * state), F32), pltpu.VMEM((8, LANES), F32), pltpu.VMEM((8, channels), F32),
        ],
        "side": LineSum.scratch(depth, (2, part, channels), BF16) * 2
        + [pltpu.VMEM((2, 2, part, channels), BF16), pltpu.VMEM((2, part, channels), BF16),
           pltpu.SemaphoreType.DMA((2, 2))],
        "common": [pltpu.VMEM((depth, 2, part, wide - side), BF16)]
        + ColumnSum.scratch(depth, (part, wide - side), BF16)
        + [pltpu.VMEM((part, wide - side), F32), pltpu.VMEM((part, wide - side), BF16)],
        "out": [
            pltpu.VMEM((reps, quarter, model), BF16), pltpu.VMEM((reps, quarter, model), BF16),
            pltpu.SemaphoreType.DMA((2, reps)),
        ] + LineSum.scratch(depth, (quarter, model), BF16)
        + [pltpu.VMEM((quarter, model), BF16)],
        "small": [pltpu.VMEM((depth, 2) + small_shape, F32)] + ColumnSum.scratch(depth, small_shape, F32)
        + [pltpu.VMEM(small_shape, F32), pltpu.VMEM((reps,) + small_shape, F32)],
        "end": [pltpu.SemaphoreType.DMA((2, 5, reps)), pltpu.SemaphoreType.DMA((6,)), pltpu.VMEM((2, 32, model), F32)],
    }

    def kernel(scales_ref, after_ref, grad_ref, x_ref, gain_ref, post_grad_ref, router_ref, lengths_ref, taps_ref,
               heads_ref, skip_ref, norm_ref, weight_ref, out_ref, low_ref, layer_ref, first_ref, proj_ref, gained_ref,
               layer_out_ref, tokens_grad_ref, side_out, common_out, out_out, small_out, *scratch):
        work, cut = {}, 0
        for name, items in groups.items():
            work[name] = scratch[cut : cut + len(items)]
            cut += len(items)
        p = Place(reps, depth)
        first_slot, proj_slots, low_slots, stream_sems = work["stream"]
        gained_slots, gained_sems = work["early"]

        def first_load(rep, core):
            return pltpu.make_async_copy(first_ref.at[rep, core], first_slot, stream_sems.at[0, 0])

        def proj_load(slot, rep, core):
            return pltpu.make_async_copy(proj_ref.at[rep, core], proj_slots.at[slot], stream_sems.at[1, slot])

        def low_load(slot, rep, core):
            return pltpu.make_async_copy(low_ref.at[rep, core], low_slots.at[slot], stream_sems.at[2, slot])

        def gained_load(slot, rep, core):
            return pltpu.make_async_copy(gained_ref.at[rep, core], gained_slots.at[slot], gained_sems.at[slot])

        def early_place(at):
            return at // 2, lax.rem(at, 2)

        for at in range(2):
            gained_load(at, *early_place(at)).start()
            low_load(at, *early_place(at)).start()
        proj_load(0, p.rep_at(1), 1 - p.core).start()
        proj_load(1, p.rep_at(1), p.core).start()
        p.barrier(plane=True, column=True)
        layer_job = ColumnSum(p, layer_ref, *work["layer"][1:], own=(first_slot, work["layer"][0]))
        in_total, out_total, taps_total, heads_total, wide_total = work["grads"]
        for total in work["grads"]:
            total[...] = jnp.zeros_like(total)

        def early(at, carry):
            rep, core = early_place(at)
            turn = lax.rem(at, 2)
            gained_load(turn, rep, core).wait()
            low_load(turn, rep, core).wait()
            scale = column_of(scales_ref[rep, core, 0][0:1, :], rows)
            out_total[...] += mm_tn((gained_slots[turn] * scale).astype(BF16), low_slots[turn])

            @pl.when(at + 2 < 2 * reps)
            def _():
                gained_load(turn, *early_place(at + 2)).start()
                low_load(turn, *early_place(at + 2)).start()

            return carry

        lax.fori_loop(0, 2 * reps, early, 0)
        low_load(0, p.rep_at(1), 1 - p.core).start()
        low_load(1, p.rep_at(1), p.core).start()
        out_parts, out_mid, out_sems, out_into, out_line_sems, out_low = work["out"]
        out_line_total = out_total.at[pl.ds(0, quarter)]
        out_parts[...] = out_total[...].astype(BF16).reshape(reps, quarter, model)
        for distance in range(1, reps):
            rep = p.rep_at(distance)
            p.send(out_parts.at[rep], out_mid.at[p.rep], out_sems.at[0, distance], out_sems.at[1, distance],
                   p.device(rep=rep))
        out_mid[p.rep] = out_parts[p.rep]
        out_job = LineSum(p, lambda at: [out_mid[at]], out_into, out_into, out_line_sems)
        layer_job.ready()
        layer_job.step(0)

        parts, own_part, pair, pair_sems, into, into_sems = work["sum"]

        def swap(distance, rep, start):
            copy = pltpu.make_async_remote_copy(
                src_ref=parts.at[lax.rem(distance, 2)], dst_ref=pair.at[rep], send_sem=pair_sems.at[0, rep],
                recv_sem=pair_sems.at[1, rep], device_id=p.sibling(), device_id_type=MESH_ID,
            )
            copy.start() if start else copy.wait_send()

        def onward(distance, rep, start):
            copy = pltpu.make_async_remote_copy(
                src_ref=pair.at[rep], dst_ref=into.at[distance - 1], send_sem=into_sems.at[0, distance],
                recv_sem=into_sems.at[1, distance], device_id=p.device(rep=rep), device_id_type=MESH_ID,
            )
            copy.start() if start else copy.wait_send()

        def visit(at, carry):
            distance, turn = lax.rem(at // 2 + 1, reps), lax.rem(at, 2)
            rep = p.rep_at(distance)
            core = jnp.where(turn == 0, 1 - p.core, p.core)
            first_load(rep, core).start()
            low_load(turn, rep, core).wait()
            proj_load(turn, rep, core).wait()
            scale = column_of(scales_ref[rep, core, 0][0:1, :], rows)
            pull = column_of(scales_ref[rep, core, 1][0:1, :], rows)
            seg_column, seg_line = segments(lengths_ref[rep, core][0:1, :], sequences, rows)
            block = Block(
                proj_slots[turn], seg_column, seg_line, taps_ref[...], heads_ref[...], channels, width, state
            )
            low_rows = low_slots[turn]
            proj_grad, tap_grads, head_grads, wide_grads = block_back(
                block, low_rows, scale, pull, taps_ref, skip_ref, norm_ref, weight_ref, out_ref[...]
            )
            taps_total[0:5, :] += tap_grads
            heads_total[0:1, :] += head_grads[0]
            heads_total[1:2, :] += head_grads[1]
            wide_total[0:2, :] += wide_grads
            part_rows = mm_nt(proj_grad, weight_ref[...])

            @pl.when(turn == 0)
            def _():
                @pl.when(at >= 4)
                def _():
                    swap(at // 2 - 1, p.rep_at(at // 2 - 1), False)

                parts[lax.rem(distance, 2)] = part_rows.astype(BF16)
                swap(distance, rep, True)

            @pl.when((turn == 1) & (distance == 0))
            def _():
                own_part[...] = part_rows

            @pl.when((turn == 1) & (distance > 0))
            def _():
                p.arrived(pair.at[rep], pair_sems.at[1, rep])
                pair[rep] = add_up(part_rows, pair[rep]).astype(BF16)
                onward(distance, rep, True)

            first_load(rep, core).wait()
            for z in range(depth):
                columns = first_slot[:, 2 * part * z : 2 * part * (z + 1)]
                for start in range(0, wide, 384):
                    piece = slice(start, min(start + 384, wide))
                    in_total[z, :, :, piece] += mm_tn(columns, proj_grad[:, piece]).reshape(2, part, -1)

            @pl.when(at < 2 * reps - 2)
            def _():
                later = p.rep_at(lax.rem(at // 2 + 2, reps))
                proj_load(turn, later, core).start()
                low_load(turn, later, core).start()

            def out_start():
                for distance in range(1, reps):
                    p.arrived(out_mid.at[p.rep_at(distance)], out_sems.at[1, distance])
                out_job.step(0)

            pl.when(at == 1)(out_start)
            for step in range(1, depth - 1):
                pl.when(at == 2 * step)(functools.partial(layer_job.step, step))
                pl.when(at == 2 * step + 1)(functools.partial(out_job.step, step))
            return carry

        lax.fori_loop(0, 2 * reps, visit, 0)

        common_parts = work["common"][0]
        common_parts[...] = in_total[:, :, :, side:].astype(BF16)
        common_job = ColumnSum(p, common_parts, *work["common"][1:5])
        side_jobs = []
        for kind in range(2):
            columns = slice(kind * channels, (kind + 1) * channels)
            side_into, side_sems = work["side"][2 * kind : 2 * kind + 2]

            def terms(at, columns=columns):
                return [in_total[at, :, :, columns]]

            side_jobs.append(LineSum(p, terms, side_into, side_into, side_sems))
        side_pair, side_away, side_swap = work["side"][4:]
        side_total = gained_slots.at[:, pl.ds(0, part)]
        side_jobs[0].step(0)

        end_sems, keep_sems, late = work["end"]

        def late_load(source, chunk):
            return pltpu.make_async_copy(
                source.at[pl.ds(32 * chunk, 32)], late.at[chunk % 2], keep_sems.at[3 + chunk % 2]
            )

        late_load(grad_ref, 0).start()
        p.arrived(pair.at[p.rep], pair_sems.at[1, p.rep])
        common_job.ready()
        common_job.step(0)
        side_jobs[1].step(0)
        for distance in range(1, reps):
            p.arrived(into.at[distance - 1], into_sems.at[1, distance])
        gain_grad = jnp.zeros((1, model), F32)
        for start in range(0, rows, 32):
            piece = slice(start, start + 32)
            if start + 32 < rows:
                late_load(grad_ref, start // 32 + 1).start()
            late_load(grad_ref, start // 32).wait()
            first_grad = add_up(
                own_part[piece, :], pair[p.rep, piece, :], *[into[at, piece, :] for at in range(reps - 1)]
            )
            x = x_ref[piece, :].astype(F32)
            x_scale = rms_rows(x)
            gain_grad = gain_grad + jnp.sum(x * first_grad * x_scale, axis=0, keepdims=True)
            weighted = first_grad * gain_ref[...]
            tokens_grad_ref[piece, :] = (
                late[start // 32 % 2]
                + x_scale * weighted
                - x * x_scale**3 * jnp.mean(x * weighted, axis=1, keepdims=True)
            ).astype(BF16)

        small = work["small"][0]
        small[...] = jnp.zeros_like(small)
        team = 2 * p.rep + p.core
        own_taps = taps_total[:, :channels]
        blank = jnp.zeros_like(own_taps)
        taps_full = jnp.concatenate(
            [jnp.where(team == member, own_taps, blank) for member in range(2 * reps)] + [taps_total[:, channels:]],
            axis=1,
        )
        for z in range(depth):
            for core in range(2):
                shard = 2 * z + core
                small[z, core, 0:8, 0:per_shard] = taps_full[:, per_shard * shard : per_shard * (shard + 1)]
                small[z, core, 12:13, 0:part] = post_grad_ref[:, part * shard : part * (shard + 1)]
                small[z, core, 13:14, 0:part] = gain_grad[:, part * shard : part * (shard + 1)]
                small[z, core, 16 : 16 + experts, 0:router_width] = router_ref[z, core]
        lane = lax.broadcasted_iota(jnp.int32, (1, LANES), 1)
        skip_row = jnp.zeros((1, LANES), F32)
        for head in range(heads):
            value = jnp.sum(wide_total[1:2, head * width : (head + 1) * width], axis=1, keepdims=True)
            skip_row = jnp.where(lane == head, value, skip_row)
        small[p.rep, p.core, 8:10, 0:LANES] = heads_total[0:2, :]
        small[p.rep, p.core, 10:11, 0:LANES] = skip_row
        small[p.rep, p.core, 11:12, 0:channels] = wide_total[0:1, :]
        small_job = ColumnSum(p, small, *work["small"][1:5])
        small_job.ready()
        small_job.step(0)
        for at in range(1, depth - 1):
            for job in (common_job, side_jobs[0], small_job):
                job.step(at)

        def to_reps(source, target, at):
            for distance in range(1, reps):
                p.send(source, target.at[p.rep], end_sems.at[0, at, distance], end_sems.at[1, at, distance],
                       p.device(rep=p.rep_at(distance)))

        def from_reps(target, at):
            for distance in range(1, reps):
                p.arrived(target.at[p.rep_at(distance)], end_sems.at[1, at, distance])

        def side_finish(kind):
            side_jobs[kind].total(side_total)
            side_pair[kind, p.core] = side_total[p.core].astype(BF16)
            side_away[kind] = side_total[1 - p.core].astype(BF16)
            p.send(side_away.at[kind], side_pair.at[kind, p.core], side_swap.at[0, kind], side_swap.at[1, kind],
                   p.sibling())
            p.arrived(side_pair.at[kind, 1 - p.core], side_swap.at[1, kind])
            to_reps(side_pair.at[kind], side_out.at[kind], kind)
            return p.local(side_pair.at[kind], side_out.at[kind, p.rep], keep_sems.at[kind])

        keeps = [side_finish(0)]
        common_total, common_low = work["common"][5:]
        common_job.total(common_total)
        common_low[...] = common_total[...].astype(BF16)
        to_reps(common_low, common_out, 2)
        keeps.append(p.local(common_low, common_out.at[p.rep], keep_sems.at[2]))
        out_job.total(out_line_total)
        out_low[...] = out_line_total[...].astype(BF16)
        to_reps(out_low, out_out, 3)
        keeps.append(p.local(out_low, out_out.at[p.rep], keep_sems.at[5]))
        small_total, small_all = work["small"][5:]
        small_job.total(small_total)
        small_all[p.rep] = small_total[...]
        to_reps(small_total, small_all, 4)
        for at in range(1, depth - 1):
            side_jobs[1].step(at)
        keeps.append(side_finish(1))

        late_load(after_ref, 0).start()
        layer_job.total(own_part)
        for chunk in range(rows // 32):
            piece = slice(32 * chunk, 32 * chunk + 32)
            if chunk + 1 < rows // 32:
                late_load(after_ref, chunk + 1).start()
            late_load(after_ref, chunk).wait()
            layer_out_ref[piece, :] = (own_part[piece, :] + late[chunk % 2]).astype(BF16)
        from_reps(small_all, 4)
        small_out[...] = add_up(*[small_all[at] for at in range(reps)])
        for at, target in ((0, side_out.at[0]), (1, side_out.at[1]), (2, common_out), (3, out_out)):
            from_reps(target, at)
        for keep in keeps:
            keep.wait()
        for distance in range(reps):
            rep = p.rep_at(distance)
            if distance in (0, reps - 1):
                swap(distance, rep, False)
            if distance:
                onward(distance, rep, False)
        p.finish()

    return pl.pallas_call(
        kernel,
        in_specs=in_vmem(1) + anywhere(2) + in_vmem(11) + anywhere(5),
        out_specs=in_vmem(2) + anywhere(3) + in_vmem(1),
        out_shape=[
            jax.ShapeDtypeStruct((rows, model), BF16),
            jax.ShapeDtypeStruct((rows, model), BF16),
            jax.ShapeDtypeStruct((2, reps, 2, part, channels), BF16),
            jax.ShapeDtypeStruct((reps, part, wide - side), BF16),
            jax.ShapeDtypeStruct((reps, quarter, model), BF16),
            jax.ShapeDtypeStruct(small_shape, F32),
        ],
        scratch_shapes=[item for items in groups.values() for item in items],
        compiler_params=remote_params(3, 63),
        name="backward_mixer",
    )(
        scales, after, after_grad, tokens, in_gain, post_grad, router_parts, lengths, taps, head_rows, skip, norm,
        weight, out_weight, low, layer_parts, first, proj, gained,
    )


def assemble_kernel(channels, state, heads, side_ref, common_ref, out_ref, in_grad_ref, out_grad_ref):
    reps = side_ref.shape[1]
    inner = 2 * reps * channels
    for kind in range(2):
        for rep in range(reps):
            for core in range(2):
                at = kind * inner + (2 * rep + core) * channels
                in_grad_ref[:, at : at + channels] = side_ref[kind, rep, core].astype(F32)
    in_grad_ref[:, 2 * inner : 2 * inner + 2 * state] = add_up(
        *[common_ref[rep, :, : 2 * state] for rep in range(reps)]
    )
    start = 2 * inner + 2 * state
    tail = []
    for rep in range(reps):
        pair = common_ref[rep, :, 2 * state :].astype(F32)
        tail += [pair[:, :heads], pair[:, LANES // 2 : LANES // 2 + heads]]
    in_grad_ref[:, start:] = jnp.concatenate(tail, axis=1)
    out_grad_ref[...] = out_ref[...].astype(F32).reshape(out_grad_ref.shape)


def assemble(side, common, out_rows, channels, state, heads):
    reps, part = side.shape[1], side.shape[3]
    columns = 4 * reps * channels + 2 * state + 2 * reps * heads
    model = out_rows.shape[2]
    return pl.pallas_call(
        functools.partial(assemble_kernel, channels, state, heads),
        in_specs=in_vmem(3),
        out_specs=in_vmem(2),
        out_shape=[
            jax.ShapeDtypeStruct((part, columns), F32),
            jax.ShapeDtypeStruct((channels, model), F32),
        ],
        compiler_params=pltpu.CompilerParams(vmem_limit_bytes=48 * 2**20),
        name="assemble",
    )(side, common, out_rows)


def slot_match(table_row, capacity, rows):
    slot = lax.broadcasted_iota(jnp.int32, (capacity, rows), 0).astype(F32) + 1.0
    return table_row == slot


def dispatch_kernel(
    local, capacity, half,
    table_ref, own_ref, second_ref, g_ref, router_ref, in_ref, out_ref,
    buffer_ref, slot_g_ref, gate_slot_ref, gates_ref, hidden_ref, grad_ref, in_grad_ref, out_grad_ref,
    in_total, out_total,
):
    at = pl.program_id(0)
    second, g = second_ref[...], g_ref[...]
    rows = second.shape[0]
    table = table_ref[...].astype(F32)
    used = table > 0.0
    logits = mm_nt(router_ref[...], second)
    top = jnp.max(jnp.where(used, logits, -jnp.inf), axis=0, keepdims=True)
    raw = jnp.where(used, jnp.exp(jnp.where(used, logits - top, 0.0)), 0.0)
    gates = raw / jnp.sum(raw, axis=0, keepdims=True)
    gates_ref[...] = gates
    expert = lax.broadcasted_iota(jnp.int32, gates.shape, 0)
    shard = 2 * lax.axis_index("z") + lax.axis_index("core")
    for i in range(local):
        match = slot_match(own_ref[i : i + 1, :].astype(F32), capacity, rows)
        onehot = match.astype(BF16)
        buffer_ref[i] = mm(onehot, second).astype(BF16)
        slot_g_ref[i] = mm(onehot, g).astype(BF16)
        gate_row = jnp.sum(jnp.where(expert == local * shard + i, gates, 0.0), axis=0, keepdims=True)
        gate_slot = jnp.sum(jnp.where(match, gate_row, 0.0), axis=1, keepdims=True)
        gate_slot_ref[i] = jnp.broadcast_to(gate_slot, (capacity, LANES))
    pre = mm(second, in_ref[...])
    a, b = pre[:, :half], pre[:, half:]
    sig = jax.nn.sigmoid(a)
    hidden = (a * sig * b).astype(BF16)
    hidden_ref[...] = hidden
    back = mm_nt(g, out_ref[...])
    grad = jnp.concatenate([back * b * silu_slope(a, sig), back * a * sig], axis=1).astype(BF16)
    grad_ref[...] = grad

    @pl.when(at == 0)
    def _():
        in_total[...] = jnp.zeros_like(in_total)
        out_total[...] = jnp.zeros_like(out_total)

    in_total[...] += mm_tn(second, grad)
    out_total[...] += mm_tn(hidden, g)

    @pl.when(at == pl.num_programs(0) - 1)
    def _():
        in_grad_ref[...] = in_total[...].astype(BF16)
        out_grad_ref[...] = out_total[...].astype(BF16)


def dispatch(table, own, second, g, router_t, shared_in, shared_out, capacity):
    group, experts, rows = table.shape
    local = own.shape[1]
    model = second.shape[1]
    half = shared_out.shape[0]
    slots = group * capacity

    def by_block(*shape):
        return pl.BlockSpec((None,) + shape, lambda q: (q,) + (0,) * len(shape))

    def by_slots(width):
        return pl.BlockSpec((local, capacity, width), lambda q: (0, q, 0))

    return pl.pallas_call(
        functools.partial(dispatch_kernel, local, capacity, half),
        grid=(group,),
        in_specs=[
            by_block(experts, rows), by_block(local, rows), by_rows((rows, model)), by_rows((rows, model)),
            whole((experts, model)), whole((model, 2 * half)), whole((half, model)),
        ],
        out_specs=[
            by_slots(model), by_slots(model), by_slots(LANES), by_block(experts, rows), by_rows((rows, half)),
            by_rows((rows, 2 * half)), whole((model, 2 * half)), whole((half, model)),
        ],
        out_shape=[
            jax.ShapeDtypeStruct((local, slots, model), BF16),
            jax.ShapeDtypeStruct((local, slots, model), BF16),
            jax.ShapeDtypeStruct((local, slots, LANES), F32),
            jax.ShapeDtypeStruct((group, experts, rows), F32),
            jax.ShapeDtypeStruct((group * rows, half), BF16),
            jax.ShapeDtypeStruct((group * rows, 2 * half), BF16),
            jax.ShapeDtypeStruct((model, 2 * half), BF16),
            jax.ShapeDtypeStruct((half, model), BF16),
        ],
        scratch_shapes=[pltpu.VMEM((model, 2 * half), F32), pltpu.VMEM((half, model), F32)],
        compiler_params=pltpu.CompilerParams(vmem_limit_bytes=56 * 2**20),
        name="dispatch",
    )(table, own, second, g, router_t, shared_in, shared_out)


def experts_kernel(
    buffer_ref, slot_g_ref, gate_ref, in_ref, out_ref,
    weighted_ref, back_ref, dot_ref, in_grad_ref, out_grad_ref, in_total, out_total,
):
    at = pl.program_id(1)
    buffer, weight_in, weight_out = buffer_ref[...], in_ref[...], out_ref[...]
    half = weight_out.shape[0]
    pre = mm(buffer, weight_in)
    a, b = pre[:, :half], pre[:, half:]
    sig = jax.nn.sigmoid(a)
    act = a * sig
    hidden = (act * b).astype(BF16)
    gate = gate_ref[:, 0:1]
    slot_g = slot_g_ref[...].astype(F32)
    result = mm(hidden, weight_out).astype(BF16).astype(F32)
    weighted_ref[...] = (gate * result).astype(BF16)
    dot_ref[...] = jnp.broadcast_to(jnp.sum(slot_g * result, axis=1, keepdims=True), dot_ref.shape)
    result_grad = (gate * slot_g).astype(BF16)
    hidden_grad = mm_nt(result_grad, weight_out)
    pre_grad = jnp.concatenate([hidden_grad * b * silu_slope(a, sig), hidden_grad * act], axis=1).astype(BF16)
    back_ref[...] = mm_nt(pre_grad, weight_in).astype(BF16)

    @pl.when(at == 0)
    def _():
        in_total[...] = jnp.zeros_like(in_total)
        out_total[...] = jnp.zeros_like(out_total)

    in_total[...] += mm_tn(buffer, pre_grad)
    out_total[...] += mm_tn(hidden, result_grad)

    @pl.when(at == pl.num_programs(1) - 1)
    def _():
        in_grad_ref[...] = in_total[...].astype(BF16)
        out_grad_ref[...] = out_total[...].astype(BF16)


def run_experts(buffer, slot_g, gate_slot, expert_in, expert_out, step):
    local, slots, model = buffer.shape
    half = expert_out.shape[1]

    def by_step(width):
        return pl.BlockSpec((None, step, width), lambda i, m: (i, m, 0))

    def by_expert(*shape):
        return pl.BlockSpec((None,) + shape, lambda i, m: (i, 0, 0))

    return pl.pallas_call(
        experts_kernel,
        grid=(local, slots // step),
        in_specs=[
            by_step(model), by_step(model), by_step(LANES), by_expert(model, 2 * half), by_expert(half, model),
        ],
        out_specs=[
            by_step(model), by_step(model), by_step(LANES), by_expert(model, 2 * half), by_expert(half, model),
        ],
        out_shape=[
            jax.ShapeDtypeStruct((local, slots, model), BF16),
            jax.ShapeDtypeStruct((local, slots, model), BF16),
            jax.ShapeDtypeStruct((local, slots, LANES), F32),
            jax.ShapeDtypeStruct((local, model, 2 * half), BF16),
            jax.ShapeDtypeStruct((local, half, model), BF16),
        ],
        scratch_shapes=[pltpu.VMEM((model, 2 * half), F32), pltpu.VMEM((half, model), F32)],
        compiler_params=pltpu.CompilerParams(vmem_limit_bytes=62 * 2**20),
        name="run_experts",
    )(buffer, slot_g, gate_slot, expert_in, expert_out)


def gather(values, axes, axis=0):
    return lax.all_gather(values, axes, axis=axis, tiled=True)


def scatter_sum(values, axes, axis=0):
    return lax.psum_scatter(values, axes, scatter_dimension=axis, tiled=True)


def columns_of(values, start, size, axis=1):
    return lax.dynamic_slice_in_dim(values, start, size, axis=axis)


def shards(
    tokens,
    cotangent,
    dealt_to,
    lengths,
    routes,
    slot_index,
    in_norm,
    in_proj,
    conv_weight,
    conv_bias,
    dt_bias,
    decay_log,
    skip_gain,
    mixer_norm,
    out_proj,
    post_norm,
    router,
    shared_in,
    shared_out,
    expert_in,
    expert_out,
):
    reps, depth = lax.axis_size("rep"), lax.axis_size("z")
    group = 2 * depth
    rep, z, core = lax.axis_index("rep"), lax.axis_index("z"), lax.axis_index("core")
    shard = 2 * z + core
    team = 2 * rep + core
    members = 2 * reps
    rows, model = tokens.shape
    top = routes.shape[1]
    local = expert_in.shape[0]
    experts = local * group
    capacity = rows * top * 4 // (3 * experts)
    inner = mixer_norm.shape[0] * group
    convolved = conv_bias.shape[0] * group
    head_count = dt_bias.shape[0] * group
    width = inner // head_count
    state = (convolved - inner) // 2
    channels = inner // members
    heads = head_count // members
    shared = shared_out.shape[0]
    part = in_norm.shape[0]

    expert_ids = jnp.arange(experts, dtype=jnp.int32)
    table = jnp.sum(
        jnp.where(routes[:, None, :] == expert_ids[None, :, None], slot_index[:, None, :] + 1, 0), axis=2
    ).astype(BF16)
    numbers = jnp.concatenate([lengths[0], dealt_to]).astype(BF16)
    vector_rows = [in_norm[None], conv_weight, conv_bias[None], dt_bias[None], decay_log[None], skip_gain[None],
                   mixer_norm[None], post_norm[None], numbers[None]]
    vector_width = -(-max(row.shape[1] for row in vector_rows) // LANES) * LANES
    vectors = jnp.concatenate(
        [jnp.pad(row, ((0, 0), (0, vector_width - row.shape[1]))) for row in vector_rows]
        + [jnp.zeros((4, vector_width), BF16)], axis=0
    )
    part_wide = -(-part // LANES) * LANES
    table_block = jnp.concatenate([table.T, jnp.pad(router.T, ((0, 0), (0, part_wide - part)))], axis=1)
    pair_heads = 2 * heads
    dt_pair = columns_of(in_proj, inner + convolved + pair_heads * rep, pair_heads)
    blank = jnp.zeros((part, LANES // 2 - heads), BF16)
    common = jnp.concatenate(
        [in_proj[:, 2 * inner : 2 * inner + 2 * state], dt_pair[:, :heads], blank, dt_pair[:, heads:], blank], axis=1
    )

    def pair_of(member):
        return jnp.concatenate(
            [columns_of(in_proj, channels * member, channels), columns_of(in_proj, inner + channels * member, channels)],
            axis=1,
        )

    sequences = lengths.shape[1]
    (after, mixer_result, scale, lengths_plane, in_gain, post_gain, taps_own, head_rows, skip_own, norm_own, table_all,
     second_column, g_column, first, weight, out_own, projected, gained) = forward_mixer(
        tokens, cotangent, pair_of(team), pair_of(2 * rep + 1 - core), common, vectors, table_block,
        out_proj.reshape(reps, channels // reps, model),
        (reps, depth, channels, width, state, sequences, inner, convolved),
    )
    second_column = second_column.reshape(group * rows, model)
    g_column = g_column.reshape(group * rows, model)
    shared_in_own = lax.all_to_all(
        shared_in.reshape(part, 2, group, shared).transpose(2, 0, 1, 3).reshape(group * part, 2 * shared),
        COLUMN, split_axis=0, concat_axis=0, tiled=True,
    )

    table_all = table_all.reshape(group, experts, -1)
    router_t = table_all[:, :, rows : rows + part].transpose(1, 0, 2).reshape(experts, model)
    dealt_column = shard ^ dealt_to[0] ^ jnp.arange(group, dtype=jnp.int32)
    table_dealt = jnp.take(table_all[:, :, :rows], dealt_column, axis=0)
    table_own = columns_of(table_dealt, local * shard, local)

    buffer, slot_g, gate_slot, gates, shared_hidden, shared_grad, shared_in_grad, shared_out_grad = dispatch(
        table_dealt, table_own, second_column, g_column, router_t, shared_in_own, shared_out, capacity
    )
    weighted, buffer_grad, dots, grad_expert_in, grad_expert_out = run_experts(
        buffer, slot_g, gate_slot, expert_in, expert_out, group * capacity // 2
    )
    shared_in_rows = lax.all_to_all(shared_in_grad, COLUMN, split_axis=0, concat_axis=0, tiled=True)
    shared_in_rows = shared_in_rows.reshape(group, part, 2, shared).transpose(1, 2, 0, 3).reshape(part, -1)
    grad_expert_in, grad_expert_out, grad_shared_out, grad_shared_in = [
        values.astype(F32)
        for values in lax.psum((grad_expert_in, grad_expert_out, shared_out_grad, shared_in_rows), "rep")
    ]

    after_grad, post_grad, router_grad, layer_parts, low_plane, scales = join_experts(
        table_own, gates, dots, shared_hidden, shared_grad, router_t, shared_in_own, shared_out, cotangent, after,
        mixer_result, scale, post_gain, buffer_grad, weighted, second_column, inner, reps, depth, capacity,
    )
    router_parts = jnp.pad(
        router_grad.reshape(experts, depth, 2, part).transpose(1, 2, 0, 3), ((0, 0), (0, 0), (0, 0), (0, part_wide - part))
    )
    layer_out, grad_tokens, side_rows, common_rows, out_rows, small_sum = backward_mixer(
        scales, after, after_grad, tokens, in_gain, post_grad, router_parts, lengths_plane, taps_own, head_rows, skip_own, norm_own, weight.reshape(model, -1),
        out_own.reshape(channels, model), low_plane, layer_parts, first, projected, gained,
        (reps, depth, channels, width, state, sequences, inner, convolved),
    )
    grad_in_proj, grad_out_proj = assemble(side_rows, common_rows, out_rows, channels, state, heads)
    per_shard = conv_bias.shape[0]

    return (
        layer_out,
        grad_tokens,
        small_sum[13, :part],
        grad_in_proj,
        small_sum[:4, :per_shard],
        small_sum[4, :per_shard],
        small_sum[8, :heads],
        small_sum[9, :heads],
        small_sum[10, :heads],
        small_sum[11, :channels],
        grad_out_proj,
        small_sum[12, :part],
        small_sum[16:, :part].T,
        grad_shared_in,
        grad_shared_out,
        grad_expert_in,
        grad_expert_out,
    )


def solution(mesh):
    reps, group = mesh.shape["rep"], mesh.shape["shard"]
    split = Mesh(mesh.devices.reshape(reps, group // 2, 2), ALL)
    one, row = P(COLUMN), P(COLUMN, None)
    token = P(ALL, None)
    return jax.shard_map(
        shards,
        mesh=split,
        in_specs=(
            token, token, P(ALL), token, token, token, one, row, P(None, COLUMN), one, one, one, one, one, row,
            one, row, row, row, P(COLUMN, None, None), P(COLUMN, None, None),
        ),
        out_specs=(
            token, token, one, row, P(None, COLUMN), one, one, one, one, one, row, one, row, row, row,
            P(COLUMN, None, None), P(COLUMN, None, None),
        ),
        check_vma=False,
    )
```

time: 768 us -> 686 us (0.89); the launches traced: 753 us -> 682 us
  local copies, waits for them, and re-layouts: 67 us -> 33 us
  Pallas kernels: 627 us -> 605 us
  other arithmetic: 35.6 us -> 18.4 us
    pallas_call x7 -> x4, Pallas kernels: 567 us -> 544 us  [the longest x1 225 us: forward_mixer(): pl.pallas_call(kernel, in_specs=in_vmem(1) + anywhere(7), out_specs=in_vm...]
    convert_element_type x11 -> x0, local copies, waits for them, and re-layouts: 17.9 us -> none  [the longest x2 9.12 us: shards(): side_rows[:, :, :, :channels].transpose(2, 0, 1, 3).reshape(part, inner)]
    convert_element_type x8 -> x1, other arithmetic: 10.5 us -> 0.01 us  [shards(): table = jnp.sum(jnp.where(routes[:, None, :] == expert_ids[None, :, None]...]
  transfers between devices with their start and end apart: 4 -> 3, of which waited for: 0 -> 0; matrix products, arithmetic and copies ran while one was open for 8% -> 4% of each run, Pallas kernels for 68% -> 86%
where the time goes in v3:
time: 686 us; the launch traced here: 682 us
  Pallas kernels  605 us (88%)
  local copies, waits for them, and re-layouts  33 us (5%)
  other arithmetic  18.4 us (3%)
  between operations  15.3 us (2%)
  starting transfers between devices  9.93 us (1%)
    pallas_call x1, Pallas kernels, forward_mixer(): pl.pallas_call(kernel, in_specs=in_vmem(1) + anywhere(7), out_specs=in_vm...  225 us
    pallas_call x1, Pallas kernels, backward_mixer(): pl.pallas_call(kernel, in_specs=in_vmem(1) + anywhere(2) + in_vmem(11) +...  207 us
    pallas_call x1, Pallas kernels, join_experts(): pl.pallas_call(kernel, in_specs=in_vmem(13) + anywhere(3), out_specs=in_v...  109 us
    pallas_call x1, Pallas kernels, run_experts(): pl.pallas_call(experts_kernel, grid=(local, slots // step), in_specs=[by_...  41.5 us
    pallas_call x1, Pallas kernels, dispatch(): pl.pallas_call(functools.partial(dispatch_kernel, local, capacity, half),...  19.1 us
    convert_element_type x4, other arithmetic, shards(): values.astype(F32)  14.8 us
  transfers between devices with their start and end apart: 3, of which 0 were waited for; matrix products, arithmetic and copies ran while one was open for 4% of the time, Pallas kernels for 86%

profile of v3, /device:TPU:0, one launch (start us, length us, event | category | flops | bytes accessed | tf_op | source)
XLA Modules:
  0.0 681.6 jit_solution(6629475821177829060)
XLA Ops:
  7.3 1.4 copy.54
  8.8 0.6 copy.50
  9.4 1.4 all_to_all.13
  10.8 6.3 all-to-all-start
  17.8 0.6 pad.48
  18.4 0.6 pad.47
  19.0 0.6 pad.43
  19.6 0.6 pad.44
  20.2 0.6 pad.45
  20.8 0.6 pad.46
  21.5 0.7 fusion.2
  22.2 0.8 concatenate.30.common_ref
  23.0 2.7 concatenate.33.vectors_ref
  25.7 0.7 select_reduce_fusion
  26.4 1.3 fusion.1.table_ref
  28.0 0.9 pad_maximum_fusion
  28.9 224.8 %forward_mixer.1 = (f32[256,1536]{1,0:T(8,128)}, bf16[256,1536]{1,0:T(8,128)(2,1)}, f32[8,256]{1,0:T(8,128)}, f32[4,2,8,128]{3,2,1,0:T(8,128)}, f32[1,1536]{1,0:...) custom-call(bf16[256,1536]{1,0:T(8,128)(2,1)} %x_ref.3, ...), custom_call_target="tpu_custom_call" | custom-call | tf_op jit(solution)/shard_map/forward_mixer/pallas_call | solution.py:784
  253.7 0.8 slice.59
  254.5 0.8 slice.58
  255.4 0.7 reshape.130.router_ref
  256.1 0.5 gather_fusion
  256.8 0.6 constant_dynamic-slice_fusion.own_ref
  257.4 0.9 copy-done.3
  258.3 19.1 %dispatch.1 = (bf16[2,1024,1536]{2,1,0:T(8,128)(2,1)}, bf16[2,1024,1536]{2,1,0:T(8,128)(2,1)}, f32[2,1024,128]{2,1,0:T(8,128)}, f32[8,16,256]{2,1,0:T(8,128)}, b...) custom-call(bf16[8,16,256]{2,1,0:T(8,128)(2,1)} %copy-done.8, ...), custom_call_target="tpu_custom_call" | custom-call | tf_op jit(solution)/shard_map/dispatch/pallas_call | solution.py:1540
  277.4 3.6 all-to-all-start.1
  281.0 41.5 %run_experts.1 = (bf16[2,1024,1536]{2,1,0:T(8,128)(2,1)}, bf16[2,1024,1536]{2,1,0:T(8,128)(2,1)}, f32[2,1024,128]{2,1,0:T(8,128)}, bf16[2,1536,1024]{2,1,0:T(8,128)(2,1)}, bf16[2,512,1536]{2,1,0:T(8,128)(2,1)}) custom-call(bf16[2,1024,1536]{2,1,0:T(8,128)(2,1)} %get-tuple-element.66.buffer_ref, bf16[2,1024,1536]{2,1,0:T(8,128)(2,1)} %get-tuple-element.67.slot_g_ref, ...), custom_call_target="tpu_custom_call" | custom-call | tf_op jit(solution)/shard_map/run_experts/pallas_call | solution.py:1613
  322.7 0.9 copy.52
  323.6 1.1 copy.59
  324.7 108.9 %join_experts.1 = (f32[256,1536]{1,0:T(8,128)}, f32[1,1536]{1,0:T(1,128)}, f32[16,1536]{1,0:T(8,128)}, bf16[4,2,256,1536]{3,2,1,0:T(8,128)(2,1)}, bf16[4,2,256,1...) custom-call(bf16[8,2,256]{2,1,0:T(2,128)(2,1)} %constant_dynamic-slice_fusion.own_ref, ...), custom_call_target="tpu_custom_call" | custom-call | tf_op jit(solution)/shard_map/join_experts/pallas_call | solution.py:1055
  433.7 1.1 reshape.132
  434.8 0.7 pad.51.router_ref
  435.5 207.1 %backward_mixer.1 = (bf16[256,1536]{1,0:T(8,128)(2,1)}, bf16[256,1536]{1,0:T(8,128)(2,1)}, bf16[2,4,2,192,384]{4,3,2,1,0:T(8,128)(2,1)}, bf16[4,192,384]{2,1,0:T...) custom-call(f32[4,2,2,8,256]{4,3,2,1,0:T(8,128)} %get-tuple-element.78.scales_ref, ...), custom_call_target="tpu_custom_call" | custom-call | tf_op jit(solution)/shard_map/backward_mixer/pallas_call | solution.py:1415
  642.6 1.3 slice.49
  643.9 1.3 slice.48
  645.2 1.7 copy-done
  646.9 1.3 copy-done.1
  648.2 1.1 copy-done.2
  649.2 3.5 assemble.1
  652.7 1.3 slice_reduce_fusion
  654.0 1.3 slice_bitcast_fusion.1
  655.3 1.3 fusion.4
  656.7 1.3 slice_bitcast_fusion
  658.0 2.6 convert_element_type.48
  660.6 2.3 convert_element_type.49
  662.9 3.6 convert_element_type.51
  666.5 6.3 convert_element_type.50
  672.8 0.9 copy.69
  673.7 0.9 copy.70
  (66 shorter events, 1.0 us)
Async XLA Ops:
  7.2 10.6 %copy-start.16 = (s32[1,3]{1,0:T(1,128)S(1)}, s32[1,3]{1,0:T(1,128)}, u32[]{:S(2)}) copy-start(s32[1,3]{1,0:T(1,128)} %param.24) | copy-start | bytes 40
  7.2 10.6 %copy-start.17 = (bf16[192]{0:T(256)(128)(2,1)S(1)}, bf16[192]{0:T(256)(128)(2,1)}, u32[]{:S(2)}) copy-start(bf16[192]{0:T(256)(128)(2,1)} %param.27) | copy-start | bytes 1156
  7.2 10.6 %copy-start.18 = (bf16[192]{0:T(256)(128)(2,1)S(1)}, bf16[192]{0:T(256)(128)(2,1)}, u32[]{:S(2)}) copy-start(bf16[192]{0:T(256)(128)(2,1)} %param.36) | copy-start | bytes 1156
  7.2 11.2 %copy-start.12 = (bf16[384]{0:T(512)(128)(2,1)S(1)}, bf16[384]{0:T(512)(128)(2,1)}, u32[]{:S(2)}) copy-start(bf16[384]{0:T(512)(128)(2,1)} %param.34) | copy-start | bytes 2308
  7.2 11.8 %copy-start.11 = (bf16[416]{0:T(512)(128)(2,1)S(1)}, bf16[416]{0:T(512)(128)(2,1)}, u32[]{:S(2)}) copy-start(bf16[416]{0:T(512)(128)(2,1)} %param.30) | copy-start | bytes 2500
  7.2 12.4 %copy-start.13 = (bf16[6]{0:T(256)(128)(2,1)S(1)}, bf16[6]{0:T(256)(128)(2,1)}, u32[]{:S(2)}) copy-start(bf16[6]{0:T(256)(128)(2,1)} %param.31) | copy-start | bytes 40
  7.3 12.9 %copy-start.14 = (bf16[6]{0:T(256)(128)(2,1)S(1)}, bf16[6]{0:T(256)(128)(2,1)}, u32[]{:S(2)}) copy-start(bf16[6]{0:T(256)(128)(2,1)} %param.32) | copy-start | bytes 40
  7.3 13.5 %copy-start.15 = (bf16[6]{0:T(256)(128)(2,1)S(1)}, bf16[6]{0:T(256)(128)(2,1)}, u32[]{:S(2)}) copy-start(bf16[6]{0:T(256)(128)(2,1)} %param.33) | copy-start | bytes 40
  7.3 14.1 %copy-start.10 = (bf16[4,416]{1,0:T(4,128)(2,1)S(1)}, bf16[4,416]{1,0:T(4,128)(2,1)}, u32[]{:S(2)}) copy-start(bf16[4,416]{1,0:T(4,128)(2,1)} %param.29) | copy-start | bytes 9988
  7.3 14.1 %copy-start.9 = (s32[256,6]{0,1:T(8,128)S(1)}, s32[256,6]{0,1:T(8,128)}, u32[]{:S(2)}) copy-start(s32[256,6]{0,1:T(8,128)} %param.26) | copy-start | bytes 18436
  7.3 14.1 %copy-start.7 = (bf16[192,6448]{1,0:T(8,128)(2,1)S(1)}, bf16[192,6448]{1,0:T(8,128)(2,1)}, u32[]{:S(2)}) copy-start(bf16[192,6448]{1,0:T(8,128)(2,1)} %param.28) | copy-start | bytes 7428100
  7.3 14.9 %slice-start.2 = ((bf16[192,6448]{1,0:T(8,128)(2,1)}), bf16[192,256]{1,0:T(8,128)(2,1)S(1)}, s32[]{:S(2)}) async-start(bf16[192,6448]{1,0:T(8,128)(2,1)} %param.28), calls=%async_computation.5 | async-start | bytes 196608 | tf_op jit(solution)/shard_map/slice | solution.py:1709
  10.8 246.7 %all-to-all-start = ((bf16[8,192,256]{2,1,0:T(8,128)(2,1)}), bf16[8,192,256]{2,1,0:T(8,128)(2,1)S(1)}, u32[]{:S(2)}, u32[]{:S(2)}) async-start(bf16[8,192,256]{2,1,0:T(8,128)(2,1)} %all_to_all.13), calls=%async_computation | async-start | bytes 1572864 | tf_op jit(solution)/shard_map/all_to_all | solution.py:1727
  256.8 0.6 copy-start.8
  257.4 0.9 copy-start.3
  277.4 45.1 %all-to-all-start.1 = ((bf16[8,192,256]{2,1,0:T(8,128)(2,1)}), bf16[8,192,256]{2,1,0:T(8,128)(2,1)S(1)}, u32[]{:S(2)}, u32[]{:S(2)}) async-start(bf16[8,192,256]{2,1,0:T(8,128)(2,1)} %bitcast.61), calls=%async_computation.1 | async-start | bytes 1572864 | tf_op jit(solution)/shard_map/all_to_all | solution.py:1744
  281.0 377.0 %all-reduce.14.cloned.1.call-start = ((), (), s32[]{:S(2)}) async-start(), calls=%async_computation.2 | async-start | bytes 21233664 | tf_op jit(solution)/shard_map/psum | solution.py:1748
  645.2 1.7 copy-start
  646.9 1.3 copy-start.1
  648.2 1.1 copy-start.2
  658.0 4.9 copy-start.4
  658.0 8.5 %slice-start = ((s8[6291456]{0:T(1024)(128)(4,1)}), s8[4194304]{0:T(1024)(128)(4,1)S(1)}, s32[]{:S(2)}) async-start(s8[6291456]{0:T(1024)(128)(4,1)} %bitcast.52), calls=%async_computation.3 | async-start | bytes 8388608
  662.9 3.6 slice-start.1
  666.5 6.3 copy-start.6
  666.5 7.2 %copy-start.5 = (bf16[256,1536]{1,0:T(8,128)(2,1)S(1)}, bf16[256,1536]{1,0:T(8,128)(2,1)}, u32[]{:S(2)}) copy-start(bf16[256,1536]{1,0:T(8,128)(2,1)} %get-tuple-element.142) | copy-start | bytes 2359300
Sparse Core Ops, SparseCore 0:
  324.9 308.0 all-reduce.13

commit v4 on v3

--- a/solution.py
+++ b/solution.py
@@ -325,47 +325,72 @@
     def scratch(depth):
         return [pltpu.SemaphoreType.DMA((8, depth)), pltpu.SemaphoreType.DMA((1,))]
 
-    def __init__(self, place, own, slot, sems, local_sem, shared=None, keep=True):
-        self.place, self.slot, self.sems, self.shared = place, slot, sems, shared
-        p = place
-        self.keep = p.local(own, slot(p.z), local_sem.at[0]) if keep else None
-        self.onward(own, slot(p.z), 0, True, True)
-        if shared is not None:
-            p.send(own, slot(p.z), sems.at[4, 0], sems.at[5, 0], p.sibling())
-
-    def onward(self, source, target, distance, up, down):
-        p = self.place
-        if up is not False:
-            p.send(source, target, self.sems.at[0, distance], self.sems.at[1, distance], p.device(z=p.z + 1),
-                   (p.z < p.depth - 1) if up is True else up & (p.z < p.depth - 1))
-        if down is not False:
-            p.send(source, target, self.sems.at[2, distance], self.sems.at[3, distance], p.device(z=p.z - 1),
-                   (p.z > 0) if down is True else down & (p.z > 0))
-
-    def hop(self, distance):
+    def __init__(self, place, own, slot, sems, local_sem, shared=None, keep=True, start=True):
+        self.place, self.own, self.slot, self.sems, self.shared = place, own, slot, sems, shared
+        self.keep = None
+        if keep:
+            self.keep = pltpu.make_async_copy(own, slot(place.z), local_sem.at[0])
+        if start:
+            self.start()
+
+    def start(self):
+        if self.keep is not None:
+            self.keep.start()
+        self.send(0)
+
+    def ends(self, distance):
         p = self.place
         below, above = p.z >= distance, p.z + distance < p.depth
-        low, high = self.slot(jnp.maximum(p.z - distance, 0)), self.slot(jnp.minimum(p.z + distance, p.depth - 1))
-        p.arrived(low, self.sems.at[1, distance - 1], below)
-        self.onward(low, low, distance, below, False)
+        return below, above, jnp.maximum(p.z - distance, 0), jnp.minimum(p.z + distance, p.depth - 1)
+
+    def copies(self, distance):
+        p = self.place
+
+        def copy(source, target, at, device):
+            return pltpu.make_async_remote_copy(
+                src_ref=source, dst_ref=target, send_sem=self.sems.at[at, distance],
+                recv_sem=self.sems.at[at + 1, distance], device_id=device, device_id_type=MESH_ID,
+            )
+
+        up, down = p.device(z=p.z + 1), p.device(z=p.z - 1)
+        if distance == 0:
+            target = self.slot(p.z)
+            yield p.z < p.depth - 1, copy(self.own, target, 0, up)
+            yield p.z > 0, copy(self.own, target, 2, down)
+            if self.shared is not None:
+                yield True, copy(self.own, target, 4, p.sibling())
+            return
+        below, above, low, high = self.ends(distance)
+        low, high = self.slot(low), self.slot(high)
+        yield below & (p.z < p.depth - 1), copy(low, low, 0, up)
+        yield above & (p.z > 0), copy(high, high, 2, down)
         if self.shared is not None:
-            p.send(low, low, self.sems.at[4, distance], self.sems.at[5, distance], p.sibling(), below)
-        p.arrived(high, self.sems.at[3, distance - 1], above)
-        self.onward(high, high, distance, False, above)
-        if self.shared is not None:
-            p.send(high, high, self.sems.at[6, distance], self.sems.at[7, distance], p.sibling(), above)
+            yield below, copy(low, low, 4, p.sibling())
+            yield above, copy(high, high, 6, p.sibling())
+
+    def send(self, distance):
+        for condition, copy in self.copies(distance):
+            when(condition, copy.start)
+
+    def hop(self, distance):
+        below, above, low, high = self.ends(distance)
+        self.place.arrived(self.slot(low), self.sems.at[1, distance - 1], below)
+        self.place.arrived(self.slot(high), self.sems.at[3, distance - 1], above)
+        self.send(distance)
 
     def finish(self):
         p = self.place
         if self.keep is not None:
             self.keep.wait()
-        if self.shared is None:
-            return
-        p.arrived(self.shared(p.z), self.sems.at[5, 0])
-        for distance in range(1, p.depth):
-            below, above = p.z >= distance, p.z + distance < p.depth
-            p.arrived(self.shared(jnp.maximum(p.z - distance, 0)), self.sems.at[5, distance], below)
-            p.arrived(self.shared(jnp.minimum(p.z + distance, p.depth - 1)), self.sems.at[7, distance], above)
+        if self.shared is not None:
+            p.arrived(self.shared(p.z), self.sems.at[5, 0])
+            for distance in range(1, p.depth):
+                below, above, low, high = self.ends(distance)
+                p.arrived(self.shared(low), self.sems.at[5, distance], below)
+                p.arrived(self.shared(high), self.sems.at[7, distance], above)
+        for distance in range(p.depth):
+            for condition, copy in self.copies(distance):
+                when(condition, copy.wait_send)
 
 
 def add_up(*terms):
@@ -532,38 +557,46 @@
     return jnp.broadcast_to(column_values, (rows, LANES)).T[0:8, :]
 
 
-def forward_mixer(tokens, cotangent, own_pair, other_pair, common, vectors, table, out_quarters, sizes):
+def forward_mixer(tokens, cotangent, own_pair, other_pair, common, small, table, out_quarters, sizes):
     reps, depth, channels, width, state, sequences, inner, convolved = sizes
     rows, model = tokens.shape
     part, side = own_pair.shape
     wide = side + common.shape[1]
     quarter = out_quarters.shape[1]
-    vector_width = vectors.shape[1]
+    vector_width = -(-max(piece.shape[1] for piece in small) // LANES) * LANES
+    vector_rows = 16
     heads = channels // width
     per_shard = convolved // (2 * depth)
 
     x_scratch = [pltpu.VMEM((reps, 2, rows, model), BF16)] + PlaneGather.scratch(reps)
     w_scratch = [pltpu.VMEM((depth, 2, part, wide), BF16)] + ColumnGather.scratch(depth) * 3
-    v_scratch = [pltpu.VMEM((depth, 2) + vectors.shape, BF16)] + ColumnGather.scratch(depth) * 2
+    v_scratch = [pltpu.VMEM((depth, 2, vector_rows, vector_width), F32)] + ColumnGather.scratch(depth) * 2
     o_scratch = [
         pltpu.VMEM((depth, quarter, model), BF16), pltpu.VMEM((reps, quarter, model), BF16),
-    ] + ColumnGather.scratch(depth) + [pltpu.SemaphoreType.DMA((2, reps)), pltpu.SemaphoreType.DMA((2,))]
+    ] + ColumnGather.scratch(depth) + [pltpu.SemaphoreType.DMA((2, max(reps, depth))), pltpu.SemaphoreType.DMA((2,))]
     n_scratch = [pltpu.VMEM((8, LANES), F32)] + PlaneGather.scratch(reps)
     sum_scratch = [
         pltpu.VMEM((reps, rows, model), BF16), pltpu.VMEM((reps, 2, 8, rows), F32),
     ] + PlaneSum.scratch(reps, (rows, model), BF16) + PlaneSum.scratch(reps, (8, rows), F32)
     groups = [x_scratch, w_scratch, v_scratch, o_scratch, n_scratch, sum_scratch]
 
-    def kernel(x_ref, g_ref, own_ref, other_ref, common_ref, vectors_ref, table_ref, quarters_ref,
-               after_ref, mixed_ref, scale_ref, lengths_ref, in_gain_ref, post_gain_ref, taps_ref, heads_ref, skip_ref,
-               norm_ref, table_out, second_out, g_out, first_out, weight_out, out_out, proj_out, mixed_out, *scratch):
+    def kernel(x_ref, g_ref, own_ref, other_ref, common_ref, table_ref, quarters_ref, *refs):
+        small_refs, refs = refs[: len(small)], refs[len(small) :]
+        (after_ref, mixed_ref, scale_ref, lengths_ref, in_gain_ref, post_gain_ref, taps_ref, heads_ref, skip_ref,
+               norm_ref, table_out, second_out, g_out, first_out, weight_out, out_out, proj_out, mixed_out), scratch = refs[:18], refs[18:]
         cut = [0]
         for group in groups:
             cut.append(cut[-1] + len(group))
         x_work, w_work, v_work, o_work, n_work, sum_work = [scratch[i:j] for i, j in zip(cut, cut[1:])]
         (second, second_sems, second_local, g_sems, g_local, proj_buffer, proj_sems, keep_sems,
-         own_part, mixed_buffer, mixed_sems) = scratch[cut[-1]:]
+         own_part, mixed_all, mixed_sems, vectors_ref) = scratch[cut[-1]:]
         p = Place(reps, depth)
+        vectors_ref[...] = jnp.zeros_like(vectors_ref)
+        row = 0
+        for piece in small_refs:
+            count, size = piece.shape
+            vectors_ref[row : row + count, :size] = piece[...].astype(F32)
+            row += count
         p.barrier(plane=True, column=True)
 
         x_all, weight_all, vectors_all = x_work[0], w_work[0], v_work[0]
@@ -583,10 +616,6 @@
         x_job = PlaneGather(p, x_ref, x_all, x_work[1], x_work[2])
         p.arrived(other_slot(p.z), keep_sems.at[1])
         job_b = ColumnGather(p, other_slot(p.z), other_slot, w_work[5], w_work[6], keep=False)
-        mid, out_all = o_work[0], o_work[1]
-        job_o = ColumnGather(p, quarters_ref.at[p.rep], lambda z: mid.at[z], o_work[2], o_work[3])
-        table_job = ColumnGather(p, table_ref, lambda z: table_out.at[z, p.core], v_work[3], v_work[4],
-                                 shared=lambda z: table_out.at[z, 1 - p.core])
         for distance in range(1, depth):
             vector_job.hop(distance)
         vector_job.finish()
@@ -623,25 +652,53 @@
         skip_ref[...] = skip
 
         n_job.relay()
+        mid, out_all, o_sems, o_local, e_sems, e_local = o_work
+        late_jobs = []
         for distance in range(1, depth):
-            for job in (job_a, job_c, job_b, job_o, table_job):
+            for job in (job_a, job_c, job_b):
                 job.hop(distance)
+            if distance == min(2, depth - 1):
+                x_job.relay()
+                late_jobs.append(ColumnGather(p, quarters_ref.at[p.rep], lambda z: mid.at[z], o_sems, o_local))
+                late_jobs.append(
+                    ColumnGather(p, table_ref, lambda z: table_out.at[z, p.core], v_work[3], v_work[4],
+                                 shared=lambda z: table_out.at[z, 1 - p.core])
+                )
+        job_o, table_job = late_jobs
+        job_o.keep.wait()
+        job_o.keep = None
+        for job in (n_job, x_job, job_a, job_b, job_c):
+            job.finish()
+        weight_keep = p.local(weight_all, weight_out, e_local.at[0])
+
+        def exchange_copy(goal):
+            return pltpu.make_async_remote_copy(
+                src_ref=mid.at[goal], dst_ref=out_all.at[p.rep], send_sem=e_sems.at[0, goal],
+                recv_sem=e_sems.at[1, p.rep], device_id=p.device(rep=goal), device_id_type=MESH_ID,
+            )
+
+        def exchange(goal, condition):
+            def own():
+                out_all[goal] = mid[goal]
+
+            when(condition & (goal == p.rep), own)
+            when(condition & (goal != p.rep), exchange_copy(goal).start)
+
+        def out_tick(distance):
             if distance == 1:
-                x_job.relay()
-        for job in (n_job, x_job, job_a, job_b, job_c, job_o, table_job):
-            job.finish()
-        e_sems, e_local = o_work[4], o_work[5]
-        for distance in range(1, reps):
-            rep = p.rep_at(distance)
-            p.send(mid.at[rep], out_all.at[p.rep], e_sems.at[0, distance], e_sems.at[1, distance], p.device(rep=rep))
-        out_all[p.rep] = mid[p.rep]
+                exchange(p.z, p.z >= 0)
+            job_o.hop(distance)
+            table_job.hop(distance)
+            below, above, low, high = job_o.ends(distance)
+            exchange(low, below)
+            exchange(high, above)
+
+        def out_wait():
+            for rep in range(reps):
+                p.arrived(out_all.at[rep], e_sems.at[1, rep], rep != p.rep)
+
         g_job = ColumnGather(p, g_ref, lambda z: g_out.at[z, p.core], g_sems, g_local,
-                             shared=lambda z: g_out.at[z, 1 - p.core])
-        for distance in range(1, reps):
-            p.arrived(out_all.at[p.rep_at(distance)], e_sems.at[1, distance])
-        weight_keep = p.local(weight_all, weight_out, e_local.at[0])
-        out_keep = p.local(out_all, out_out, e_local.at[1])
-
+                             shared=lambda z: g_out.at[z, 1 - p.core], start=False)
         p.finish()
         parts, squares = sum_work[0], sum_work[1]
         pair, pair_sems, into, into_sems = sum_work[2:6]
@@ -674,14 +731,16 @@
         def proj_copy(slot, rep, core):
             return pltpu.make_async_copy(proj_buffer.at[slot], proj_out.at[rep, core], proj_sems.at[slot])
 
-        def mixed_copy(slot, rep, core):
-            return pltpu.make_async_copy(mixed_buffer.at[slot], mixed_out.at[rep, core], mixed_sems.at[slot])
-
-        def visit(at, carry):
+        def mixed_copy(at, rep, core):
+            return pltpu.make_async_copy(mixed_all.at[at], mixed_out.at[rep, core], mixed_sems.at[at])
+
+        def place_of(at):
             distance = lax.rem(at // 2 + 1, reps)
-            rep = p.rep_at(distance)
             turn = lax.rem(at, 2)
-            core = jnp.where(turn == 0, 1 - p.core, p.core)
+            return distance, p.rep_at(distance), turn, jnp.where(turn == 0, 1 - p.core, p.core)
+
+        def mix(at):
+            distance, rep, turn, core = place_of(at)
             x = x_all[rep, core].astype(F32)
             first = (x * rms_rows(x) * in_gain_ref[...]).astype(BF16)
             x_all[rep, core] = first
@@ -709,15 +768,12 @@
                 mixed.append((y + skip_ref[:, start:stop] * xin) * gate * jax.nn.sigmoid(gate))
             mixed = jnp.concatenate(mixed, axis=1)
             squares[rep, core] = row_of(jnp.sum(mixed * mixed, axis=1, keepdims=True), rows)
-            mixed = mixed * norm_ref[...]
-
-            @pl.when(at >= 2)
-            def _():
-                mixed_copy(turn, rep, core).wait()
-
-            mixed_buffer[turn] = mixed
-            mixed_copy(turn, rep, core).start()
-            mixed, mixed_rest = split_two(mixed)
+            mixed_all[at] = mixed * norm_ref[...]
+            mixed_copy(at, rep, core).start()
+
+        def put(at):
+            distance, rep, turn, core = place_of(at)
+            mixed, mixed_rest = split_two(mixed_all[at])
             out_weight = out_all[...].reshape(channels, model)
             part_rows = mm(mixed, out_weight) + mm(mixed_rest, out_weight)
 
@@ -738,11 +794,20 @@
                 s_pair[rep] = add_up(squares[rep, p.core], s_pair[rep])
                 onward(distance, rep, True)
 
+        delay = 4
+
+        def visit(at, carry):
+            pl.when(at < 2 * reps)(functools.partial(mix, at))
+            for distance in range(1, depth):
+                pl.when(at == min(distance - 1, delay - 1))(functools.partial(out_tick, distance))
+            pl.when(at == delay - 1)(g_job.start)
+            pl.when(at == delay)(out_wait)
+            pl.when(at >= delay)(functools.partial(put, at - delay))
+            pl.when(at == 2 * delay - 1)(functools.partial(g_job.hop, 1))
             return carry
 
-        lax.fori_loop(0, reps, visit, 0)
-        g_job.hop(1)
-        lax.fori_loop(reps, 2 * reps, visit, 0)
+        lax.fori_loop(0, 2 * reps + delay, visit, 0)
+        out_keep = p.local(out_all, out_out, e_local.at[1])
         first_keep = p.local(x_all, first_out, keep_sems.at[2])
         if depth > 2:
             g_job.hop(2)
@@ -776,14 +841,19 @@
                 onward(distance, rep, False)
         for slot in range(2):
             proj_copy(slot, p.rep, p.core).wait()
-            mixed_copy(slot, p.rep, p.core).wait()
+        for at in range(2 * reps):
+            mixed_copy(at, p.rep, p.core).wait()
+        job_o.finish()
+        table_job.finish()
+        for goal in range(depth):
+            when(goal != p.rep, exchange_copy(goal).wait_send)
         for keep in (weight_keep, out_keep, first_keep):
             keep.wait()
         p.finish()
 
     return pl.pallas_call(
         kernel,
-        in_specs=in_vmem(1) + anywhere(7),
+        in_specs=in_vmem(1) + anywhere(6) + in_vmem(len(small)),
         out_specs=in_vmem(10) + anywhere(8),
         out_shape=[
             jax.ShapeDtypeStruct((rows, model), F32),
@@ -809,10 +879,11 @@
         + [pltpu.VMEM((rows, model), BF16)]
         + ColumnGather.scratch(depth) * 2
         + [pltpu.VMEM((2, rows, wide), F32), pltpu.SemaphoreType.DMA((2,)), pltpu.SemaphoreType.DMA((3,)),
-           pltpu.VMEM((rows, model), F32), pltpu.VMEM((2, rows, channels), F32), pltpu.SemaphoreType.DMA((2,))],
+           pltpu.VMEM((rows, model), F32), pltpu.VMEM((2 * reps, rows, channels), F32),
+           pltpu.SemaphoreType.DMA((2 * reps,)), pltpu.VMEM((vector_rows, vector_width), F32)],
         compiler_params=remote_params(0),
         name="forward_mixer",
-    )(tokens, cotangent, own_pair, other_pair, common, vectors, table, out_quarters)
+    )(tokens, cotangent, own_pair, other_pair, common, table, out_quarters, *small)
 
 
 def join_experts(
@@ -1433,7 +1504,9 @@
     )
 
 
-def assemble_kernel(channels, state, heads, side_ref, common_ref, out_ref, in_grad_ref, out_grad_ref):
+def assemble_kernel(
+    channels, state, heads, side_ref, common_ref, out_ref, small_ref, in_grad_ref, out_grad_ref, *small_refs
+):
     reps = side_ref.shape[1]
     inner = 2 * reps * channels
     for kind in range(2):
@@ -1451,23 +1524,30 @@
         tail += [pair[:, :heads], pair[:, LANES // 2 : LANES // 2 + heads]]
     in_grad_ref[:, start:] = jnp.concatenate(tail, axis=1)
     out_grad_ref[...] = out_ref[...].astype(F32).reshape(out_grad_ref.shape)
-
-
-def assemble(side, common, out_rows, channels, state, heads):
+    router_grad_ref = small_refs[-1]
+    for ref, row in zip(small_refs[:-1], (0, 4, 8, 9, 10, 11, 12, 13)):
+        ref[...] = small_ref[row : row + ref.shape[0], : ref.shape[1]]
+    part, experts = router_grad_ref.shape
+    wide = -(-part // LANES) * LANES
+    router = jnp.concatenate([small_ref[16:, :wide], jnp.zeros((LANES - experts, wide), F32)], axis=0)
+    router_grad_ref[...] = router.T[:part, :experts]
+
+
+def assemble(side, common, out_rows, small, small_shapes, channels, state, heads):
     reps, part = side.shape[1], side.shape[3]
     columns = 4 * reps * channels + 2 * state + 2 * reps * heads
     model = out_rows.shape[2]
     return pl.pallas_call(
         functools.partial(assemble_kernel, channels, state, heads),
-        in_specs=in_vmem(3),
-        out_specs=in_vmem(2),
+        in_specs=in_vmem(4),
+        out_specs=in_vmem(2 + len(small_shapes)),
         out_shape=[
             jax.ShapeDtypeStruct((part, columns), F32),
             jax.ShapeDtypeStruct((channels, model), F32),
-        ],
+        ] + [jax.ShapeDtypeStruct(shape, F32) for shape in small_shapes],
         compiler_params=pltpu.CompilerParams(vmem_limit_bytes=48 * 2**20),
         name="assemble",
-    )(side, common, out_rows)
+    )(side, common, out_rows, small)
 
 
 def slot_match(table_row, capacity, rows):
@@ -1692,14 +1772,8 @@
     table = jnp.sum(
         jnp.where(routes[:, None, :] == expert_ids[None, :, None], slot_index[:, None, :] + 1, 0), axis=2
     ).astype(BF16)
-    numbers = jnp.concatenate([lengths[0], dealt_to]).astype(BF16)
-    vector_rows = [in_norm[None], conv_weight, conv_bias[None], dt_bias[None], decay_log[None], skip_gain[None],
-                   mixer_norm[None], post_norm[None], numbers[None]]
-    vector_width = -(-max(row.shape[1] for row in vector_rows) // LANES) * LANES
-    vectors = jnp.concatenate(
-        [jnp.pad(row, ((0, 0), (0, vector_width - row.shape[1]))) for row in vector_rows]
-        + [jnp.zeros((4, vector_width), BF16)], axis=0
-    )
+    small = [in_norm[None], conv_weight, conv_bias[None], dt_bias[None], decay_log[None], skip_gain[None],
+             mixer_norm[None], post_norm[None], jnp.concatenate([lengths, dealt_to[None]], axis=1)]
     part_wide = -(-part // LANES) * LANES
     table_block = jnp.concatenate([table.T, jnp.pad(router.T, ((0, 0), (0, part_wide - part)))], axis=1)
     pair_heads = 2 * heads
@@ -1718,7 +1792,7 @@
     sequences = lengths.shape[1]
     (after, mixer_result, scale, lengths_plane, in_gain, post_gain, taps_own, head_rows, skip_own, norm_own, table_all,
      second_column, g_column, first, weight, out_own, projected, gained) = forward_mixer(
-        tokens, cotangent, pair_of(team), pair_of(2 * rep + 1 - core), common, vectors, table_block,
+        tokens, cotangent, pair_of(team), pair_of(2 * rep + 1 - core), common, small, table_block,
         out_proj.reshape(reps, channels // reps, model),
         (reps, depth, channels, width, state, sequences, inner, convolved),
     )
@@ -1760,23 +1834,29 @@
         out_own.reshape(channels, model), low_plane, layer_parts, first, projected, gained,
         (reps, depth, channels, width, state, sequences, inner, convolved),
     )
-    grad_in_proj, grad_out_proj = assemble(side_rows, common_rows, out_rows, channels, state, heads)
     per_shard = conv_bias.shape[0]
-
+    small_shapes = [
+        (4, per_shard), (1, per_shard), (1, heads), (1, heads), (1, heads), (1, channels), (1, part), (1, part),
+        (part, experts),
+    ]
+    (grad_in_proj, grad_out_proj, grad_taps, grad_bias, grad_dt, grad_decay, grad_skip, grad_mixer_norm, grad_post,
+     grad_in_norm, grad_router) = assemble(
+        side_rows, common_rows, out_rows, small_sum, small_shapes, channels, state, heads
+    )
     return (
         layer_out,
         grad_tokens,
-        small_sum[13, :part],
+        grad_in_norm[0],
         grad_in_proj,
-        small_sum[:4, :per_shard],
-        small_sum[4, :per_shard],
-        small_sum[8, :heads],
-        small_sum[9, :heads],
-        small_sum[10, :heads],
-        small_sum[11, :channels],
+        grad_taps,
+        grad_bias[0],
+        grad_dt[0],
+        grad_decay[0],
+        grad_skip[0],
+        grad_mixer_norm[0],
         grad_out_proj,
-        small_sum[12, :part],
-        small_sum[16:, :part].T,
+        grad_post[0],
+        grad_router,
         grad_shared_in,
         grad_shared_out,
         grad_expert_in,

time: 686 us -> 675 us (0.984)
  local copies, waits for them, and re-layouts: 33 us -> 22.7 us
    pallas_call x1, Pallas kernels: 225 us -> 209 us  [forward_mixer(): pl.pallas_call(kernel, in_specs=in_vmem(1) + anywhere(6) + in_vmem(len(sm...]
    pallas_call x1, Pallas kernels: 207 us -> 216 us  [backward_mixer(): pl.pallas_call(kernel, in_specs=in_vmem(1) + anywhere(2) + in_vmem(11) +...]
  transfers between devices with their start and end apart: 3 -> 3, of which waited for: 0 -> 0; matrix products, arithmetic and copies ran while one was open for 4% -> 2% of each run, Pallas kernels for 86% -> 87%
where the time goes in v4:
time: 675 us; the launch traced here: 671 us
  Pallas kernels  604 us (89%)
  local copies, waits for them, and re-layouts  22.7 us (3%)
  other arithmetic  18.9 us (3%)
  between operations  15.2 us (2%)
  starting transfers between devices  10.5 us (2%)
    pallas_call x1, Pallas kernels, backward_mixer(): pl.pallas_call(kernel, in_specs=in_vmem(1) + anywhere(2) + in_vmem(11) +...  216 us
    pallas_call x1, Pallas kernels, forward_mixer(): pl.pallas_call(kernel, in_specs=in_vmem(1) + anywhere(6) + in_vmem(len(sm...  209 us
    pallas_call x1, Pallas kernels, join_experts(): pl.pallas_call(kernel, in_specs=in_vmem(13) + anywhere(3), out_specs=in_v...  116 us
    pallas_call x1, Pallas kernels, run_experts(): pl.pallas_call(experts_kernel, grid=(local, slots // step), in_specs=[by_...  41.4 us
    pallas_call x1, Pallas kernels, dispatch(): pl.pallas_call(functools.partial(dispatch_kernel, local, capacity, half),...  18.9 us
    convert_element_type x4, other arithmetic, shards(): values.astype(F32)  14.8 us
  transfers between devices with their start and end apart: 3, of which 0 were waited for; matrix products, arithmetic and copies ran while one was open for 2% of the time, Pallas kernels for 87%

profile of v4, /device:TPU:0, one launch (start us, length us, event | category | flops | bytes accessed | tf_op | source)
XLA Modules:
  0.0 671.2 jit_solution(12670739977146388076)
XLA Ops:
  7.3 1.4 copy.57
  8.7 0.6 copy.52
  9.3 1.4 all_to_all.13
  10.7 6.3 all-to-all-start
  17.7 0.6 broadcast_in_dim.56.refs_0_
  18.3 0.6 broadcast_in_dim.62.refs_7_
  18.8 0.6 broadcast_in_dim.61.refs_6_
  19.4 0.6 broadcast_in_dim.57.refs_2_
  20.0 0.1 constant_dynamic-slice_fusion.2
  20.2 0.8 concatenate.17.common_ref
  21.0 1.2 pad_add_fusion.refs_8_
  22.2 1.3 fusion.1.table_ref
  23.5 0.3 constant_dynamic-slice_fusion.4
  23.8 0.9 pad_maximum_fusion
  24.7 208.7 %forward_mixer.1 = (f32[256,1536]{1,0:T(8,128)}, bf16[256,1536]{1,0:T(8,128)(2,1)}, f32[8,256]{1,0:T(8,128)}, f32[4,2,8,128]{3,2,1,0:T(8,128)}, f32[1,1536]{1,0:...) custom-call(bf16[256,1536]{1,0:T(8,128)(2,1)} %x_ref.3, ...), custom_call_target="tpu_custom_call" | custom-call | tf_op jit(solution)/shard_map/forward_mixer/pallas_call | solution.py:854
  233.4 0.8 slice.23
  234.3 0.8 slice.22
  235.1 0.7 reshape.102.router_ref
  235.9 0.5 gather_fusion
  236.4 0.1 broadcast_select_fusion.table_ref
  236.5 0.0 copy-start.9
  236.5 0.6 constant_dynamic-slice_fusion.own_ref
  237.2 0.9 copy-done.4
  238.0 18.9 %dispatch.1 = (bf16[2,1024,1536]{2,1,0:T(8,128)(2,1)}, bf16[2,1024,1536]{2,1,0:T(8,128)(2,1)}, f32[2,1024,128]{2,1,0:T(8,128)}, f32[8,16,256]{2,1,0:T(8,128)}, b...) custom-call(bf16[8,16,256]{2,1,0:T(8,128)(2,1)} %copy-done.9, ...), custom_call_target="tpu_custom_call" | custom-call | tf_op jit(solution)/shard_map/dispatch/pallas_call | solution.py:1620
  257.0 3.6 all-to-all-start.1
  260.5 0.6 all-reduce.5.cloned.1.call-start
  261.1 41.4 %run_experts.1 = (bf16[2,1024,1536]{2,1,0:T(8,128)(2,1)}, bf16[2,1024,1536]{2,1,0:T(8,128)(2,1)}, f32[2,1024,128]{2,1,0:T(8,128)}, bf16[2,1536,1024]{2,1,0:T(8,128)(2,1)}, bf16[2,512,1536]{2,1,0:T(8,128)(2,1)}) custom-call(bf16[2,1024,1536]{2,1,0:T(8,128)(2,1)} %get-tuple-element.75.buffer_ref, bf16[2,1024,1536]{2,1,0:T(8,128)(2,1)} %get-tuple-element.76.slot_g_ref, ...), custom_call_target="tpu_custom_call" | custom-call | tf_op jit(solution)/shard_map/run_experts/pallas_call | solution.py:1693
  302.5 0.2 reshape.107
  302.7 0.9 copy.54
  303.6 1.1 copy.62
  304.7 0.0 all-reduce.5.cloned.1.call-update
  304.8 115.6 %join_experts.1 = (f32[256,1536]{1,0:T(8,128)}, f32[1,1536]{1,0:T(1,128)}, f32[16,1536]{1,0:T(8,128)}, bf16[4,2,256,1536]{3,2,1,0:T(8,128)(2,1)}, bf16[4,2,256,1...) custom-call(bf16[8,2,256]{2,1,0:T(2,128)(2,1)} %constant_dynamic-slice_fusion.own_ref, ...), custom_call_target="tpu_custom_call" | custom-call | tf_op jit(solution)/shard_map/join_experts/pallas_call | solution.py:1126
  420.4 1.0 reshape.104
  421.5 0.7 pad.9.router_ref
  422.2 215.8 %backward_mixer.1 = (bf16[256,1536]{1,0:T(8,128)(2,1)}, bf16[256,1536]{1,0:T(8,128)(2,1)}, bf16[2,4,2,192,384]{4,3,2,1,0:T(8,128)(2,1)}, bf16[4,192,384]{2,1,0:T...) custom-call(f32[4,2,2,8,256]{4,3,2,1,0:T(8,128)} %get-tuple-element.87.scales_ref, ...), custom_call_target="tpu_custom_call" | custom-call | tf_op jit(solution)/shard_map/backward_mixer/pallas_call | solution.py:1486
  638.0 1.7 copy-done
  639.7 1.3 copy-done.1
  640.9 1.1 copy-done.2
  642.0 0.8 copy-done.3
  642.8 3.4 assemble.1
  646.2 0.7 copy.55
  646.9 0.6 reduce
  647.5 2.6 convert_element_type.25
  650.1 2.3 convert_element_type.26
  652.4 3.6 convert_element_type.28
  656.0 6.3 convert_element_type.27
  662.3 0.9 copy.72
  663.2 0.9 copy.73
  (45 shorter events, 0.2 us)
Async XLA Ops:
  7.2 10.5 %copy-start.14 = (bf16[192]{0:T(256)(128)(2,1)S(1)}, bf16[192]{0:T(256)(128)(2,1)}, u32[]{:S(2)}) copy-start(bf16[192]{0:T(256)(128)(2,1)} %param.27) | copy-start | bytes 1156
  7.2 11.1 %copy-start.15 = (bf16[192]{0:T(256)(128)(2,1)S(1)}, bf16[192]{0:T(256)(128)(2,1)}, u32[]{:S(2)}) copy-start(bf16[192]{0:T(256)(128)(2,1)} %param.36) | copy-start | bytes 1156
  7.2 11.6 %copy-start.13 = (bf16[384]{0:T(512)(128)(2,1)S(1)}, bf16[384]{0:T(512)(128)(2,1)}, u32[]{:S(2)}) copy-start(bf16[384]{0:T(512)(128)(2,1)} %param.34) | copy-start | bytes 2308
  7.2 12.2 %copy-start.12 = (bf16[416]{0:T(512)(128)(2,1)S(1)}, bf16[416]{0:T(512)(128)(2,1)}, u32[]{:S(2)}) copy-start(bf16[416]{0:T(512)(128)(2,1)} %param.30) | copy-start | bytes 2500
  7.2 12.8 %copy-start.10 = (s32[256,6]{0,1:T(8,128)S(1)}, s32[256,6]{0,1:T(8,128)}, u32[]{:S(2)}) copy-start(s32[256,6]{0,1:T(8,128)} %param.26) | copy-start | bytes 18436
  7.2 12.8 %copy-start.8 = (bf16[192,6448]{1,0:T(8,128)(2,1)S(1)}, bf16[192,6448]{1,0:T(8,128)(2,1)}, u32[]{:S(2)}) copy-start(bf16[192,6448]{1,0:T(8,128)(2,1)} %param.28) | copy-start | bytes 7428100
  7.3 12.9 %slice-start.2 = ((bf16[192,6448]{1,0:T(8,128)(2,1)}), bf16[192,256]{1,0:T(8,128)(2,1)S(1)}, s32[]{:S(2)}) async-start(bf16[192,6448]{1,0:T(8,128)(2,1)} %param.28), calls=%async_computation.5 | async-start | bytes 196608 | tf_op jit(solution)/shard_map/slice | solution.py:1783
  7.3 12.9 %copy-start.11 = (s32[256,6]{0,1:T(8,128)S(1)}, s32[256,6]{0,1:T(8,128)}, u32[]{:S(2)}) copy-start(s32[256,6]{0,1:T(8,128)} %param.25) | copy-start | bytes 18436
  10.7 226.4 %all-to-all-start = ((bf16[8,192,256]{2,1,0:T(8,128)(2,1)}), bf16[8,192,256]{2,1,0:T(8,128)(2,1)S(1)}, u32[]{:S(2)}, u32[]{:S(2)}) async-start(bf16[8,192,256]{2,1,0:T(8,128)(2,1)} %all_to_all.13), calls=%async_computation | async-start | bytes 1572864 | tf_op jit(solution)/shard_map/all_to_all | solution.py:1801
  236.5 0.6 copy-start.9
  237.2 0.9 copy-start.4
  257.0 45.6 %all-to-all-start.1 = ((bf16[8,192,256]{2,1,0:T(8,128)(2,1)}), bf16[8,192,256]{2,1,0:T(8,128)(2,1)S(1)}, u32[]{:S(2)}, u32[]{:S(2)}) async-start(bf16[8,192,256]{2,1,0:T(8,128)(2,1)} %bitcast.57), calls=%async_computation.1 | async-start | bytes 1572864 | tf_op jit(solution)/shard_map/all_to_all | solution.py:1818
  260.5 387.0 %all-reduce.5.cloned.1.call-start = ((), (), s32[]{:S(2)}) async-start(), calls=%async_computation.2 | async-start | bytes 21233664 | tf_op jit(solution)/shard_map/psum | solution.py:1822
  638.0 1.7 copy-start
  639.7 1.3 copy-start.1
  640.9 1.1 copy-start.2
  642.0 0.8 copy-start.3
  647.5 4.9 copy-start.5
  647.5 8.5 %slice-start = ((s8[6291456]{0:T(1024)(128)(4,1)}), s8[4194304]{0:T(1024)(128)(4,1)S(1)}, s32[]{:S(2)}) async-start(s8[6291456]{0:T(1024)(128)(4,1)} %bitcast.48), calls=%async_computation.3 | async-start | bytes 8388608
  652.4 3.6 slice-start.1
  656.0 6.3 copy-start.7
  656.0 7.2 %copy-start.6 = (bf16[256,1536]{1,0:T(8,128)(2,1)S(1)}, bf16[256,1536]{1,0:T(8,128)(2,1)}, u32[]{:S(2)}) copy-start(bf16[256,1536]{1,0:T(8,128)(2,1)} %get-tuple-element.206) | copy-start | bytes 2359300
Sparse Core Ops, SparseCore 0:
  304.9 323.4 all-reduce.4

commit v5 on v4

--- a/solution.py
+++ b/solution.py
@@ -234,31 +234,28 @@
             place *= 2
         return result
 
-    def barrier(self, plane=False, column=False, everyone=False):
+    def in_column(self, distance):
+        other = lax.rem(2 * self.z + self.core + distance, 2 * self.depth)
+        return self.device(z=other // 2, core=lax.rem(other, 2))
+
+    def barrier(self, plane=False, column=False, whole=False):
         semaphore = pltpu.get_barrier_semaphore()
 
         def greet(device):
             pl.semaphore_signal(semaphore, inc=1, device_id=device, device_id_type=MESH_ID)
 
-        if everyone:
-            count = self.reps * self.depth * 2
-            mine = (self.rep * self.depth + self.z) * 2 + self.core
-
-            def step(distance, carry):
-                other = lax.rem(mine + distance, count)
-                greet({"rep": other // (2 * self.depth), "z": lax.rem(other // 2, self.depth), "core": lax.rem(other, 2)})
-                return carry
-
-            lax.fori_loop(1, count, step, 0)
-            pl.semaphore_wait(semaphore, count - 1)
-            return
         amount = 1
-        greet(self.sibling())
+        if whole:
+            for distance in range(1, 2 * self.depth):
+                greet(self.in_column(distance))
+            amount = 2 * self.depth - 1
+        else:
+            greet(self.sibling())
         if plane:
             for distance in range(1, self.reps):
                 greet(self.device(rep=self.rep_at(distance)))
             amount = amount + self.reps - 1
-        if column:
+        if column and not whole:
             above, below = self.z < self.depth - 1, self.z > 0
             when(above, lambda: greet(self.device(z=self.z + 1)))
             when(below, lambda: greet(self.device(z=self.z - 1)))
@@ -294,22 +291,35 @@
 class PlaneGather:
     @staticmethod
     def scratch(reps):
-        return [pltpu.SemaphoreType.DMA((4, reps)), pltpu.SemaphoreType.DMA((1,))]
-
-    def __init__(self, place, own, out, sems, local_sem):
+        return [pltpu.SemaphoreType.DMA((4, reps + 1)), pltpu.SemaphoreType.DMA((1,))]
+
+    def __init__(self, place, own, out, sems, local_sem, corner=True):
         self.place, self.out, self.sems = place, out, sems
         p = place
+        self.half = own.shape[0] // 2
+        self.corner = corner and p.reps == 4 and self.half % 16 == 0
         self.keep = p.local(own, out.at[p.rep, p.core], local_sem.at[0])
-        for distance in range(1, p.reps):
+        for distance in range(1, 3 if self.corner else p.reps):
             p.send(own, out.at[p.rep, p.core], sems.at[0, distance], sems.at[1, distance],
                    p.device(rep=p.rep_at(distance)))
         p.send(own, out.at[p.rep, p.core], sems.at[2, 0], sems.at[3, 0], p.sibling())
+
+    def part(self, distance, at):
+        p = self.place
+        return self.out.at[p.rep_at(distance), p.core, pl.ds(self.half * at, self.half)]
 
     def relay(self):
         p = self.place
         for distance in range(1, p.reps):
             source = self.out.at[p.rep_at(distance), p.core]
-            p.arrived(source, self.sems.at[1, distance])
+            if self.corner and distance == 3:
+                for at in range(2):
+                    p.arrived(self.part(3, at), self.sems.at[1, 3 + at])
+            else:
+                p.arrived(source, self.sems.at[1, distance])
+            if self.corner and distance < 3:
+                piece, at = self.part(distance, distance - 1), distance + 2
+                p.send(piece, piece, self.sems.at[0, at], self.sems.at[1, at], p.device(rep=p.rep_at(3 - distance)))
             p.send(source, source, self.sems.at[2, distance], self.sems.at[3, distance], p.sibling())
 
     def finish(self):
@@ -557,7 +567,7 @@
     return jnp.broadcast_to(column_values, (rows, LANES)).T[0:8, :]
 
 
-def forward_mixer(tokens, cotangent, own_pair, other_pair, common, small, table, out_quarters, sizes):
+def forward_mixer(tokens, cotangent, own_pair, other_pair, common, small, table, out_quarters, shared_in, sizes):
     reps, depth, channels, width, state, sequences, inner, convolved = sizes
     rows, model = tokens.shape
     part, side = own_pair.shape
@@ -565,6 +575,8 @@
     quarter = out_quarters.shape[1]
     vector_width = -(-max(piece.shape[1] for piece in small) // LANES) * LANES
     vector_rows = 16
+    group = 2 * depth
+    shared = shared_in.shape[1] // (2 * group)
     heads = channels // width
     per_shard = convolved // (2 * depth)
 
@@ -580,16 +592,16 @@
     ] + PlaneSum.scratch(reps, (rows, model), BF16) + PlaneSum.scratch(reps, (8, rows), F32)
     groups = [x_scratch, w_scratch, v_scratch, o_scratch, n_scratch, sum_scratch]
 
-    def kernel(x_ref, g_ref, own_ref, other_ref, common_ref, table_ref, quarters_ref, *refs):
+    def kernel(x_ref, g_ref, own_ref, other_ref, common_ref, table_ref, quarters_ref, shared_ref, *refs):
         small_refs, refs = refs[: len(small)], refs[len(small) :]
         (after_ref, mixed_ref, scale_ref, lengths_ref, in_gain_ref, post_gain_ref, taps_ref, heads_ref, skip_ref,
-               norm_ref, table_out, second_out, g_out, first_out, weight_out, out_out, proj_out, mixed_out), scratch = refs[:18], refs[18:]
+               norm_ref, table_out, second_out, g_out, first_out, weight_out, out_out, proj_out, mixed_out, shared_out), scratch = refs[:19], refs[19:]
         cut = [0]
-        for group in groups:
-            cut.append(cut[-1] + len(group))
+        for items in groups:
+            cut.append(cut[-1] + len(items))
         x_work, w_work, v_work, o_work, n_work, sum_work = [scratch[i:j] for i, j in zip(cut, cut[1:])]
         (second, second_sems, second_local, g_sems, g_local, proj_buffer, proj_sems, keep_sems,
-         own_part, mixed_all, mixed_sems, vectors_ref) = scratch[cut[-1]:]
+         own_part, mixed_all, mixed_sems, vectors_ref, shared_sems, shared_local) = scratch[cut[-1]:]
         p = Place(reps, depth)
         vectors_ref[...] = jnp.zeros_like(vectors_ref)
         row = 0
@@ -597,7 +609,7 @@
             count, size = piece.shape
             vectors_ref[row : row + count, :size] = piece[...].astype(F32)
             row += count
-        p.barrier(plane=True, column=True)
+        p.barrier(plane=True, column=True, whole=True)
 
         x_all, weight_all, vectors_all = x_work[0], w_work[0], v_work[0]
 
@@ -628,7 +640,7 @@
                 row = vectors_all[z, core].astype(F32)[11:12, :LANES]
                 lengths_row = jnp.where(dealt == float(2 * z + core), row, lengths_row)
         n_work[0][...] = jnp.broadcast_to(lengths_row, (8, LANES))
-        n_job = PlaneGather(p, n_work[0], lengths_ref, n_work[1], n_work[2])
+        n_job = PlaneGather(p, n_work[0], lengths_ref, n_work[1], n_work[2], corner=False)
 
         pieces = [vectors_all[z, core].astype(F32) for z in range(depth) for core in range(2)]
         in_gain_ref[...] = jnp.concatenate([piece[0:1, :part] for piece in pieces], axis=1)
@@ -665,6 +677,24 @@
                                  shared=lambda z: table_out.at[z, 1 - p.core])
                 )
         job_o, table_job = late_jobs
+        shard = 2 * p.z + p.core
+
+        def shared_piece(kind, other):
+            start = pl.multiple_of((kind * group + other) * shared, LANES)
+            return shared_ref.at[:, pl.ds(start, shared)]
+
+        def shared_slot(kind, other):
+            return shared_out.at[other, :, pl.ds(kind * shared, shared)]
+
+        shared_keep = [
+            p.local(shared_piece(kind, shard), shared_slot(kind, shard), shared_local.at[kind]) for kind in range(2)
+        ]
+        for distance in range(1, group):
+            goal = p.in_column(distance)
+            for kind in range(2):
+                p.send(shared_piece(kind, 2 * goal["z"] + goal["core"]), shared_slot(kind, shard),
+                       shared_sems.at[2 * kind, distance], shared_sems.at[2 * kind + 1, distance], goal)
+        shared_pending, p.pending = p.pending[-2 * (group - 1) :], p.pending[: -2 * (group - 1)]
         job_o.keep.wait()
         job_o.keep = None
         for job in (n_job, x_job, job_a, job_b, job_c):
@@ -845,6 +875,13 @@
             mixed_copy(at, p.rep, p.core).wait()
         job_o.finish()
         table_job.finish()
+        for distance in range(1, group):
+            other = lax.rem(shard - distance + group, group)
+            for kind in range(2):
+                p.arrived(shared_slot(kind, other), shared_sems.at[2 * kind + 1, distance])
+        for keep in shared_keep:
+            keep.wait()
+        p.pending = p.pending + shared_pending
         for goal in range(depth):
             when(goal != p.rep, exchange_copy(goal).wait_send)
         for keep in (weight_keep, out_keep, first_keep):
@@ -853,8 +890,8 @@
 
     return pl.pallas_call(
         kernel,
-        in_specs=in_vmem(1) + anywhere(6) + in_vmem(len(small)),
-        out_specs=in_vmem(10) + anywhere(8),
+        in_specs=in_vmem(1) + anywhere(7) + in_vmem(len(small)),
+        out_specs=in_vmem(10) + anywhere(9),
         out_shape=[
             jax.ShapeDtypeStruct((rows, model), F32),
             jax.ShapeDtypeStruct((rows, model), BF16),
@@ -874,16 +911,18 @@
             jax.ShapeDtypeStruct((reps, quarter, model), BF16),
             jax.ShapeDtypeStruct((reps, 2, rows, wide), F32),
             jax.ShapeDtypeStruct((reps, 2, rows, channels), F32),
+            jax.ShapeDtypeStruct((group, part, 2 * shared), BF16),
         ],
-        scratch_shapes=[item for group in groups for item in group]
+        scratch_shapes=[item for items in groups for item in items]
         + [pltpu.VMEM((rows, model), BF16)]
         + ColumnGather.scratch(depth) * 2
         + [pltpu.VMEM((2, rows, wide), F32), pltpu.SemaphoreType.DMA((2,)), pltpu.SemaphoreType.DMA((3,)),
            pltpu.VMEM((rows, model), F32), pltpu.VMEM((2 * reps, rows, channels), F32),
-           pltpu.SemaphoreType.DMA((2 * reps,)), pltpu.VMEM((vector_rows, vector_width), F32)],
+           pltpu.SemaphoreType.DMA((2 * reps,)), pltpu.VMEM((vector_rows, vector_width), F32),
+           pltpu.SemaphoreType.DMA((4, group)), pltpu.SemaphoreType.DMA((2,))],
         compiler_params=remote_params(0),
         name="forward_mixer",
-    )(tokens, cotangent, own_pair, other_pair, common, table, out_quarters, *small)
+    )(tokens, cotangent, own_pair, other_pair, common, table, out_quarters, shared_in, *small)
 
 
 def join_experts(
@@ -907,13 +946,16 @@
         ],
         "line": LineSum.scratch(depth, (half_rows, model), BF16) * 2,
         "low": [pltpu.VMEM((2, half_rows, model), BF16), pltpu.VMEM((2, 8, rows), F32)] + PlaneGather.scratch(reps) * 3,
-        "logits": [pltpu.VMEM((2 * depth, 2 * experts, rows), BF16), pltpu.VMEM((2,) + stack, BF16),
-                   pltpu.SemaphoreType.DMA((2,))],
+        "logits": [pltpu.VMEM((2 * depth, 2 * experts, rows), BF16)],
+        "layer": [
+            pltpu.VMEM((2,) + stack, BF16), pltpu.VMEM(stack, F32), pltpu.VMEM((depth,) + stack, BF16),
+            pltpu.SemaphoreType.DMA((2, depth)),
+        ] + LineSum.scratch(depth, stack, BF16),
     }
 
     def kernel(own_ref, gates_ref, dots_ref, hidden_ref, shared_ref, router_ref, in_ref, out_ref, g_ref, after_ref,
                mixed_ref, scale_ref, gain_ref, back_ref, weighted_ref, second_ref,
-               grad_ref, gain_grad_ref, router_grad_ref, layer_out, low_out, scale_out, *scratch):
+               grad_ref, gain_grad_ref, router_grad_ref, layer_out_ref, low_out, scale_out, *scratch):
         work, cut = {}, 0
         for name, items in groups.items():
             work[name] = scratch[cut : cut + len(items)]
@@ -921,7 +963,8 @@
         p = Place(reps, depth)
         slots, slot_sems, second_slots, second_sems = work["stream"]
         parts, own_part, pair, pair_sems = work["parts"]
-        logits_all, layer_slots, layer_sems = work["logits"]
+        logits_all = work["logits"][0]
+        layer_parts, layer_own, layer_pair, layer_pair_sems, layer_into, layer_sems = work["layer"]
         lower = p.z < depth // 2
 
         def goal_at(index):
@@ -1065,10 +1108,10 @@
                 second_ref.at[pl.ds(start, rows)], second_slots.at[lax.rem(at, 2)], second_sems.at[lax.rem(at, 2)]
             )
 
-        def layer_store(at):
-            goal, core = block_at(at)
-            return pltpu.make_async_copy(
-                layer_slots.at[lax.rem(at, 2)], layer_out.at[goal, core], layer_sems.at[lax.rem(at, 2)]
+        def layer_swap(goal, slot):
+            return pltpu.make_async_remote_copy(
+                src_ref=layer_parts.at[slot], dst_ref=layer_pair.at[goal], send_sem=layer_pair_sems.at[0, goal],
+                recv_sem=layer_pair_sems.at[1, goal], device_id=p.sibling(), device_id_type=MESH_ID,
             )
 
         def layer_visit(at, carry):
@@ -1087,12 +1130,29 @@
             for i, match in enumerate(matches(q)):
                 total = total + mm_tn(match.astype(BF16), slots[turn, i])
 
-            @pl.when(at >= 2)
+            @pl.when(turn == 0)
             def _():
-                layer_store(at).wait()
-
-            layer_slots[turn] = total.astype(BF16)
-            layer_store(at).start()
+                slot = lax.rem(at // 2, 2)
+
+                @pl.when(at >= 4)
+                def _():
+                    layer_swap(goal_at(at // 2 - 2), slot).wait_send()
+
+                layer_parts[slot] = total.astype(BF16)
+                layer_swap(goal, slot).start()
+
+            @pl.when(turn == 1)
+            def _():
+                p.arrived(layer_pair.at[goal], layer_pair_sems.at[1, goal])
+
+                @pl.when(goal == p.z)
+                def _():
+                    layer_own[...] = add_up(total, layer_pair[goal])
+
+                @pl.when(goal != p.z)
+                def _():
+                    layer_pair[goal] = add_up(total, layer_pair[goal]).astype(BF16)
+
             both = mm(logits_all[q], second_slots[turn])
             router_grad_ref[...] += both[:experts, :] + both[experts:, :]
             return carry
@@ -1100,23 +1160,28 @@
         router_grad_ref[...] = jnp.zeros_like(router_grad_ref)
         load(weighted_ref, 0).start()
         layer_load(0).start()
-        lax.fori_loop(0, depth, layer_visit, 0)
+        lax.fori_loop(0, 2 * depth, layer_visit, 0)
         first_job.relay()
         second_job = norm_back(1)
+        layer_line = LineSum(p, lambda goal: [layer_pair[goal]], layer_pair, layer_into, layer_sems)
+        layer_line.step(0)
         dot_row = row_of(jnp.concatenate(row_dots, axis=0), rows)
         scale_row = scale_ref[...]
         scales[0] = scale_row
         scales[1] = scale_row**2 * dot_row / inner
-        scale_job = PlaneGather(p, scales, scale_out, *gather_sems[4:6])
-        lax.fori_loop(depth, 2 * depth, layer_visit, 0)
+        scale_job = PlaneGather(p, scales, scale_out, *gather_sems[4:6], corner=False)
+        for step in range(1, depth - 1):
+            layer_line.step(step)
         scale_job.relay()
         second_job.relay()
+        layer_line.gather(layer_own)
+        layer_out_ref[...] = (layer_own[...] + after_ref[...]).astype(BF16)
         for job in (first_job, scale_job, second_job):
             job.finish()
-        for slot in range(2):
-            layer_store(slot).wait()
         for at in range(max(depth - 2, 0), depth):
             swap(goal_at(at), at % 2, False)
+            layer_swap(goal_at(at), at % 2).wait_send()
+        layer_line.finish()
         for line in lines:
             line.finish()
         p.finish()
@@ -1126,12 +1191,12 @@
     return pl.pallas_call(
         kernel,
         in_specs=in_vmem(13) + anywhere(3),
-        out_specs=in_vmem(3) + anywhere(3),
+        out_specs=in_vmem(4) + anywhere(2),
         out_shape=[
             jax.ShapeDtypeStruct((rows, model), F32),
             jax.ShapeDtypeStruct((1, model), F32),
             jax.ShapeDtypeStruct((experts, model), F32),
-            jax.ShapeDtypeStruct((depth, 2, rows, model), BF16),
+            jax.ShapeDtypeStruct((rows, model), BF16),
             jax.ShapeDtypeStruct((reps, 2, rows, model), BF16),
             jax.ShapeDtypeStruct((reps, 2, 2, 8, rows), F32),
         ],
@@ -1145,8 +1210,8 @@
 
 
 def backward_mixer(
-    scales, after, after_grad, tokens, in_gain, post_grad, router_parts, lengths, taps, head_rows, skip, norm, weight,
-    out_weight, low, layer_parts, first, proj, gained, sizes,
+    scales, after_grad, tokens, in_gain, post_grad, router_parts, lengths, taps, head_rows, skip, norm, weight,
+    out_weight, low, first, proj, gained, sizes,
 ):
     reps, depth, channels, width, state, sequences, inner, convolved = sizes
     rows, model = tokens.shape
@@ -1162,8 +1227,6 @@
     stack = (rows, model)
     groups = {
         "early": [pltpu.VMEM((2, rows, channels), F32), pltpu.SemaphoreType.DMA((2,))],
-        "layer": [pltpu.SemaphoreType.DMA((1,))]
-        + ColumnSum.scratch(depth, stack, BF16),
         "stream": [
             pltpu.VMEM(stack, BF16), pltpu.VMEM((2, rows, wide), F32), pltpu.VMEM((2,) + stack, BF16),
             pltpu.SemaphoreType.DMA((3, 2)),
@@ -1193,9 +1256,9 @@
         "end": [pltpu.SemaphoreType.DMA((2, 5, reps)), pltpu.SemaphoreType.DMA((6,)), pltpu.VMEM((2, 32, model), F32)],
     }
 
-    def kernel(scales_ref, after_ref, grad_ref, x_ref, gain_ref, post_grad_ref, router_ref, lengths_ref, taps_ref,
-               heads_ref, skip_ref, norm_ref, weight_ref, out_ref, low_ref, layer_ref, first_ref, proj_ref, gained_ref,
-               layer_out_ref, tokens_grad_ref, side_out, common_out, out_out, small_out, *scratch):
+    def kernel(scales_ref, grad_ref, x_ref, gain_ref, post_grad_ref, router_ref, lengths_ref, taps_ref,
+               heads_ref, skip_ref, norm_ref, weight_ref, out_ref, low_ref, first_ref, proj_ref, gained_ref,
+               tokens_grad_ref, side_out, common_out, out_out, small_out, *scratch):
         work, cut = {}, 0
         for name, items in groups.items():
             work[name] = scratch[cut : cut + len(items)]
@@ -1225,7 +1288,6 @@
         proj_load(0, p.rep_at(1), 1 - p.core).start()
         proj_load(1, p.rep_at(1), p.core).start()
         p.barrier(plane=True, column=True)
-        layer_job = ColumnSum(p, layer_ref, *work["layer"][1:], own=(first_slot, work["layer"][0]))
         in_total, out_total, taps_total, heads_total, wide_total = work["grads"]
         for total in work["grads"]:
             total[...] = jnp.zeros_like(total)
@@ -1257,8 +1319,6 @@
                    p.device(rep=rep))
         out_mid[p.rep] = out_parts[p.rep]
         out_job = LineSum(p, lambda at: [out_mid[at]], out_into, out_into, out_line_sems)
-        layer_job.ready()
-        layer_job.step(0)
 
         parts, own_part, pair, pair_sems, into, into_sems = work["sum"]
 
@@ -1338,7 +1398,6 @@
 
             pl.when(at == 1)(out_start)
             for step in range(1, depth - 1):
-                pl.when(at == 2 * step)(functools.partial(layer_job.step, step))
                 pl.when(at == 2 * step + 1)(functools.partial(out_job.step, step))
             return carry
 
@@ -1461,14 +1520,6 @@
             side_jobs[1].step(at)
         keeps.append(side_finish(1))
 
-        late_load(after_ref, 0).start()
-        layer_job.total(own_part)
-        for chunk in range(rows // 32):
-            piece = slice(32 * chunk, 32 * chunk + 32)
-            if chunk + 1 < rows // 32:
-                late_load(after_ref, chunk + 1).start()
-            late_load(after_ref, chunk).wait()
-            layer_out_ref[piece, :] = (own_part[piece, :] + late[chunk % 2]).astype(BF16)
         from_reps(small_all, 4)
         small_out[...] = add_up(*[small_all[at] for at in range(reps)])
         for at, target in ((0, side_out.at[0]), (1, side_out.at[1]), (2, common_out), (3, out_out)):
@@ -1485,10 +1536,9 @@
 
     return pl.pallas_call(
         kernel,
-        in_specs=in_vmem(1) + anywhere(2) + in_vmem(11) + anywhere(5),
-        out_specs=in_vmem(2) + anywhere(3) + in_vmem(1),
+        in_specs=in_vmem(1) + anywhere(1) + in_vmem(11) + anywhere(4),
+        out_specs=in_vmem(1) + anywhere(3) + in_vmem(1),
         out_shape=[
-            jax.ShapeDtypeStruct((rows, model), BF16),
             jax.ShapeDtypeStruct((rows, model), BF16),
             jax.ShapeDtypeStruct((2, reps, 2, part, channels), BF16),
             jax.ShapeDtypeStruct((reps, part, wide - side), BF16),
@@ -1499,8 +1549,8 @@
         compiler_params=remote_params(3, 63),
         name="backward_mixer",
     )(
-        scales, after, after_grad, tokens, in_gain, post_grad, router_parts, lengths, taps, head_rows, skip, norm,
-        weight, out_weight, low, layer_parts, first, proj, gained,
+        scales, after_grad, tokens, in_gain, post_grad, router_parts, lengths, taps, head_rows, skip, norm,
+        weight, out_weight, low, first, proj, gained,
     )
 
 
@@ -1789,19 +1839,22 @@
             axis=1,
         )
 
+    shared_lanes = -(-shared // LANES) * LANES
+    shared_padded = shared_in
+    if shared_lanes != shared:
+        shared_padded = jnp.pad(
+            shared_in.reshape(part, 2 * group, shared), ((0, 0), (0, 0), (0, shared_lanes - shared))
+        ).reshape(part, -1)
     sequences = lengths.shape[1]
     (after, mixer_result, scale, lengths_plane, in_gain, post_gain, taps_own, head_rows, skip_own, norm_own, table_all,
-     second_column, g_column, first, weight, out_own, projected, gained) = forward_mixer(
+     second_column, g_column, first, weight, out_own, projected, gained, shared_in_own) = forward_mixer(
         tokens, cotangent, pair_of(team), pair_of(2 * rep + 1 - core), common, small, table_block,
-        out_proj.reshape(reps, channels // reps, model),
+        out_proj.reshape(reps, channels // reps, model), shared_padded,
         (reps, depth, channels, width, state, sequences, inner, convolved),
     )
     second_column = second_column.reshape(group * rows, model)
     g_column = g_column.reshape(group * rows, model)
-    shared_in_own = lax.all_to_all(
-        shared_in.reshape(part, 2, group, shared).transpose(2, 0, 1, 3).reshape(group * part, 2 * shared),
-        COLUMN, split_axis=0, concat_axis=0, tiled=True,
-    )
+    shared_in_own = shared_in_own.reshape(model, 2, shared_lanes)[:, :, :shared].reshape(model, 2 * shared)
 
     table_all = table_all.reshape(group, experts, -1)
     router_t = table_all[:, :, rows : rows + part].transpose(1, 0, 2).reshape(experts, model)
@@ -1822,16 +1875,16 @@
         for values in lax.psum((grad_expert_in, grad_expert_out, shared_out_grad, shared_in_rows), "rep")
     ]
 
-    after_grad, post_grad, router_grad, layer_parts, low_plane, scales = join_experts(
+    after_grad, post_grad, router_grad, layer_out, low_plane, scales = join_experts(
         table_own, gates, dots, shared_hidden, shared_grad, router_t, shared_in_own, shared_out, cotangent, after,
         mixer_result, scale, post_gain, buffer_grad, weighted, second_column, inner, reps, depth, capacity,
     )
     router_parts = jnp.pad(
         router_grad.reshape(experts, depth, 2, part).transpose(1, 2, 0, 3), ((0, 0), (0, 0), (0, 0), (0, part_wide - part))
     )
-    layer_out, grad_tokens, side_rows, common_rows, out_rows, small_sum = backward_mixer(
-        scales, after, after_grad, tokens, in_gain, post_grad, router_parts, lengths_plane, taps_own, head_rows, skip_own, norm_own, weight.reshape(model, -1),
-        out_own.reshape(channels, model), low_plane, layer_parts, first, projected, gained,
+    grad_tokens, side_rows, common_rows, out_rows, small_sum = backward_mixer(
+        scales, after_grad, tokens, in_gain, post_grad, router_parts, lengths_plane, taps_own, head_rows, skip_own, norm_own, weight.reshape(model, -1),
+        out_own.reshape(channels, model), low_plane, first, projected, gained,
         (reps, depth, channels, width, state, sequences, inner, convolved),
     )
     per_shard = conv_bias.shape[0]

time: 675 us -> 672 us (level)
    pallas_call x2, Pallas kernels: 425 us -> 404 us  [the longest x1 210 us: forward_mixer(): pl.pallas_call(kernel, in_specs=in_vmem(1) + anywhere(7) + in_vmem(len(sm...]
    pallas_call x1, Pallas kernels: 116 us -> 130 us  [join_experts(): pl.pallas_call(kernel, in_specs=in_vmem(13) + anywhere(3), out_specs=in_v...]
  transfers between devices with their start and end apart: 3 -> 2, of which waited for: 0 -> 0; matrix products, arithmetic and copies ran while one was open for 2% -> 0% of each run, Pallas kernels for 87% -> 56%
where the time goes in v5:
time: 672 us; the launch traced here: 662 us
  Pallas kernels  598 us (89%)
  local copies, waits for them, and re-layouts  23.9 us (4%)
  other arithmetic  20.3 us (3%)
  between operations  15.1 us (2%)
    pallas_call x1, Pallas kernels, forward_mixer(): pl.pallas_call(kernel, in_specs=in_vmem(1) + anywhere(7) + in_vmem(len(sm...  210 us
    pallas_call x1, Pallas kernels, backward_mixer(): pl.pallas_call(kernel, in_specs=in_vmem(1) + anywhere(1) + in_vmem(11) +...  195 us
    pallas_call x1, Pallas kernels, join_experts(): pl.pallas_call(kernel, in_specs=in_vmem(13) + anywhere(3), out_specs=in_v...  130 us
    pallas_call x1, Pallas kernels, run_experts(): pl.pallas_call(experts_kernel, grid=(local, slots // step), in_specs=[by_...  41.5 us
    pallas_call x1, Pallas kernels, dispatch(): pl.pallas_call(functools.partial(dispatch_kernel, local, capacity, half),...  18.9 us
    convert_element_type x4, other arithmetic, shards(): values.astype(F32)  14.8 us
  transfers between devices with their start and end apart: 2, of which 0 were waited for; matrix products, arithmetic and copies ran while one was open for 0% of the time, Pallas kernels for 56%

profile of v5, /device:TPU:0, one launch (start us, length us, event | category | flops | bytes accessed | tf_op | source)
XLA Modules:
  0.0 661.7 jit_solution(10337150076788863260)
XLA Ops:
  7.9 1.2 broadcast_in_dim.56.refs_0_
  9.1 1.2 broadcast_in_dim.62.refs_7_
  10.3 1.2 broadcast_in_dim.61.refs_6_
  11.6 1.3 broadcast_in_dim.57.refs_2_
  12.8 0.7 broadcast_add_fusion
  13.5 0.7 select_reduce_fusion
  14.3 0.9 slice.15
  15.2 1.0 constant_dynamic-slice_fusion.2
  16.1 1.2 pad_add_fusion.refs_8_
  17.4 1.3 fusion.1.table_ref
  18.7 0.8 concatenate.17.common_ref
  19.5 1.5 constant_dynamic-slice_fusion.4
  21.0 0.9 pad_maximum_fusion
  21.8 209.5 %forward_mixer.1 = (f32[256,1536]{1,0:T(8,128)}, bf16[256,1536]{1,0:T(8,128)(2,1)}, f32[8,256]{1,0:T(8,128)}, f32[4,2,8,128]{3,2,1,0:T(8,128)}, f32[1,1536]{1,0:...) custom-call(bf16[256,1536]{1,0:T(8,128)(2,1)} %x_ref.3, ...), custom_call_target="tpu_custom_call" | custom-call | tf_op jit(solution)/shard_map/forward_mixer/pallas_call | solution.py:891
  231.4 0.8 slice.23
  232.2 0.8 slice.22
  233.1 0.7 reshape.95.router_ref
  233.8 0.5 gather_fusion
  234.4 0.1 broadcast_select_fusion.table_ref
  234.5 0.0 copy-start.7
  234.5 0.6 constant_dynamic-slice_fusion.own_ref
  235.1 18.9 %dispatch.1 = (bf16[2,1024,1536]{2,1,0:T(8,128)(2,1)}, bf16[2,1024,1536]{2,1,0:T(8,128)(2,1)}, f32[2,1024,128]{2,1,0:T(8,128)}, f32[8,16,256]{2,1,0:T(8,128)}, b...) custom-call(bf16[8,16,256]{2,1,0:T(8,128)(2,1)} %copy-done.7, ...), custom_call_target="tpu_custom_call" | custom-call | tf_op jit(solution)/shard_map/dispatch/pallas_call | solution.py:1670
  254.0 3.6 all-to-all-start
  257.7 0.2 all-reduce.5.cloned.1.call-start
  257.9 41.5 %run_experts.1 = (bf16[2,1024,1536]{2,1,0:T(8,128)(2,1)}, bf16[2,1024,1536]{2,1,0:T(8,128)(2,1)}, f32[2,1024,128]{2,1,0:T(8,128)}, bf16[2,1536,1024]{2,1,0:T(8,128)(2,1)}, bf16[2,512,1536]{2,1,0:T(8,128)(2,1)}) custom-call(bf16[2,1024,1536]{2,1,0:T(8,128)(2,1)} %get-tuple-element.76.buffer_ref, bf16[2,1024,1536]{2,1,0:T(8,128)(2,1)} %get-tuple-element.77.slot_g_ref, ...), custom_call_target="tpu_custom_call" | custom-call | tf_op jit(solution)/shard_map/run_experts/pallas_call | solution.py:1743
  299.4 0.0 all-to-all-done
  299.4 0.2 reshape.99
  299.6 0.9 copy.51
  300.5 1.1 copy.58
  301.6 0.0 all-reduce.5.cloned.1.call-update
  301.6 130.5 %join_experts.1 = (f32[256,1536]{1,0:T(8,128)}, f32[1,1536]{1,0:T(1,128)}, f32[16,1536]{1,0:T(8,128)}, bf16[256,1536]{1,0:T(8,128)(2,1)}, bf16[4,2,256,1536]{3,2...) custom-call(bf16[8,2,256]{2,1,0:T(2,128)(2,1)} %constant_dynamic-slice_fusion.own_ref, ...), custom_call_target="tpu_custom_call" | custom-call | tf_op jit(solution)/shard_map/join_experts/pallas_call | solution.py:1191
  432.1 1.0 reshape.96
  433.2 0.7 pad.9.router_ref
  433.9 194.6 %backward_mixer.1 = (bf16[256,1536]{1,0:T(8,128)(2,1)}, bf16[2,4,2,192,384]{4,3,2,1,0:T(8,128)(2,1)}, bf16[4,192,384]{2,1,0:T(8,128)(2,1)}, bf16[4,96,1536]{2,1,0:T(8,128)(2,1)}, f32[32,512]{1,0:T(8,128)}) custom-call(f32[4,2,2,8,256]{4,3,2,1,0:T(8,128)} %get-tuple-element.89.scales_ref, f32[256,1536]{1,0:T(8,128)} %get-tuple-element.90.grad_ref, ...), custom_call_target="tpu_custom_call" | custom-call | tf_op jit(solution)/shard_map/backward_mixer/pallas_call | solution.py:1537
  628.5 1.7 copy-done
  630.2 1.3 copy-done.1
  631.4 1.1 copy-done.2
  632.5 0.8 copy-done.3
  633.3 3.4 assemble.1
  636.7 0.7 copy.52
  637.4 0.6 reduce
  638.0 2.6 convert_element_type.25
  640.6 2.3 convert_element_type.26
  642.9 0.0 copy-done.4
  642.9 3.6 convert_element_type.28
  646.5 6.3 convert_element_type.27
  652.8 0.9 copy.68
  653.7 0.9 copy.69
  (23 shorter events, 0.1 us)
Async XLA Ops:
  234.5 0.6 copy-start.7
  254.0 45.4 %all-to-all-start = ((bf16[8,192,256]{2,1,0:T(8,128)(2,1)}), bf16[8,192,256]{2,1,0:T(8,128)(2,1)S(1)}, u32[]{:S(2)}, u32[]{:S(2)}) async-start(bf16[8,192,256]{2,1,0:T(8,128)(2,1)} %bitcast.50), calls=%async_computation | async-start | bytes 1572864 | tf_op jit(solution)/shard_map/all_to_all | solution.py:1871
  257.7 380.3 %all-reduce.5.cloned.1.call-start = ((), (), s32[]{:S(2)}) async-start(), calls=%async_computation.1 | async-start | bytes 21233664 | tf_op jit(solution)/shard_map/psum | solution.py:1875
  628.5 1.7 copy-start
  630.2 1.3 copy-start.1
  631.4 1.1 copy-start.2
  632.5 0.8 copy-start.3
  638.0 4.9 copy-start.4
  638.0 8.5 %slice-start = ((s8[6291456]{0:T(1024)(128)(4,1)}), s8[4194304]{0:T(1024)(128)(4,1)S(1)}, s32[]{:S(2)}) async-start(s8[6291456]{0:T(1024)(128)(4,1)} %bitcast.41), calls=%async_computation.2 | async-start | bytes 8388608
  642.9 3.6 slice-start.1
  646.5 6.3 copy-start.5
  646.5 7.2 %copy-start.6 = (bf16[256,1536]{1,0:T(8,128)(2,1)S(1)}, bf16[256,1536]{1,0:T(8,128)(2,1)}, u32[]{:S(2)}) copy-start(bf16[256,1536]{1,0:T(8,128)(2,1)} %get-tuple-element.206) | copy-start | bytes 2359300
Sparse Core Ops, SparseCore 0:
  301.7 310.7 all-reduce.4

commit v6 on v5

--- a/solution.py
+++ b/solution.py
@@ -747,8 +747,32 @@
                 else:
                     copy.wait_send()
 
-        def onward(distance, rep, start):
-            for values, target, sems in ((pair, into, into_sems), (s_pair, s_into, s_into_sems)):
+        corner = reps == 4 and rows % 32 == 0
+        half_rows = rows // 2
+
+        def distance_at(index):
+            if corner:
+                return jnp.where(index == 0, 3, jnp.where(index == 3, 0, index))
+            return lax.rem(index + 1, reps)
+
+        def to_corner(start):
+            for half, index in ((0, 3), (1, 0)):
+                piece = pl.ds(half_rows * half, half_rows)
+                copy = pltpu.make_async_remote_copy(
+                    src_ref=pair.at[p.rep_at(3), piece], dst_ref=into.at[0, piece],
+                    send_sem=into_sems.at[0, index], recv_sem=into_sems.at[1, index],
+                    device_id=p.device(rep=p.rep_at(half + 1)), device_id_type=MESH_ID,
+                )
+                copy.start() if start else copy.wait_send()
+
+        def add_corner(rep, half, index):
+            piece = pl.ds(half_rows * half, half_rows)
+            p.arrived(into.at[0, piece], into_sems.at[1, index])
+            pair[rep, piece, :] = add_up(pair[rep, piece, :], into[0, piece, :]).astype(BF16)
+
+        def onward(distance, rep, start, rows_too=True):
+            kinds = [(s_pair, s_into, s_into_sems)] + ([(pair, into, into_sems)] if rows_too else [])
+            for values, target, sems in kinds:
                 copy = pltpu.make_async_remote_copy(
                     src_ref=values.at[rep], dst_ref=target.at[distance], send_sem=sems.at[0, distance],
                     recv_sem=sems.at[1, distance], device_id=p.device(rep=rep), device_id_type=MESH_ID,
@@ -765,7 +789,7 @@
             return pltpu.make_async_copy(mixed_all.at[at], mixed_out.at[rep, core], mixed_sems.at[at])
 
         def place_of(at):
-            distance = lax.rem(at // 2 + 1, reps)
+            distance = distance_at(at // 2)
             turn = lax.rem(at, 2)
             return distance, p.rep_at(distance), turn, jnp.where(turn == 0, 1 - p.core, p.core)
 
@@ -822,7 +846,14 @@
                 pair[rep] = add_up(part_rows, pair[rep]).astype(BF16)
                 p.arrived(s_pair.at[rep], s_pair_sems.at[1, rep])
                 s_pair[rep] = add_up(squares[rep, p.core], s_pair[rep])
-                onward(distance, rep, True)
+                if corner:
+                    pl.when(distance == 1)(functools.partial(add_corner, rep, 1, 0))
+                    pl.when(distance == 2)(functools.partial(add_corner, rep, 0, 3))
+                    pl.when(distance < 3)(functools.partial(onward, distance, rep, True))
+                    pl.when(distance == 3)(functools.partial(onward, distance, rep, True, False))
+                    pl.when(distance == 3)(functools.partial(to_corner, True))
+                else:
+                    onward(distance, rep, True)
 
         delay = 4
 
@@ -847,8 +878,9 @@
         for distance in range(1, reps):
             p.arrived(s_into.at[distance], s_into_sems.at[1, distance])
             square_terms.append(s_into[distance])
-            p.arrived(into.at[distance], into_sems.at[1, distance])
-            terms.append(into[distance])
+            if not (corner and distance == 3):
+                p.arrived(into.at[distance], into_sems.at[1, distance])
+                terms.append(into[distance])
         scale_row = lax.rsqrt(add_up(*square_terms) / inner + EPS)
         scale_ref[...] = scale_row
         mixed = column_of(scale_row[0:1, :], rows) * add_up(*terms)
@@ -868,7 +900,9 @@
             rep = p.rep_at(distance) if distance else p.rep
             swap(rep, False)
             if distance:
-                onward(distance, rep, False)
+                onward(distance, rep, False, not (corner and distance == 3))
+        if corner:
+            to_corner(False)
         for slot in range(2):
             proj_copy(slot, p.rep, p.core).wait()
         for at in range(2 * reps):
@@ -1225,6 +1259,8 @@
     small_width = -(-max(per_shard, channels, router_width) // LANES) * LANES
     small_shape = (16 + experts, small_width)
     stack = (rows, model)
+    corner = reps == 4 and rows % 32 == 0
+    half_rows = rows // 2
     groups = {
         "early": [pltpu.VMEM((2, rows, channels), F32), pltpu.SemaphoreType.DMA((2,))],
         "stream": [
@@ -1234,7 +1270,8 @@
         "sum": [
             pltpu.VMEM((2,) + stack, BF16), pltpu.VMEM(stack, F32),
             pltpu.VMEM((reps,) + stack, BF16), pltpu.SemaphoreType.DMA((2, reps)),
-            pltpu.VMEM((reps - 1,) + stack, BF16), pltpu.SemaphoreType.DMA((2, reps)),
+            pltpu.VMEM((2 if corner else reps - 1,) + stack, BF16), pltpu.SemaphoreType.DMA((2, reps)),
+            pltpu.VMEM((2, half_rows, model), BF16),
         ],
         "grads": [
             pltpu.VMEM((depth, 2, part, wide), F32), pltpu.VMEM((channels, model), F32),
@@ -1285,8 +1322,14 @@
         for at in range(2):
             gained_load(at, *early_place(at)).start()
             low_load(at, *early_place(at)).start()
-        proj_load(0, p.rep_at(1), 1 - p.core).start()
-        proj_load(1, p.rep_at(1), p.core).start()
+        def distance_at(index):
+            if corner:
+                return jnp.where(index == 0, 3, jnp.where(index == 3, 0, index))
+            return lax.rem(index + 1, reps)
+
+        opening = p.rep_at(distance_at(0))
+        proj_load(0, opening, 1 - p.core).start()
+        proj_load(1, opening, p.core).start()
         p.barrier(plane=True, column=True)
         in_total, out_total, taps_total, heads_total, wide_total = work["grads"]
         for total in work["grads"]:
@@ -1308,8 +1351,8 @@
             return carry
 
         lax.fori_loop(0, 2 * reps, early, 0)
-        low_load(0, p.rep_at(1), 1 - p.core).start()
-        low_load(1, p.rep_at(1), p.core).start()
+        low_load(0, opening, 1 - p.core).start()
+        low_load(1, opening, p.core).start()
         out_parts, out_mid, out_sems, out_into, out_line_sems, out_low = work["out"]
         out_line_total = out_total.at[pl.ds(0, quarter)]
         out_parts[...] = out_total[...].astype(BF16).reshape(reps, quarter, model)
@@ -1320,11 +1363,12 @@
         out_mid[p.rep] = out_parts[p.rep]
         out_job = LineSum(p, lambda at: [out_mid[at]], out_into, out_into, out_line_sems)
 
-        parts, own_part, pair, pair_sems, into, into_sems = work["sum"]
-
-        def swap(distance, rep, start):
+        parts, own_part, pair, pair_sems, into, into_sems, extra = work["sum"]
+
+        def swap(index, start):
+            rep = p.rep_at(distance_at(index))
             copy = pltpu.make_async_remote_copy(
-                src_ref=parts.at[lax.rem(distance, 2)], dst_ref=pair.at[rep], send_sem=pair_sems.at[0, rep],
+                src_ref=parts.at[lax.rem(index, 2)], dst_ref=pair.at[rep], send_sem=pair_sems.at[0, rep],
                 recv_sem=pair_sems.at[1, rep], device_id=p.sibling(), device_id_type=MESH_ID,
             )
             copy.start() if start else copy.wait_send()
@@ -1336,8 +1380,22 @@
             )
             copy.start() if start else copy.wait_send()
 
+        def to_corner(start):
+            for half, index in ((0, 3), (1, 0)):
+                copy = pltpu.make_async_remote_copy(
+                    src_ref=pair.at[p.rep_at(3), pl.ds(half_rows * half, half_rows)], dst_ref=extra.at[half],
+                    send_sem=into_sems.at[0, index], recv_sem=into_sems.at[1, index],
+                    device_id=p.device(rep=p.rep_at(half + 1)), device_id_type=MESH_ID,
+                )
+                copy.start() if start else copy.wait_send()
+
+        def add_corner(rep, half, index):
+            piece = pl.ds(half_rows * half, half_rows)
+            p.arrived(extra.at[half], into_sems.at[1, index])
+            pair[rep, piece, :] = add_up(pair[rep, piece, :], extra[half]).astype(BF16)
+
         def visit(at, carry):
-            distance, turn = lax.rem(at // 2 + 1, reps), lax.rem(at, 2)
+            distance, turn = distance_at(at // 2), lax.rem(at, 2)
             rep = p.rep_at(distance)
             core = jnp.where(turn == 0, 1 - p.core, p.core)
             first_load(rep, core).start()
@@ -1363,10 +1421,10 @@
             def _():
                 @pl.when(at >= 4)
                 def _():
-                    swap(at // 2 - 1, p.rep_at(at // 2 - 1), False)
-
-                parts[lax.rem(distance, 2)] = part_rows.astype(BF16)
-                swap(distance, rep, True)
+                    swap(at // 2 - 2, False)
+
+                parts[lax.rem(at // 2, 2)] = part_rows.astype(BF16)
+                swap(at // 2, True)
 
             @pl.when((turn == 1) & (distance == 0))
             def _():
@@ -1376,7 +1434,13 @@
             def _():
                 p.arrived(pair.at[rep], pair_sems.at[1, rep])
                 pair[rep] = add_up(part_rows, pair[rep]).astype(BF16)
-                onward(distance, rep, True)
+                if corner:
+                    pl.when(distance == 3)(functools.partial(to_corner, True))
+                    pl.when(distance == 1)(functools.partial(add_corner, rep, 1, 0))
+                    pl.when(distance == 2)(functools.partial(add_corner, rep, 0, 3))
+                    pl.when(distance < 3)(functools.partial(onward, distance, rep, True))
+                else:
+                    onward(distance, rep, True)
 
             first_load(rep, core).wait()
             for z in range(depth):
@@ -1387,7 +1451,7 @@
 
             @pl.when(at < 2 * reps - 2)
             def _():
-                later = p.rep_at(lax.rem(at // 2 + 2, reps))
+                later = p.rep_at(distance_at(at // 2 + 1))
                 proj_load(turn, later, core).start()
                 low_load(turn, later, core).start()
 
@@ -1431,7 +1495,8 @@
         common_job.ready()
         common_job.step(0)
         side_jobs[1].step(0)
-        for distance in range(1, reps):
+        sources = 2 if corner else reps - 1
+        for distance in range(1, sources + 1):
             p.arrived(into.at[distance - 1], into_sems.at[1, distance])
         gain_grad = jnp.zeros((1, model), F32)
         for start in range(0, rows, 32):
@@ -1440,7 +1505,7 @@
                 late_load(grad_ref, start // 32 + 1).start()
             late_load(grad_ref, start // 32).wait()
             first_grad = add_up(
-                own_part[piece, :], pair[p.rep, piece, :], *[into[at, piece, :] for at in range(reps - 1)]
+                own_part[piece, :], pair[p.rep, piece, :], *[into[at, piece, :] for at in range(sources)]
             )
             x = x_ref[piece, :].astype(F32)
             x_scale = rms_rows(x)
@@ -1526,12 +1591,12 @@
             from_reps(target, at)
         for keep in keeps:
             keep.wait()
-        for distance in range(reps):
-            rep = p.rep_at(distance)
-            if distance in (0, reps - 1):
-                swap(distance, rep, False)
-            if distance:
-                onward(distance, rep, False)
+        for index in (reps - 2, reps - 1):
+            swap(index, False)
+        for distance in range(1, sources + 1):
+            onward(distance, p.rep_at(distance), False)
+        if corner:
+            to_corner(False)
         p.finish()
 
     return pl.pallas_call(
@@ -1718,20 +1783,18 @@
 
     @pl.when(at == 0)
     def _():
-        in_total[...] = jnp.zeros_like(in_total)
-        out_total[...] = jnp.zeros_like(out_total)
-
-    in_total[...] += mm_tn(buffer, pre_grad)
-    out_total[...] += mm_tn(hidden, result_grad)
-
-    @pl.when(at == pl.num_programs(1) - 1)
+        in_total[...] = mm_tn(buffer, pre_grad)
+        out_total[...] = mm_tn(hidden, result_grad)
+
+    @pl.when(at == 1)
     def _():
-        in_grad_ref[...] = in_total[...].astype(BF16)
-        out_grad_ref[...] = out_total[...].astype(BF16)
-
-
-def run_experts(buffer, slot_g, gate_slot, expert_in, expert_out, step):
+        in_grad_ref[...] = (in_total[...] + mm_tn(buffer, pre_grad)).astype(BF16)
+        out_grad_ref[...] = (out_total[...] + mm_tn(hidden, result_grad)).astype(BF16)
+
+
+def run_experts(buffer, slot_g, gate_slot, expert_in, expert_out):
     local, slots, model = buffer.shape
+    step = slots // 2
     half = expert_out.shape[1]
 
     def by_step(width):
@@ -1742,7 +1805,7 @@
 
     return pl.pallas_call(
         experts_kernel,
-        grid=(local, slots // step),
+        grid=(local, 2),
         in_specs=[
             by_step(model), by_step(model), by_step(LANES), by_expert(model, 2 * half), by_expert(half, model),
         ],
@@ -1866,7 +1929,7 @@
         table_dealt, table_own, second_column, g_column, router_t, shared_in_own, shared_out, capacity
     )
     weighted, buffer_grad, dots, grad_expert_in, grad_expert_out = run_experts(
-        buffer, slot_g, gate_slot, expert_in, expert_out, group * capacity // 2
+        buffer, slot_g, gate_slot, expert_in, expert_out
     )
     shared_in_rows = lax.all_to_all(shared_in_grad, COLUMN, split_axis=0, concat_axis=0, tiled=True)
     shared_in_rows = shared_in_rows.reshape(group, part, 2, shared).transpose(1, 2, 0, 3).reshape(part, -1)

time: 672 us -> 659 us (0.981)
  Pallas kernels: 598 us -> 586 us
  transfers between devices with their start and end apart: 2 -> 2, of which waited for: 0 -> 0; matrix products, arithmetic and copies ran while one was open for 0% -> 0% of each run, Pallas kernels for 56% -> 55%
where the time goes in v6:
time: 659 us; the launch traced here: 650 us
  Pallas kernels  586 us (89%)
  local copies, waits for them, and re-layouts  23.9 us (4%)
  other arithmetic  20.3 us (3%)
  between operations  15.3 us (2%)
    pallas_call x1, Pallas kernels, forward_mixer(): pl.pallas_call(kernel, in_specs=in_vmem(1) + anywhere(7) + in_vmem(len(sm...  210 us
    pallas_call x1, Pallas kernels, backward_mixer(): pl.pallas_call(kernel, in_specs=in_vmem(1) + anywhere(1) + in_vmem(11) +...  190 us
    pallas_call x1, Pallas kernels, join_experts(): pl.pallas_call(kernel, in_specs=in_vmem(13) + anywhere(3), out_specs=in_v...  125 us
    pallas_call x1, Pallas kernels, run_experts(): pl.pallas_call(experts_kernel, grid=(local, 2), in_specs=[by_step(model),...  39.4 us
    pallas_call x1, Pallas kernels, dispatch(): pl.pallas_call(functools.partial(dispatch_kernel, local, capacity, half),...  18.9 us
    convert_element_type x4, other arithmetic, shards(): values.astype(F32)  14.8 us
  transfers between devices with their start and end apart: 2, of which 0 were waited for; matrix products, arithmetic and copies ran while one was open for 0% of the time, Pallas kernels for 55%

profile of v6, /device:TPU:0, one launch (start us, length us, event | category | flops | bytes accessed | tf_op | source)
XLA Modules:
  0.0 650.2 jit_solution(18315054518261181480)
XLA Ops:
  7.9 1.2 broadcast_in_dim.56.refs_0_
  9.1 1.2 broadcast_in_dim.62.refs_7_
  10.3 1.2 broadcast_in_dim.61.refs_6_
  11.6 1.3 broadcast_in_dim.57.refs_2_
  12.8 0.7 broadcast_add_fusion
  13.5 0.7 select_reduce_fusion
  14.3 0.9 slice.15
  15.2 1.0 constant_dynamic-slice_fusion.2
  16.1 1.2 pad_add_fusion.refs_8_
  17.4 1.3 fusion.1.table_ref
  18.7 0.8 concatenate.17.common_ref
  19.5 1.5 constant_dynamic-slice_fusion.4
  21.0 0.9 pad_maximum_fusion
  21.8 209.8 %forward_mixer.1 = (f32[256,1536]{1,0:T(8,128)}, bf16[256,1536]{1,0:T(8,128)(2,1)}, f32[8,256]{1,0:T(8,128)}, f32[4,2,8,128]{3,2,1,0:T(8,128)}, f32[1,1536]{1,0:...) custom-call(bf16[256,1536]{1,0:T(8,128)(2,1)} %x_ref.3, ...), custom_call_target="tpu_custom_call" | custom-call | tf_op jit(solution)/shard_map/forward_mixer/pallas_call | solution.py:925
  231.7 0.8 slice.23
  232.5 0.8 slice.22
  233.4 0.7 reshape.95.router_ref
  234.2 0.5 gather_fusion
  234.7 0.1 broadcast_select_fusion.table_ref
  234.8 0.0 copy-start.7
  234.8 0.6 constant_dynamic-slice_fusion.own_ref
  235.4 18.9 %dispatch.1 = (bf16[2,1024,1536]{2,1,0:T(8,128)(2,1)}, bf16[2,1024,1536]{2,1,0:T(8,128)(2,1)}, f32[2,1024,128]{2,1,0:T(8,128)}, f32[8,16,256]{2,1,0:T(8,128)}, b...) custom-call(bf16[8,16,256]{2,1,0:T(8,128)(2,1)} %copy-done.7, ...), custom_call_target="tpu_custom_call" | custom-call | tf_op jit(solution)/shard_map/dispatch/pallas_call | solution.py:1735
  254.3 3.6 all-to-all-start
  257.9 0.5 all-reduce.5.cloned.1.call-start
  258.4 39.4 %run_experts.1 = (bf16[2,1024,1536]{2,1,0:T(8,128)(2,1)}, bf16[2,1024,1536]{2,1,0:T(8,128)(2,1)}, f32[2,1024,128]{2,1,0:T(8,128)}, bf16[2,1536,1024]{2,1,0:T(8,128)(2,1)}, bf16[2,512,1536]{2,1,0:T(8,128)(2,1)}) custom-call(bf16[2,1024,1536]{2,1,0:T(8,128)(2,1)} %get-tuple-element.76.buffer_ref, bf16[2,1024,1536]{2,1,0:T(8,128)(2,1)} %get-tuple-element.77.slot_g_ref, ...), custom_call_target="tpu_custom_call" | custom-call | tf_op jit(solution)/shard_map/run_experts/pallas_call | solution.py:1806
  297.8 0.0 all-to-all-done
  297.8 0.2 reshape.99
  298.0 0.9 copy.51
  298.9 1.1 copy.58
  300.0 0.0 all-reduce.5.cloned.1.call-update
  300.0 125.0 %join_experts.1 = (f32[256,1536]{1,0:T(8,128)}, f32[1,1536]{1,0:T(1,128)}, f32[16,1536]{1,0:T(8,128)}, bf16[256,1536]{1,0:T(8,128)(2,1)}, bf16[4,2,256,1536]{3,2...) custom-call(bf16[8,2,256]{2,1,0:T(2,128)(2,1)} %constant_dynamic-slice_fusion.own_ref, ...), custom_call_target="tpu_custom_call" | custom-call | tf_op jit(solution)/shard_map/join_experts/pallas_call | solution.py:1225
  425.1 1.0 reshape.96
  426.2 0.7 pad.9.router_ref
  426.8 190.0 %backward_mixer.1 = (bf16[256,1536]{1,0:T(8,128)(2,1)}, bf16[2,4,2,192,384]{4,3,2,1,0:T(8,128)(2,1)}, bf16[4,192,384]{2,1,0:T(8,128)(2,1)}, bf16[4,96,1536]{2,1,0:T(8,128)(2,1)}, f32[32,512]{1,0:T(8,128)}) custom-call(f32[4,2,2,8,256]{4,3,2,1,0:T(8,128)} %get-tuple-element.89.scales_ref, f32[256,1536]{1,0:T(8,128)} %get-tuple-element.90.grad_ref, ...), custom_call_target="tpu_custom_call" | custom-call | tf_op jit(solution)/shard_map/backward_mixer/pallas_call | solution.py:1602
  616.8 0.0 copy-start
  616.8 1.7 copy-done
  618.5 1.3 copy-done.1
  619.7 1.1 copy-done.2
  620.8 0.8 copy-done.3
  621.6 3.4 assemble.1
  625.0 0.7 copy.52
  625.7 0.6 reduce
  626.3 2.6 convert_element_type.25
  628.9 2.3 convert_element_type.26
  631.2 3.6 convert_element_type.28
  634.8 6.3 convert_element_type.27
  641.1 0.9 copy.68
  642.0 0.9 copy.69
  (23 shorter events, 0.1 us)
Async XLA Ops:
  234.8 0.6 copy-start.7
  254.3 43.5 %all-to-all-start = ((bf16[8,192,256]{2,1,0:T(8,128)(2,1)}), bf16[8,192,256]{2,1,0:T(8,128)(2,1)S(1)}, u32[]{:S(2)}, u32[]{:S(2)}) async-start(bf16[8,192,256]{2,1,0:T(8,128)(2,1)} %bitcast.50), calls=%async_computation | async-start | bytes 1572864 | tf_op jit(solution)/shard_map/all_to_all | solution.py:1934
  257.9 368.4 %all-reduce.5.cloned.1.call-start = ((), (), s32[]{:S(2)}) async-start(), calls=%async_computation.1 | async-start | bytes 21233664 | tf_op jit(solution)/shard_map/psum | solution.py:1938
  616.8 1.7 copy-start
  618.5 1.3 copy-start.1
  619.7 1.1 copy-start.2
  620.8 0.8 copy-start.3
  626.3 4.9 copy-start.4
  626.3 8.5 %slice-start = ((s8[6291456]{0:T(1024)(128)(4,1)}), s8[4194304]{0:T(1024)(128)(4,1)S(1)}, s32[]{:S(2)}) async-start(s8[6291456]{0:T(1024)(128)(4,1)} %bitcast.41), calls=%async_computation.2 | async-start | bytes 8388608
  631.2 3.6 slice-start.1
  634.8 6.3 copy-start.5
  634.8 7.2 %copy-start.6 = (bf16[256,1536]{1,0:T(8,128)(2,1)S(1)}, bf16[256,1536]{1,0:T(8,128)(2,1)}, u32[]{:S(2)}) copy-start(bf16[256,1536]{1,0:T(8,128)(2,1)} %get-tuple-element.206) | copy-start | bytes 2359300
Sparse Core Ops, SparseCore 0:
  300.1 303.1 all-reduce.4

commit v7 on v6

--- a/solution.py
+++ b/solution.py
@@ -632,8 +632,7 @@
             vector_job.hop(distance)
         vector_job.finish()
 
-        own_row = vectors_all[p.z, p.core].astype(F32)[11:12, :LANES]
-        dealt = own_row[:, sequences : sequences + 1]
+        dealt = vectors_all[p.z, p.core].astype(F32)[12:13, 0:1]
         lengths_row = jnp.zeros((1, LANES), F32)
         for z in range(depth):
             for core in range(2):
@@ -1825,6 +1824,27 @@
     )(buffer, slot_g, gate_slot, expert_in, expert_out)
 
 
+def widen_kernel(*refs):
+    count = len(refs) // 2
+    for source, target in zip(refs[:count], refs[count:]):
+        target[...] = source[...].astype(F32)
+
+
+def widen(streamed, kept, steps):
+    specs = [by_rows((values.shape[0] // steps, values.shape[1])) for values in streamed]
+    specs += [whole(values.shape) for values in kept]
+    arrays = list(streamed) + list(kept)
+    return pl.pallas_call(
+        widen_kernel,
+        grid=(steps,),
+        in_specs=specs,
+        out_specs=specs,
+        out_shape=[jax.ShapeDtypeStruct(values.shape, F32) for values in arrays],
+        compiler_params=pltpu.CompilerParams(vmem_limit_bytes=48 * 2**20),
+        name="widen",
+    )(*arrays)
+
+
 def gather(values, axes, axis=0):
     return lax.all_gather(values, axes, axis=axis, tiled=True)
 
@@ -1886,7 +1906,7 @@
         jnp.where(routes[:, None, :] == expert_ids[None, :, None], slot_index[:, None, :] + 1, 0), axis=2
     ).astype(BF16)
     small = [in_norm[None], conv_weight, conv_bias[None], dt_bias[None], decay_log[None], skip_gain[None],
-             mixer_norm[None], post_norm[None], jnp.concatenate([lengths, dealt_to[None]], axis=1)]
+             mixer_norm[None], post_norm[None], lengths, dealt_to[None]]
     part_wide = -(-part // LANES) * LANES
     table_block = jnp.concatenate([table.T, jnp.pad(router.T, ((0, 0), (0, part_wide - part)))], axis=1)
     pair_heads = 2 * heads
@@ -1933,10 +1953,12 @@
     )
     shared_in_rows = lax.all_to_all(shared_in_grad, COLUMN, split_axis=0, concat_axis=0, tiled=True)
     shared_in_rows = shared_in_rows.reshape(group, part, 2, shared).transpose(1, 2, 0, 3).reshape(part, -1)
-    grad_expert_in, grad_expert_out, grad_shared_out, grad_shared_in = [
-        values.astype(F32)
-        for values in lax.psum((grad_expert_in, grad_expert_out, shared_out_grad, shared_in_rows), "rep")
-    ]
+    summed = lax.psum((grad_expert_in, grad_expert_out, shared_out_grad, shared_in_rows), "rep")
+    wide_expert_in, wide_expert_out, grad_shared_out, grad_shared_in = widen(
+        [summed[0].reshape(-1, summed[0].shape[2]), summed[1].reshape(-1, model)], summed[2:], 8
+    )
+    grad_expert_in = wide_expert_in.reshape(expert_in.shape)
+    grad_expert_out = wide_expert_out.reshape(expert_out.shape)
 
     after_grad, post_grad, router_grad, layer_out, low_plane, scales = join_experts(
         table_own, gates, dots, shared_hidden, shared_grad, router_t, shared_in_own, shared_out, cotangent, after,

time: 659 us -> 659 us (level)
  other arithmetic: 20.3 us -> 4.28 us
  Pallas kernels: 586 us -> 598 us
    convert_element_type x4 -> x0, other arithmetic: 14.8 us -> none  [shards(): values.astype(F32)]
    pallas_call x0 -> x1, Pallas kernels: none -> 10.9 us  [widen(): pl.pallas_call(widen_kernel, grid=(steps,), in_specs=specs, out_specs=spe...]
where the time goes in v7:
time: 659 us; the launch traced here: 649 us
  Pallas kernels  598 us (91%)
  local copies, waits for them, and re-layouts  28 us (4%)
  between operations  15.1 us (2%)
    pallas_call x1, Pallas kernels, forward_mixer(): pl.pallas_call(kernel, in_specs=in_vmem(1) + anywhere(7) + in_vmem(len(sm...  210 us
    pallas_call x1, Pallas kernels, backward_mixer(): pl.pallas_call(kernel, in_specs=in_vmem(1) + anywhere(1) + in_vmem(11) +...  190 us
    pallas_call x1, Pallas kernels, join_experts(): pl.pallas_call(kernel, in_specs=in_vmem(13) + anywhere(3), out_specs=in_v...  125 us
    pallas_call x1, Pallas kernels, run_experts(): pl.pallas_call(experts_kernel, grid=(local, 2), in_specs=[by_step(model),...  39.4 us
    pallas_call x1, Pallas kernels, dispatch(): pl.pallas_call(functools.partial(dispatch_kernel, local, capacity, half),...  18.9 us
  transfers between devices with their start and end apart: 2, of which 0 were waited for; matrix products, arithmetic and copies ran while one was open for 0% of the time, Pallas kernels for 55%

profile of v7, /device:TPU:0, one launch (start us, length us, event | category | flops | bytes accessed | tf_op | source)
XLA Modules:
  0.0 648.8 jit_solution(8315238957962607190)
XLA Ops:
  7.9 1.2 broadcast_in_dim.56.refs_0_
  9.1 1.2 broadcast_in_dim.62.refs_7_
  10.3 1.2 broadcast_in_dim.61.refs_6_
  11.6 1.3 broadcast_in_dim.57.refs_2_
  12.8 0.7 broadcast_add_fusion
  13.5 0.7 select_reduce_fusion
  14.3 0.9 slice.15
  15.2 1.0 constant_dynamic-slice_fusion.2
  16.1 1.3 fusion.1.table_ref
  17.5 0.8 concatenate.14.common_ref
  18.2 1.5 constant_dynamic-slice_fusion.4
  19.7 0.9 pad_maximum_fusion
  20.6 209.8 %forward_mixer.1 = (f32[256,1536]{1,0:T(8,128)}, bf16[256,1536]{1,0:T(8,128)(2,1)}, f32[8,256]{1,0:T(8,128)}, f32[4,2,8,128]{3,2,1,0:T(8,128)}, f32[1,1536]{1,0:...) custom-call(bf16[256,1536]{1,0:T(8,128)(2,1)} %x_ref.3, ...), custom_call_target="tpu_custom_call" | custom-call | tf_op jit(solution)/shard_map/forward_mixer/pallas_call | solution.py:924
  230.5 0.8 slice.23
  231.3 0.8 slice.22
  232.2 0.7 reshape.107.router_ref
  232.9 0.5 gather_fusion
  233.5 0.1 broadcast_select_fusion.table_ref
  233.6 0.0 copy-start.9
  233.6 0.6 constant_dynamic-slice_fusion.own_ref
  234.2 0.0 copy-done.9
  234.2 18.9 %dispatch.1 = (bf16[2,1024,1536]{2,1,0:T(8,128)(2,1)}, bf16[2,1024,1536]{2,1,0:T(8,128)(2,1)}, f32[2,1024,128]{2,1,0:T(8,128)}, f32[8,16,256]{2,1,0:T(8,128)}, b...) custom-call(bf16[8,16,256]{2,1,0:T(8,128)(2,1)} %copy-done.9, ...), custom_call_target="tpu_custom_call" | custom-call | tf_op jit(solution)/shard_map/dispatch/pallas_call | solution.py:1734
  253.1 3.6 all-to-all-start
  256.7 0.3 all-reduce.5.cloned.1.call-start
  256.9 39.4 %run_experts.1 = (bf16[2,1024,1536]{2,1,0:T(8,128)(2,1)}, bf16[2,1024,1536]{2,1,0:T(8,128)(2,1)}, f32[2,1024,128]{2,1,0:T(8,128)}, bf16[2,1536,1024]{2,1,0:T(8,128)(2,1)}, bf16[2,512,1536]{2,1,0:T(8,128)(2,1)}) custom-call(bf16[2,1024,1536]{2,1,0:T(8,128)(2,1)} %get-tuple-element.80.buffer_ref, bf16[2,1024,1536]{2,1,0:T(8,128)(2,1)} %get-tuple-element.81.slot_g_ref, ...), custom_call_target="tpu_custom_call" | custom-call | tf_op jit(solution)/shard_map/run_experts/pallas_call | solution.py:1805
  296.3 0.0 all-to-all-done
  296.3 0.2 reshape.113
  296.5 0.9 copy.50
  297.4 1.1 copy.57
  298.5 0.0 all-reduce.5.cloned.1.call-update
  298.5 125.5 %join_experts.1 = (f32[256,1536]{1,0:T(8,128)}, f32[1,1536]{1,0:T(1,128)}, f32[16,1536]{1,0:T(8,128)}, bf16[256,1536]{1,0:T(8,128)(2,1)}, bf16[4,2,256,1536]{3,2...) custom-call(bf16[8,2,256]{2,1,0:T(2,128)(2,1)} %constant_dynamic-slice_fusion.own_ref, ...), custom_call_target="tpu_custom_call" | custom-call | tf_op jit(solution)/shard_map/join_experts/pallas_call | solution.py:1224
  424.0 1.0 reshape.108
  425.1 0.7 pad.9.router_ref
  425.8 189.7 %backward_mixer.1 = (bf16[256,1536]{1,0:T(8,128)(2,1)}, bf16[2,4,2,192,384]{4,3,2,1,0:T(8,128)(2,1)}, bf16[4,192,384]{2,1,0:T(8,128)(2,1)}, bf16[4,96,1536]{2,1,0:T(8,128)(2,1)}, f32[32,512]{1,0:T(8,128)}) custom-call(f32[4,2,2,8,256]{4,3,2,1,0:T(8,128)} %get-tuple-element.93.scales_ref, f32[256,1536]{1,0:T(8,128)} %get-tuple-element.94.grad_ref, ...), custom_call_target="tpu_custom_call" | custom-call | tf_op jit(solution)/shard_map/backward_mixer/pallas_call | solution.py:1601
  615.5 1.7 copy-done.1
  617.1 1.3 copy-done.2
  618.4 1.1 copy-done.4
  619.5 0.8 copy-done.6
  620.3 3.4 assemble.1
  623.7 0.7 copy.51
  624.4 0.6 reduce
  625.0 1.9 copy-done
  626.8 1.1 copy-done.3
  628.0 1.0 copy-done.5
  629.0 10.9 %widen.1 = (f32[3072,1024]{1,0:T(8,128)}, f32[1024,1536]{1,0:T(8,128)}, f32[128,1536]{1,0:T(8,128)}, f32[192,2048]{1,0:T(8,128)}) custom-call(bf16[3072,1024]{1,0:T(8,128)(2,1)} %get-tuple-element.184.refs_0_, bf16[1024,1536]{1,0:T(8,128)(2,1)S(1)} %copy-done, bf16[128,1536]{1,0:T(8,128)(2,1)S(1)} %copy-done.5, bf16[192,2048]{1,0:T(8,128)(2,1)S(1)} %copy-done.3), custom_call_target="tpu_custom_call" | custom-call | tf_op jit(solution)/shard_map/widen/pallas_call | solution.py:1837
  639.9 0.9 copy.67
  640.8 0.0 copy-done.8
  640.8 0.9 copy.68
  (18 shorter events, 0.1 us)
Async XLA Ops:
  233.6 0.6 copy-start.9
  253.1 43.2 %all-to-all-start = ((bf16[8,192,256]{2,1,0:T(8,128)(2,1)}), bf16[8,192,256]{2,1,0:T(8,128)(2,1)S(1)}, u32[]{:S(2)}, u32[]{:S(2)}) async-start(bf16[8,192,256]{2,1,0:T(8,128)(2,1)} %bitcast.55), calls=%async_computation | async-start | bytes 1572864 | tf_op jit(solution)/shard_map/all_to_all | solution.py:1954
  256.7 368.3 %all-reduce.5.cloned.1.call-start = ((), (), s32[]{:S(2)}) async-start(), calls=%async_computation.1 | async-start | bytes 21233664 | tf_op jit(solution)/shard_map/psum | solution.py:1956
  615.4 1.7 copy-start.1
  617.1 1.3 copy-start.2
  618.4 1.1 copy-start.4
  619.4 0.8 copy-start.6
  625.0 1.9 copy-start
  626.8 1.1 copy-start.3
  628.0 1.0 copy-start.5
  629.0 10.9 %copy-start.7 = (bf16[256,1536]{1,0:T(8,128)(2,1)S(1)}, bf16[256,1536]{1,0:T(8,128)(2,1)}, u32[]{:S(2)}) copy-start(bf16[256,1536]{1,0:T(8,128)(2,1)} %get-tuple-element.213) | copy-start | bytes 2359300
  629.0 11.8 %copy-start.8 = (bf16[256,1536]{1,0:T(8,128)(2,1)S(1)}, bf16[256,1536]{1,0:T(8,128)(2,1)}, u32[]{:S(2)}) copy-start(bf16[256,1536]{1,0:T(8,128)(2,1)} %get-tuple-element.214) | copy-start | bytes 2359300
Sparse Core Ops, SparseCore 0:
  298.6 302.8 all-reduce.4
